TPU v7x, 256 devices: a whole 4x4x8 slice. The times are simulated.
256 devices in a mesh: blk: 64 (over z, y, core), rhs: 4 (over x).
Axes of the slice: x: 4, y: 4, z: 8, core: 2. Of those that a mesh axis runs over, the one named last changes fastest.
Arguments:
- rhs: float32 [8, 8, 64, 256, 128], P(None, None, 'blk', 'rhs'), parts along dimension 3, may hold values from -6 to 6
- lower_tiles: bfloat16 [8, 8, 64, 3, 128, 128], P(None, None, 'blk'), may hold values from -0.25 to 0.25
- lower_block_columns: int32 [8, 8, 64, 3], P(None, None, 'blk'), may hold values from 0 to 4095, as said below
- upper_tiles: bfloat16 [8, 8, 64, 3, 128, 128], P(None, None, 'blk'), may hold values from -0.25 to 0.25
- upper_cols: int32 [8, 8, 64, 3], P(None, None, 'blk'), may hold values from 0 to 4095, as said below
- diag_inverse: bfloat16 [8, 8, 64, 128, 128], P(None, None, 'blk')
Outputs:
- solution: bfloat16 [8, 8, 64, 256, 128], P(None, None, 'blk', 'rhs'), parts along dimension 3
There are 4 independent parts, one for each index of `rhs`. A program takes and returns all parts, laid end to end along the dimension named above; an argument that names none is the same for every part. Nothing has to cross between parts.
Inputs may be any that keep to these rules, and one draw needn't show every extreme that they name: `lower_block_columns`: entry k of block row (l * 8 + m) * 64 + p is either that row's own number (an empty slot) or ((l - 1) * 8 + m) * 64 + (p + d) mod 64 with d one of -1, 0, 1; the nonempty slots of a row have distinct d; rows with l = 0 have only empty slots. `upper_cols`: entry k of block row (l * 8 + m) * 64 + p is either that row's own number (an empty slot) or ((l + 1) * 8 + m) * 64 + (p + d) mod 64 with d one of -1, 0, 1; the nonempty slots of a row have distinct d; rows with l = 7 have only empty slots.
All inputs are finite; a program needn't handle non-finite values.
Results may differ from a plain program's by a relative error of at most 0.015.
Values may be sent and summed in bfloat16 or wider, within the bound.
No kernel may reach another device: no remote copies, remote signals or barrier semaphores. Data moves between devices by JAX's collectives and lax.ppermute only.
A program may use at most 64 MiB of HBM per device.

v0:
```python
import jax
import jax.numpy as jnp
from jax import lax
from jax.sharding import PartitionSpec as P


def extended(block, sides, width):
    for axis, dim in sides:
        count = lax.axis_size(axis)
        forward = [(i, i + 1) for i in range(count - 1)]
        forward.append((count - 1, 0))
        backward = [(target, source) for source, target in forward]
        low = lax.ppermute(
            lax.slice_in_dim(block, block.shape[dim] - width, None, axis=dim), axis, forward
        )
        high = lax.ppermute(lax.slice_in_dim(block, 0, width, axis=dim), axis, backward)
        block = jnp.concatenate([low, block, high], axis=dim)
    return block


def row_numbers(level_id, row_count, cycle_size, home_spot):
    return (level_id * row_count + jnp.arange(row_count, dtype=jnp.int32)) * cycle_size + home_spot


def select_terms(
    window, halo_width, shift_amount_value, tile_collection, columns, numbers, cycle_size
):
    home_spot = (numbers % cycle_size)[:, None]
    distance = (columns % cycle_size - home_spot) % cycle_size
    offset_step = jnp.where(distance == 1, 1, jnp.where(distance == cycle_size - 1, -1, 0))
    source = offset_step + (shift_amount_value + halo_width)
    present = columns != numbers[:, None]
    places = jnp.arange(2 * halo_width + 1, dtype=jnp.int32)
    select = ((source[:, :, None] == places) & present[:, :, None]).astype(jnp.bfloat16)
    chosen_entries = jnp.einsum(
        "mkw,wmsb->mksb", select, window, preferred_element_type=jnp.float32
    ).astype(jnp.bfloat16)
    return jnp.einsum(
        "lqfp,lqcp->lfc", chosen_entries, tile_collection, preferred_element_type=jnp.float32
    )


def apply_inverse(summed_terms, inverted_tile_matrix):
    return jnp.einsum(
        "vdj,voj->vdo", summed_terms, inverted_tile_matrix, preferred_element_type=jnp.float32
    ).astype(jnp.bfloat16)


def on_device(rhs, lower_tiles, lower_block_columns, upper_tiles, upper_cols, diag_inverse):
    cycle_size = lax.axis_size("blk")
    position = lax.axis_index("blk")
    level_count = rhs.shape[0]
    row_count = rhs.shape[1]
    sides_in = rhs[:, :, 0]
    lower_tile_group = lower_tiles[:, :, 0]
    lower_index = lower_block_columns[:, :, 0]
    upper_set = upper_tiles[:, :, 0]
    upper_index = upper_cols[:, :, 0]
    inverse = diag_inverse[:, :, 0]
    level_ids = jnp.arange(level_count, dtype=jnp.int32)

    def forward(previous, inputs):
        tile_collection, columns, side_rows, level_id = inputs
        window = extended(previous[None], (("blk", 0),), 1)
        numbers = row_numbers(level_id, row_count, cycle_size, position)
        products = select_terms(window, 1, 0, tile_collection, columns, numbers, cycle_size)
        solved_now = (side_rows - products).astype(jnp.bfloat16)
        return (solved_now, solved_now)

    first_level = sides_in[0].astype(jnp.bfloat16)
    unused, later_levels = lax.scan(
        forward, first_level, (lower_tile_group[1:], lower_index[1:], sides_in[1:], level_ids[1:])
    )
    solved = jnp.concatenate([first_level[None], later_levels], axis=0)
    top_level = apply_inverse(solved[-1], inverse[-1])

    def backward(next_level, inputs):
        tile_collection, columns, inverted_tile_matrix, forward_rows, level_id = inputs
        window = extended(next_level[None], (("blk", 0),), 1)
        numbers = row_numbers(level_id, row_count, cycle_size, position)
        products = select_terms(window, 1, 0, tile_collection, columns, numbers, cycle_size)
        summed_terms = (forward_rows.astype(jnp.float32) - products).astype(jnp.bfloat16)
        solved_now = apply_inverse(summed_terms, inverted_tile_matrix)
        return (solved_now, solved_now)

    unused, lower_levels = lax.scan(
        backward,
        top_level,
        (upper_set[:-1], upper_index[:-1], inverse[:-1], solved[:-1], level_ids[:-1]),
        reverse=True,
    )
    result = jnp.concatenate([lower_levels, top_level[None]], axis=0)
    return result[:, :, None]


def solution(mesh):
    return jax.shard_map(
        on_device,
        mesh=mesh,
        in_specs=(
            P(None, None, "blk", "rhs", None),
            P(None, None, "blk", None, None, None),
            P(None, None, "blk", None),
            P(None, None, "blk", None, None, None),
            P(None, None, "blk", None),
            P(None, None, "blk", None, None),
        ),
        out_specs=P(None, None, "blk", "rhs", None),
        check_vma=False,
    )
```

profile of v0, /device:TPU:6, one launch (start us, length us, event | category | flops | bytes accessed | tf_op | source)
XLA Modules:
  0.0 172.3 jit_solution(12492925341129720685)
XLA Ops:
  1.0 7.4 %slice_bitcast_fusion.1 = bf16[7,8,3,128,128]{4,3,2,1,0:T(8,128)(2,1)} fusion(bf16[8,8,1,3,128,128]{5,4,3,1,0,2:T(8,128)(2,1)} %bitcast.140), kind=kLoop, calls=%fused_computation.71 | loop fusion | bytes 11010048 | tf_op jit(solution)/shard_map/slice | solution.py:72
  9.4 78.5 %while.30 = (s32[]{:T(128)}, bf16[8,64,128]{2,1,0:T(8,128)(2,1)S(1)}, bf16[7,8,64,128]{3,2,1,0:T(8,128)(2,1)S(1)}, f32[7,8,64,128]{3,2,1,0:T(8,128)S(1)}, s32[7,...) while((s32[]{:T(128)}, ...), condition=%wide.region_1.2_spmd, body=%wide.region_0.1_spmd.sunk | while | flops 52036536 | bytes 4458501 | solution.py:71
  9.4 7.8 %collective-permute-start = (bf16[1,8,64,128]{3,2,1,0:T(8,128)(2,1)S(1)}, bf16[1,8,64,128]{3,2,1,0:T(8,128)(2,1)S(1)}, u32[]{:S(2)}, u32[]{:S(2)}) collective-permute-start(bf16[1,8,64,128]{3,2,1,0:T(8,128)(2,1)S(1)} %bitcast.142), channel_id=1, source_target_pairs={{4,0},{8,4},{12,8},{16,12},{20,16},{24,20},{28,24},{32,28},{36,32}... | collective-permute-start | bytes 393224 | tf_op jit(solution)/shard_map/while/body/eval_jaxpr/ppermute | solution.py:16
  19.7 5.2 %collective-permute-done.1 = bf16[1,8,64,128]{3,2,1,0:T(8,128)(2,1)S(1)} collective-permute-done((bf16[1,8,64,128]{3,2,1,0:T(8,128)(2,1)S(1)}, bf16[1,8,64,128]{3,2,1,0:T(8,128)(2,1)S(1)}, u32[]{:S(2)}, u32[]{:S(2)}) %collective-permute-start.1) | collective-permute-done | bytes 131104 | tf_op jit(solution)/shard_map/while/body/eval_jaxpr/ppermute | solution.py:13
  29.8 5.3 %collective-permute-done.1 = bf16[1,8,64,128]{3,2,1,0:T(8,128)(2,1)S(1)} collective-permute-done((bf16[1,8,64,128]{3,2,1,0:T(8,128)(2,1)S(1)}, bf16[1,8,64,128]{3,2,1,0:T(8,128)(2,1)S(1)}, u32[]{:S(2)}, u32[]{:S(2)}) %collective-permute-start.1) | collective-permute-done | bytes 131104 | tf_op jit(solution)/shard_map/while/body/eval_jaxpr/ppermute | solution.py:13
  39.9 5.3 %collective-permute-done.1 = bf16[1,8,64,128]{3,2,1,0:T(8,128)(2,1)S(1)} collective-permute-done((bf16[1,8,64,128]{3,2,1,0:T(8,128)(2,1)S(1)}, bf16[1,8,64,128]{3,2,1,0:T(8,128)(2,1)S(1)}, u32[]{:S(2)}, u32[]{:S(2)}) %collective-permute-start.1) | collective-permute-done | bytes 131104 | tf_op jit(solution)/shard_map/while/body/eval_jaxpr/ppermute | solution.py:13
  50.0 5.3 %collective-permute-done.1 = bf16[1,8,64,128]{3,2,1,0:T(8,128)(2,1)S(1)} collective-permute-done((bf16[1,8,64,128]{3,2,1,0:T(8,128)(2,1)S(1)}, bf16[1,8,64,128]{3,2,1,0:T(8,128)(2,1)S(1)}, u32[]{:S(2)}, u32[]{:S(2)}) %collective-permute-start.1) | collective-permute-done | bytes 131104 | tf_op jit(solution)/shard_map/while/body/eval_jaxpr/ppermute | solution.py:13
  60.1 5.3 %collective-permute-done.1 = bf16[1,8,64,128]{3,2,1,0:T(8,128)(2,1)S(1)} collective-permute-done((bf16[1,8,64,128]{3,2,1,0:T(8,128)(2,1)S(1)}, bf16[1,8,64,128]{3,2,1,0:T(8,128)(2,1)S(1)}, u32[]{:S(2)}, u32[]{:S(2)}) %collective-permute-start.1) | collective-permute-done | bytes 131104 | tf_op jit(solution)/shard_map/while/body/eval_jaxpr/ppermute | solution.py:13
  70.2 5.3 %collective-permute-done.1 = bf16[1,8,64,128]{3,2,1,0:T(8,128)(2,1)S(1)} collective-permute-done((bf16[1,8,64,128]{3,2,1,0:T(8,128)(2,1)S(1)}, bf16[1,8,64,128]{3,2,1,0:T(8,128)(2,1)S(1)}, u32[]{:S(2)}, u32[]{:S(2)}) %collective-permute-start.1) | collective-permute-done | bytes 131104 | tf_op jit(solution)/shard_map/while/body/eval_jaxpr/ppermute | solution.py:13
  80.3 5.3 %collective-permute-done.1 = bf16[1,8,64,128]{3,2,1,0:T(8,128)(2,1)S(1)} collective-permute-done((bf16[1,8,64,128]{3,2,1,0:T(8,128)(2,1)S(1)}, bf16[1,8,64,128]{3,2,1,0:T(8,128)(2,1)S(1)}, u32[]{:S(2)}, u32[]{:S(2)}) %collective-permute-start.1) | collective-permute-done | bytes 131104 | tf_op jit(solution)/shard_map/while/body/eval_jaxpr/ppermute | solution.py:13
  90.1 7.4 %slice_bitcast_fusion = bf16[7,8,3,128,128]{4,3,2,1,0:T(8,128)(2,1)} fusion(bf16[8,8,1,3,128,128]{5,4,3,1,0,2:T(8,128)(2,1)} %bitcast.141), kind=kLoop, calls=%fused_computation.70 | loop fusion | bytes 11010048 | tf_op jit(solution)/shard_map/slice | solution.py:89
  99.0 72.2 %while.31 = (s32[]{:T(128)}, bf16[8,64,128]{2,1,0:T(8,128)(2,1)S(1)}, bf16[7,8,64,128]{3,2,1,0:T(8,128)(2,1)S(1)}, bf16[7,8,64,128]{3,2,1,0:T(8,128)(2,1)}, s32[...) while((s32[]{:T(128)}, ...), condition=%wide.region_3.4_spmd, body=%wide.region_2.3_spmd.sunk | while | flops 68944824 | bytes 4590617 | solution.py:86
  102.4 4.5 %collective-permute-done.3 = bf16[1,8,64,128]{3,2,1,0:T(8,128)(2,1)S(1)} collective-permute-done((bf16[1,8,64,128]{3,2,1,0:T(8,128)(2,1)S(1)}, bf16[1,8,64,128]{3,2,1,0:T(8,128)(2,1)S(1)}, u32[]{:S(2)}, u32[]{:S(2)}) %collective-permute-start.3) | collective-permute-done | bytes 131104 | tf_op jit(solution)/shard_map/while/body/eval_jaxpr/ppermute | solution.py:13
  112.7 4.6 %collective-permute-done.3 = bf16[1,8,64,128]{3,2,1,0:T(8,128)(2,1)S(1)} collective-permute-done((bf16[1,8,64,128]{3,2,1,0:T(8,128)(2,1)S(1)}, bf16[1,8,64,128]{3,2,1,0:T(8,128)(2,1)S(1)}, u32[]{:S(2)}, u32[]{:S(2)}) %collective-permute-start.3) | collective-permute-done | bytes 131104 | tf_op jit(solution)/shard_map/while/body/eval_jaxpr/ppermute | solution.py:13
  117.8 1.8 %bitcast_dynamic-update-slice_fusion.5 = (bf16[7,8,64,128]{3,2,1,0:T(8,128)(2,1)S(1)}, bf16[8,64,128]{2,1,0:T(8,128)(2,1)S(1)}) fusion(bf16[7,8,64,128]{3,2,1,0:T(8,128)(2,1)S(1)} %get-tuple-element.498, s32[]{:T(128)S(6)} %sub.88, bf16[7,8,128,128]{3,2,1,0:T(8,128)(2,1)S(1)} %get-tuple-element.516, ...), kind=kOutput, calls=%fused_computation.46.clone.1 | convolution fusion | flops 67371008 | bytes 1968128 | tf_op jit(solution)/shard_map/while/body/eval_jaxpr/vdj,voj->vdo/dot_general | solution.py:44
  123.0 4.6 %collective-permute-done.3 = bf16[1,8,64,128]{3,2,1,0:T(8,128)(2,1)S(1)} collective-permute-done((bf16[1,8,64,128]{3,2,1,0:T(8,128)(2,1)S(1)}, bf16[1,8,64,128]{3,2,1,0:T(8,128)(2,1)S(1)}, u32[]{:S(2)}, u32[]{:S(2)}) %collective-permute-start.3) | collective-permute-done | bytes 131104 | tf_op jit(solution)/shard_map/while/body/eval_jaxpr/ppermute | solution.py:13
  128.1 1.8 %bitcast_dynamic-update-slice_fusion.5 = (bf16[7,8,64,128]{3,2,1,0:T(8,128)(2,1)S(1)}, bf16[8,64,128]{2,1,0:T(8,128)(2,1)S(1)}) fusion(bf16[7,8,64,128]{3,2,1,0:T(8,128)(2,1)S(1)} %get-tuple-element.498, s32[]{:T(128)S(6)} %sub.88, bf16[7,8,128,128]{3,2,1,0:T(8,128)(2,1)S(1)} %get-tuple-element.516, ...), kind=kOutput, calls=%fused_computation.46.clone.1 | convolution fusion | flops 67371008 | bytes 1968128 | tf_op jit(solution)/shard_map/while/body/eval_jaxpr/vdj,voj->vdo/dot_general | solution.py:44
  133.3 4.5 %collective-permute-done.3 = bf16[1,8,64,128]{3,2,1,0:T(8,128)(2,1)S(1)} collective-permute-done((bf16[1,8,64,128]{3,2,1,0:T(8,128)(2,1)S(1)}, bf16[1,8,64,128]{3,2,1,0:T(8,128)(2,1)S(1)}, u32[]{:S(2)}, u32[]{:S(2)}) %collective-permute-start.3) | collective-permute-done | bytes 131104 | tf_op jit(solution)/shard_map/while/body/eval_jaxpr/ppermute | solution.py:13
  138.4 1.8 %bitcast_dynamic-update-slice_fusion.5 = (bf16[7,8,64,128]{3,2,1,0:T(8,128)(2,1)S(1)}, bf16[8,64,128]{2,1,0:T(8,128)(2,1)S(1)}) fusion(bf16[7,8,64,128]{3,2,1,0:T(8,128)(2,1)S(1)} %get-tuple-element.498, s32[]{:T(128)S(6)} %sub.88, bf16[7,8,128,128]{3,2,1,0:T(8,128)(2,1)S(1)} %get-tuple-element.516, ...), kind=kOutput, calls=%fused_computation.46.clone.1 | convolution fusion | flops 67371008 | bytes 1968128 | tf_op jit(solution)/shard_map/while/body/eval_jaxpr/vdj,voj->vdo/dot_general | solution.py:44
  143.6 4.5 %collective-permute-done.3 = bf16[1,8,64,128]{3,2,1,0:T(8,128)(2,1)S(1)} collective-permute-done((bf16[1,8,64,128]{3,2,1,0:T(8,128)(2,1)S(1)}, bf16[1,8,64,128]{3,2,1,0:T(8,128)(2,1)S(1)}, u32[]{:S(2)}, u32[]{:S(2)}) %collective-permute-start.3) | collective-permute-done | bytes 131104 | tf_op jit(solution)/shard_map/while/body/eval_jaxpr/ppermute | solution.py:13
  148.7 1.8 %bitcast_dynamic-update-slice_fusion.5 = (bf16[7,8,64,128]{3,2,1,0:T(8,128)(2,1)S(1)}, bf16[8,64,128]{2,1,0:T(8,128)(2,1)S(1)}) fusion(bf16[7,8,64,128]{3,2,1,0:T(8,128)(2,1)S(1)} %get-tuple-element.498, s32[]{:T(128)S(6)} %sub.88, bf16[7,8,128,128]{3,2,1,0:T(8,128)(2,1)S(1)} %get-tuple-element.516, ...), kind=kOutput, calls=%fused_computation.46.clone.1 | convolution fusion | flops 67371008 | bytes 1968128 | tf_op jit(solution)/shard_map/while/body/eval_jaxpr/vdj,voj->vdo/dot_general | solution.py:44
  153.9 4.6 %collective-permute-done.3 = bf16[1,8,64,128]{3,2,1,0:T(8,128)(2,1)S(1)} collective-permute-done((bf16[1,8,64,128]{3,2,1,0:T(8,128)(2,1)S(1)}, bf16[1,8,64,128]{3,2,1,0:T(8,128)(2,1)S(1)}, u32[]{:S(2)}, u32[]{:S(2)}) %collective-permute-start.3) | collective-permute-done | bytes 131104 | tf_op jit(solution)/shard_map/while/body/eval_jaxpr/ppermute | solution.py:13
  159.1 1.8 %bitcast_dynamic-update-slice_fusion.5 = (bf16[7,8,64,128]{3,2,1,0:T(8,128)(2,1)S(1)}, bf16[8,64,128]{2,1,0:T(8,128)(2,1)S(1)}) fusion(bf16[7,8,64,128]{3,2,1,0:T(8,128)(2,1)S(1)} %get-tuple-element.498, s32[]{:T(128)S(6)} %sub.88, bf16[7,8,128,128]{3,2,1,0:T(8,128)(2,1)S(1)} %get-tuple-element.516, ...), kind=kOutput, calls=%fused_computation.46.clone.1 | convolution fusion | flops 67371008 | bytes 1968128 | tf_op jit(solution)/shard_map/while/body/eval_jaxpr/vdj,voj->vdo/dot_general | solution.py:44
  164.3 4.5 %collective-permute-done.3 = bf16[1,8,64,128]{3,2,1,0:T(8,128)(2,1)S(1)} collective-permute-done((bf16[1,8,64,128]{3,2,1,0:T(8,128)(2,1)S(1)}, bf16[1,8,64,128]{3,2,1,0:T(8,128)(2,1)S(1)}, u32[]{:S(2)}, u32[]{:S(2)}) %collective-permute-start.3) | collective-permute-done | bytes 131104 | tf_op jit(solution)/shard_map/while/body/eval_jaxpr/ppermute | solution.py:13
  (189 shorter events, 62.6 us)
Async XLA Ops:
  9.4 10.3 %collective-permute-start = (bf16[1,8,64,128]{3,2,1,0:T(8,128)(2,1)S(1)}, bf16[1,8,64,128]{3,2,1,0:T(8,128)(2,1)S(1)}, u32[]{:S(2)}, u32[]{:S(2)}) collective-permute-start(bf16[1,8,64,128]{3,2,1,0:T(8,128)(2,1)S(1)} %bitcast.142), channel_id=1, source_target_pairs={{4,0},{8,4},{12,8},{16,12},{20,16},{24,20},{28,24},{32,28},{36,32}... | collective-permute-start | bytes 393224 | tf_op jit(solution)/shard_map/while/body/eval_jaxpr/ppermute | solution.py:16
  17.2 7.7 %collective-permute-start.1 = (bf16[1,8,64,128]{3,2,1,0:T(8,128)(2,1)S(1)}, bf16[1,8,64,128]{3,2,1,0:T(8,128)(2,1)S(1)}, u32[]{:S(2)}, u32[]{:S(2)}) collective-permute-start(bf16[1,8,64,128]{3,2,1,0:T(8,128)(2,1)S(1)} %bitcast.143), channel_id=1, source_target_pairs={{0,4},{4,8},{8,12},{12,16},{16,20},{20,24},{24,28},{28,32},{32,36}... | collective-permute-start | bytes 393224 | tf_op jit(solution)/shard_map/while/body/eval_jaxpr/ppermute | solution.py:13
  27.2 2.6 %collective-permute-start = (bf16[1,8,64,128]{3,2,1,0:T(8,128)(2,1)S(1)}, bf16[1,8,64,128]{3,2,1,0:T(8,128)(2,1)S(1)}, u32[]{:S(2)}, u32[]{:S(2)}) collective-permute-start(bf16[1,8,64,128]{3,2,1,0:T(8,128)(2,1)S(1)} %bitcast.142), channel_id=1, source_target_pairs={{4,0},{8,4},{12,8},{16,12},{20,16},{24,20},{28,24},{32,28},{36,32}... | collective-permute-start | bytes 393224 | tf_op jit(solution)/shard_map/while/body/eval_jaxpr/ppermute | solution.py:16
  27.3 7.8 %collective-permute-start.1 = (bf16[1,8,64,128]{3,2,1,0:T(8,128)(2,1)S(1)}, bf16[1,8,64,128]{3,2,1,0:T(8,128)(2,1)S(1)}, u32[]{:S(2)}, u32[]{:S(2)}) collective-permute-start(bf16[1,8,64,128]{3,2,1,0:T(8,128)(2,1)S(1)} %bitcast.143), channel_id=1, source_target_pairs={{0,4},{4,8},{8,12},{12,16},{16,20},{20,24},{24,28},{28,32},{32,36}... | collective-permute-start | bytes 393224 | tf_op jit(solution)/shard_map/while/body/eval_jaxpr/ppermute | solution.py:13
  37.4 7.8 %collective-permute-start.1 = (bf16[1,8,64,128]{3,2,1,0:T(8,128)(2,1)S(1)}, bf16[1,8,64,128]{3,2,1,0:T(8,128)(2,1)S(1)}, u32[]{:S(2)}, u32[]{:S(2)}) collective-permute-start(bf16[1,8,64,128]{3,2,1,0:T(8,128)(2,1)S(1)} %bitcast.143), channel_id=1, source_target_pairs={{0,4},{4,8},{8,12},{12,16},{16,20},{20,24},{24,28},{28,32},{32,36}... | collective-permute-start | bytes 393224 | tf_op jit(solution)/shard_map/while/body/eval_jaxpr/ppermute | solution.py:13
  47.4 2.6 %collective-permute-start = (bf16[1,8,64,128]{3,2,1,0:T(8,128)(2,1)S(1)}, bf16[1,8,64,128]{3,2,1,0:T(8,128)(2,1)S(1)}, u32[]{:S(2)}, u32[]{:S(2)}) collective-permute-start(bf16[1,8,64,128]{3,2,1,0:T(8,128)(2,1)S(1)} %bitcast.142), channel_id=1, source_target_pairs={{4,0},{8,4},{12,8},{16,12},{20,16},{24,20},{28,24},{32,28},{36,32}... | collective-permute-start | bytes 393224 | tf_op jit(solution)/shard_map/while/body/eval_jaxpr/ppermute | solution.py:16
  47.5 7.8 %collective-permute-start.1 = (bf16[1,8,64,128]{3,2,1,0:T(8,128)(2,1)S(1)}, bf16[1,8,64,128]{3,2,1,0:T(8,128)(2,1)S(1)}, u32[]{:S(2)}, u32[]{:S(2)}) collective-permute-start(bf16[1,8,64,128]{3,2,1,0:T(8,128)(2,1)S(1)} %bitcast.143), channel_id=1, source_target_pairs={{0,4},{4,8},{8,12},{12,16},{16,20},{20,24},{24,28},{28,32},{32,36}... | collective-permute-start | bytes 393224 | tf_op jit(solution)/shard_map/while/body/eval_jaxpr/ppermute | solution.py:13
  57.6 7.8 %collective-permute-start.1 = (bf16[1,8,64,128]{3,2,1,0:T(8,128)(2,1)S(1)}, bf16[1,8,64,128]{3,2,1,0:T(8,128)(2,1)S(1)}, u32[]{:S(2)}, u32[]{:S(2)}) collective-permute-start(bf16[1,8,64,128]{3,2,1,0:T(8,128)(2,1)S(1)} %bitcast.143), channel_id=1, source_target_pairs={{0,4},{4,8},{8,12},{12,16},{16,20},{20,24},{24,28},{28,32},{32,36}... | collective-permute-start | bytes 393224 | tf_op jit(solution)/shard_map/while/body/eval_jaxpr/ppermute | solution.py:13
  67.7 7.8 %collective-permute-start.1 = (bf16[1,8,64,128]{3,2,1,0:T(8,128)(2,1)S(1)}, bf16[1,8,64,128]{3,2,1,0:T(8,128)(2,1)S(1)}, u32[]{:S(2)}, u32[]{:S(2)}) collective-permute-start(bf16[1,8,64,128]{3,2,1,0:T(8,128)(2,1)S(1)} %bitcast.143), channel_id=1, source_target_pairs={{0,4},{4,8},{8,12},{12,16},{16,20},{20,24},{24,28},{28,32},{32,36}... | collective-permute-start | bytes 393224 | tf_op jit(solution)/shard_map/while/body/eval_jaxpr/ppermute | solution.py:13
  77.8 7.8 %collective-permute-start.1 = (bf16[1,8,64,128]{3,2,1,0:T(8,128)(2,1)S(1)}, bf16[1,8,64,128]{3,2,1,0:T(8,128)(2,1)S(1)}, u32[]{:S(2)}, u32[]{:S(2)}) collective-permute-start(bf16[1,8,64,128]{3,2,1,0:T(8,128)(2,1)S(1)} %bitcast.143), channel_id=1, source_target_pairs={{0,4},{4,8},{8,12},{12,16},{16,20},{20,24},{24,28},{28,32},{32,36}... | collective-permute-start | bytes 393224 | tf_op jit(solution)/shard_map/while/body/eval_jaxpr/ppermute | solution.py:13
  99.0 3.4 %collective-permute-start.2 = (bf16[1,8,64,128]{3,2,1,0:T(8,128)(2,1)S(1)}, bf16[1,8,64,128]{3,2,1,0:T(8,128)(2,1)S(1)}, u32[]{:S(2)}, u32[]{:S(2)}) collective-permute-start(bf16[1,8,64,128]{3,2,1,0:T(8,128)(2,1)S(1)} %bitcast.146), channel_id=1, source_target_pairs={{4,0},{8,4},{12,8},{16,12},{20,16},{24,20},{28,24},{32,28},{36,32}... | collective-permute-start | bytes 393224 | tf_op jit(solution)/shard_map/while/body/eval_jaxpr/ppermute | solution.py:16
  99.1 7.8 %collective-permute-start.3 = (bf16[1,8,64,128]{3,2,1,0:T(8,128)(2,1)S(1)}, bf16[1,8,64,128]{3,2,1,0:T(8,128)(2,1)S(1)}, u32[]{:S(2)}, u32[]{:S(2)}) collective-permute-start(bf16[1,8,64,128]{3,2,1,0:T(8,128)(2,1)S(1)} %bitcast.147), channel_id=1, source_target_pairs={{0,4},{4,8},{8,12},{12,16},{16,20},{20,24},{24,28},{28,32},{32,36}... | collective-permute-start | bytes 393224 | tf_op jit(solution)/shard_map/while/body/eval_jaxpr/ppermute | solution.py:13
  109.3 3.4 %collective-permute-start.2 = (bf16[1,8,64,128]{3,2,1,0:T(8,128)(2,1)S(1)}, bf16[1,8,64,128]{3,2,1,0:T(8,128)(2,1)S(1)}, u32[]{:S(2)}, u32[]{:S(2)}) collective-permute-start(bf16[1,8,64,128]{3,2,1,0:T(8,128)(2,1)S(1)} %bitcast.146), channel_id=1, source_target_pairs={{4,0},{8,4},{12,8},{16,12},{20,16},{24,20},{28,24},{32,28},{36,32}... | collective-permute-start | bytes 393224 | tf_op jit(solution)/shard_map/while/body/eval_jaxpr/ppermute | solution.py:16
  109.5 7.7 %collective-permute-start.3 = (bf16[1,8,64,128]{3,2,1,0:T(8,128)(2,1)S(1)}, bf16[1,8,64,128]{3,2,1,0:T(8,128)(2,1)S(1)}, u32[]{:S(2)}, u32[]{:S(2)}) collective-permute-start(bf16[1,8,64,128]{3,2,1,0:T(8,128)(2,1)S(1)} %bitcast.147), channel_id=1, source_target_pairs={{0,4},{4,8},{8,12},{12,16},{16,20},{20,24},{24,28},{28,32},{32,36}... | collective-permute-start | bytes 393224 | tf_op jit(solution)/shard_map/while/body/eval_jaxpr/ppermute | solution.py:13
  119.6 3.3 %collective-permute-start.2 = (bf16[1,8,64,128]{3,2,1,0:T(8,128)(2,1)S(1)}, bf16[1,8,64,128]{3,2,1,0:T(8,128)(2,1)S(1)}, u32[]{:S(2)}, u32[]{:S(2)}) collective-permute-start(bf16[1,8,64,128]{3,2,1,0:T(8,128)(2,1)S(1)} %bitcast.146), channel_id=1, source_target_pairs={{4,0},{8,4},{12,8},{16,12},{20,16},{24,20},{28,24},{32,28},{36,32}... | collective-permute-start | bytes 393224 | tf_op jit(solution)/shard_map/while/body/eval_jaxpr/ppermute | solution.py:16
  119.9 7.7 %collective-permute-start.3 = (bf16[1,8,64,128]{3,2,1,0:T(8,128)(2,1)S(1)}, bf16[1,8,64,128]{3,2,1,0:T(8,128)(2,1)S(1)}, u32[]{:S(2)}, u32[]{:S(2)}) collective-permute-start(bf16[1,8,64,128]{3,2,1,0:T(8,128)(2,1)S(1)} %bitcast.147), channel_id=1, source_target_pairs={{0,4},{4,8},{8,12},{12,16},{16,20},{20,24},{24,28},{28,32},{32,36}... | collective-permute-start | bytes 393224 | tf_op jit(solution)/shard_map/while/body/eval_jaxpr/ppermute | solution.py:13
  129.9 3.4 %collective-permute-start.2 = (bf16[1,8,64,128]{3,2,1,0:T(8,128)(2,1)S(1)}, bf16[1,8,64,128]{3,2,1,0:T(8,128)(2,1)S(1)}, u32[]{:S(2)}, u32[]{:S(2)}) collective-permute-start(bf16[1,8,64,128]{3,2,1,0:T(8,128)(2,1)S(1)} %bitcast.146), channel_id=1, source_target_pairs={{4,0},{8,4},{12,8},{16,12},{20,16},{24,20},{28,24},{32,28},{36,32}... | collective-permute-start | bytes 393224 | tf_op jit(solution)/shard_map/while/body/eval_jaxpr/ppermute | solution.py:16
  130.1 7.7 %collective-permute-start.3 = (bf16[1,8,64,128]{3,2,1,0:T(8,128)(2,1)S(1)}, bf16[1,8,64,128]{3,2,1,0:T(8,128)(2,1)S(1)}, u32[]{:S(2)}, u32[]{:S(2)}) collective-permute-start(bf16[1,8,64,128]{3,2,1,0:T(8,128)(2,1)S(1)} %bitcast.147), channel_id=1, source_target_pairs={{0,4},{4,8},{8,12},{12,16},{16,20},{20,24},{24,28},{28,32},{32,36}... | collective-permute-start | bytes 393224 | tf_op jit(solution)/shard_map/while/body/eval_jaxpr/ppermute | solution.py:13
  140.2 3.4 %collective-permute-start.2 = (bf16[1,8,64,128]{3,2,1,0:T(8,128)(2,1)S(1)}, bf16[1,8,64,128]{3,2,1,0:T(8,128)(2,1)S(1)}, u32[]{:S(2)}, u32[]{:S(2)}) collective-permute-start(bf16[1,8,64,128]{3,2,1,0:T(8,128)(2,1)S(1)} %bitcast.146), channel_id=1, source_target_pairs={{4,0},{8,4},{12,8},{16,12},{20,16},{24,20},{28,24},{32,28},{36,32}... | collective-permute-start | bytes 393224 | tf_op jit(solution)/shard_map/while/body/eval_jaxpr/ppermute | solution.py:16
  140.5 7.7 %collective-permute-start.3 = (bf16[1,8,64,128]{3,2,1,0:T(8,128)(2,1)S(1)}, bf16[1,8,64,128]{3,2,1,0:T(8,128)(2,1)S(1)}, u32[]{:S(2)}, u32[]{:S(2)}) collective-permute-start(bf16[1,8,64,128]{3,2,1,0:T(8,128)(2,1)S(1)} %bitcast.147), channel_id=1, source_target_pairs={{0,4},{4,8},{8,12},{12,16},{16,20},{20,24},{24,28},{28,32},{32,36}... | collective-permute-start | bytes 393224 | tf_op jit(solution)/shard_map/while/body/eval_jaxpr/ppermute | solution.py:13
  150.6 3.4 %collective-permute-start.2 = (bf16[1,8,64,128]{3,2,1,0:T(8,128)(2,1)S(1)}, bf16[1,8,64,128]{3,2,1,0:T(8,128)(2,1)S(1)}, u32[]{:S(2)}, u32[]{:S(2)}) collective-permute-start(bf16[1,8,64,128]{3,2,1,0:T(8,128)(2,1)S(1)} %bitcast.146), channel_id=1, source_target_pairs={{4,0},{8,4},{12,8},{16,12},{20,16},{24,20},{28,24},{32,28},{36,32}... | collective-permute-start | bytes 393224 | tf_op jit(solution)/shard_map/while/body/eval_jaxpr/ppermute | solution.py:16
  150.8 7.7 %collective-permute-start.3 = (bf16[1,8,64,128]{3,2,1,0:T(8,128)(2,1)S(1)}, bf16[1,8,64,128]{3,2,1,0:T(8,128)(2,1)S(1)}, u32[]{:S(2)}, u32[]{:S(2)}) collective-permute-start(bf16[1,8,64,128]{3,2,1,0:T(8,128)(2,1)S(1)} %bitcast.147), channel_id=1, source_target_pairs={{0,4},{4,8},{8,12},{12,16},{16,20},{20,24},{24,28},{28,32},{32,36}... | collective-permute-start | bytes 393224 | tf_op jit(solution)/shard_map/while/body/eval_jaxpr/ppermute | solution.py:13
  160.9 3.4 %collective-permute-start.2 = (bf16[1,8,64,128]{3,2,1,0:T(8,128)(2,1)S(1)}, bf16[1,8,64,128]{3,2,1,0:T(8,128)(2,1)S(1)}, u32[]{:S(2)}, u32[]{:S(2)}) collective-permute-start(bf16[1,8,64,128]{3,2,1,0:T(8,128)(2,1)S(1)} %bitcast.146), channel_id=1, source_target_pairs={{4,0},{8,4},{12,8},{16,12},{20,16},{24,20},{28,24},{32,28},{36,32}... | collective-permute-start | bytes 393224 | tf_op jit(solution)/shard_map/while/body/eval_jaxpr/ppermute | solution.py:16
  161.1 7.7 %collective-permute-start.3 = (bf16[1,8,64,128]{3,2,1,0:T(8,128)(2,1)S(1)}, bf16[1,8,64,128]{3,2,1,0:T(8,128)(2,1)S(1)}, u32[]{:S(2)}, u32[]{:S(2)}) collective-permute-start(bf16[1,8,64,128]{3,2,1,0:T(8,128)(2,1)S(1)} %bitcast.147), channel_id=1, source_target_pairs={{0,4},{4,8},{8,12},{12,16},{16,20},{20,24},{24,28},{28,32},{32,36}... | collective-permute-start | bytes 393224 | tf_op jit(solution)/shard_map/while/body/eval_jaxpr/ppermute | solution.py:13
  (11 other events, 107.8 us)
where the time goes:
time: 173 us; the launch traced here: 172 us
  waiting for transfers between devices  73 us (42%)
  matrix products  32.4 us (19%)
  local copies, waits for them, and re-layouts  29.2 us (17%)
  starting transfers between devices  15.4 us (9%)
  other arithmetic  12.7 us (7%)
  loops' own time  9.48 us (5%)
    ppermute x14, waiting for transfers between devices, extended(): lax.ppermute(lax.slice_in_dim(block, block.shape[dim] - width, None, axis...  68.7 us
    dot_general x8, matrix products, apply_inverse(): jnp.einsum('vdj,voj->vdo', summed_terms, inverted_tile_matrix, preferred_...  13.7 us
    dot_general x7, matrix products, select_terms(): jnp.einsum('lqfp,lqcp->lfc', chosen_entries, tile_collection, preferred_e...  11.5 us
    ppermute x14, starting transfers between devices, extended(): lax.ppermute(lax.slice_in_dim(block, 0, width, axis=dim), axis, backward)  9.79 us
    dynamic_slice x14, local copies, waits for them, and re-layouts, on_device(): lax.scan(forward, first_level, (lower_tile_group[1:], lower_index[1:], si...  8.38 us
    slice x1, local copies, waits for them, and re-layouts, on_device(): lower_tile_group[1:]  7.37 us
    slice x1, local copies, waits for them, and re-layouts, on_device(): upper_set[:-1]  7.37 us
    dot_general x14, matrix products, select_terms(): jnp.einsum('mkw,wmsb->mksb', select, window, preferred_element_type=jnp.f...  7.24 us
  transfers between devices with their start and end apart: 28, of which 21 were waited for; matrix products, arithmetic and copies ran while one was open for 12% of the time, Pallas kernels for 0%

commit v1 on v0

v1 whole, which is shorter than its diff:
```python
import functools
import jax
import jax.numpy as jnp
from jax import lax
from jax.experimental import pallas as pl
from jax.experimental.pallas import tpu as pltpu
from jax.sharding import PartitionSpec as P

LANES_LAST = (((1,), (1,)), ((), ()))


def times_transposed(left, right):
    return lax.dot_general(left, right, LANES_LAST, preferred_element_type=jnp.float32)


def prepare_kernel(level, with_inverse, place_ref, cols_ref, base_ref, tiles_ref, own_ref, *refs):
    if with_inverse:
        inverse_ref, total_ref, beside_ref, inverse_out = refs
        inverse_out[...] = inverse_ref[0, :, 0]
    else:
        total_ref, beside_ref = refs
    rows = own_ref.shape[0]
    span = place_ref[1]
    here = place_ref[0]
    partner = place_ref[2]
    other = place_ref[3]
    for m in range(rows):
        number = (level * rows + m) * span + here
        columns = [cols_ref[0, (level * rows + m) * 3 + k] for k in range(3)]
        spots = [jnp.where(c == number, -1, lax.rem(c, span)) for c in columns]

        def tile_of(spot):
            hits = [s == spot for s in spots]
            slot = jnp.where(hits[1], 1, jnp.where(hits[2], 2, 0))
            found = hits[0] | hits[1] | hits[2]
            tile = tiles_ref[0, m, 0, slot]
            return jnp.where(found, tile, jnp.zeros_like(tile))

        beside_ref[m, :, 0:128] = tile_of(partner)
        beside_ref[m, :, 128:256] = tile_of(other)
        base = base_ref[m] if len(base_ref.shape) == 3 else base_ref[0, m, 0]
        total_ref[m] = base.astype(jnp.float32) - times_transposed(own_ref[m], tile_of(here))


def prepare(level, place, columns, base, tiles, own, inverse=None):
    rows, sides, width = own.shape
    level_block = lambda a: pl.BlockSpec(
        (1,) + a.shape[1:], lambda i: (level,) + (0,) * (len(a.shape) - 1)
    )
    whole = lambda a: pl.BlockSpec(a.shape, lambda i: (0,) * len(a.shape))
    args = [place, columns, base, tiles, own]
    specs = [
        pl.BlockSpec(memory_space=pltpu.SMEM),
        pl.BlockSpec(memory_space=pltpu.SMEM),
        level_block(base) if len(base.shape) == 5 else whole(base),
        level_block(tiles),
        whole(own),
    ]
    shapes = [
        jax.ShapeDtypeStruct((rows, sides, width), jnp.float32),
        jax.ShapeDtypeStruct((rows, width, 2 * width), jnp.bfloat16),
    ]
    if inverse is not None:
        args.append(inverse)
        specs.append(level_block(inverse))
        shapes.append(jax.ShapeDtypeStruct((rows, width, width), jnp.bfloat16))
    return pl.pallas_call(
        functools.partial(prepare_kernel, level, inverse is not None),
        grid=(1,),
        out_shape=shapes,
        in_specs=specs,
        out_specs=[whole(s) for s in shapes],
        compiler_params=pltpu.CompilerParams(vmem_limit_bytes=12 << 20),
        cost_estimate=pl.CostEstimate(flops=20_000_000, bytes_accessed=4 << 20, transcendentals=0),
        name="prepare",
    )(*args)


def finish_kernel(with_inverse, near_ref, far_ref, total_ref, beside_ref, *refs):
    if with_inverse:
        inverse_ref, out_ref = refs
    else:
        (out_ref,) = refs
    for m in range(near_ref.shape[0]):
        both = jnp.concatenate([near_ref[m], far_ref[m]], axis=1)
        solved = (total_ref[m] - times_transposed(both, beside_ref[m])).astype(jnp.bfloat16)
        if with_inverse:
            solved = times_transposed(solved, inverse_ref[m]).astype(jnp.bfloat16)
        out_ref[m] = solved


def finish(near, far, total, beside, inverse=None):
    args = [near, far, total, beside] + ([] if inverse is None else [inverse])
    whole = pl.BlockSpec(memory_space=pltpu.VMEM)
    return pl.pallas_call(
        functools.partial(finish_kernel, inverse is not None),
        out_shape=jax.ShapeDtypeStruct(near.shape, jnp.bfloat16),
        in_specs=[whole] * len(args),
        out_specs=whole,
        compiler_params=pltpu.CompilerParams(vmem_limit_bytes=6 << 20),
        name="finish",
    )(*args)


def on_device(rhs, lower_tiles, lower_block_columns, upper_tiles, upper_cols, diag_inverse):
    span = lax.axis_size("blk")
    here = lax.axis_index("blk")
    levels, rows = rhs.shape[:2]
    odd = here % 2
    partner = here + 1 - 2 * odd
    other = (here - 1 + 2 * odd + span) % span
    place = jnp.stack([here, jnp.int32(span), partner, other]).astype(jnp.int32)
    lower_index = lower_block_columns.reshape(1, -1)
    upper_index = upper_cols.reshape(1, -1)
    pairs = [(i, i ^ 1) for i in range(span)]
    across = [(i, (i - 1 + 2 * (i % 2)) % span) for i in range(span)]

    def neighbours(block):
        far = lax.ppermute(block, "blk", across)
        near = lax.ppermute(block, "blk", pairs)
        return near, far

    solved = [rhs[0, :, 0].astype(jnp.bfloat16)]
    for level in range(1, levels):
        near, far = neighbours(solved[-1])
        last = level == levels - 1
        parts = prepare(
            level, place, lower_index, rhs, lower_tiles, solved[-1], diag_inverse if last else None
        )
        solved.append(finish(near, far, *parts))
    results = [solved.pop()]
    for level in range(levels - 2, -1, -1):
        near, far = neighbours(results[-1])
        parts = prepare(
            level, place, upper_index, solved[level], upper_tiles, results[-1], diag_inverse
        )
        results.append(finish(near, far, *parts))
    return jnp.stack(results[::-1])[:, :, None]


def solution(mesh):
    return jax.shard_map(
        on_device,
        mesh=mesh,
        in_specs=(
            P(None, None, "blk", "rhs", None),
            P(None, None, "blk", None, None, None),
            P(None, None, "blk", None),
            P(None, None, "blk", None, None, None),
            P(None, None, "blk", None),
            P(None, None, "blk", None, None),
        ),
        out_specs=P(None, None, "blk", "rhs", None),
        check_vma=False,
    )
```

time: 173 us -> 124 us (0.72)
  matrix products: 32.4 us -> 0 us
  Pallas kernels: 0 us -> 18.8 us
  local copies, waits for them, and re-layouts: 29.2 us -> 13.3 us
  other arithmetic: 12.7 us -> 0.08 us
  starting transfers between devices: 15.4 us -> 26.5 us
  loops' own time: 9.48 us -> 0 us
  waiting for transfers between devices: 73 us -> 64.9 us
    dot_general x29 -> x0, matrix products: 32.4 us -> none  [the longest x8 13.7 us: apply_inverse(): jnp.einsum('vdj,voj->vdo', summed_terms, inverted_tile_matrix, preferred_...]
    pallas_call x0 -> x28, Pallas kernels: none -> 18.8 us  [the longest x14 13 us: prepare(): pl.pallas_call(functools.partial(prepare_kernel, level, inverse is not No...]
    slice x9 -> x0, local copies, waits for them, and re-layouts: 16.2 us -> none  [the longest x1 7.37 us: on_device(): lower_tile_group[1:]]
    unnamed x12 -> x23, local copies, waits for them, and re-layouts: 0.64 us -> 12 us
    ppermute x28, starting transfers between devices: 15.4 us -> 26.5 us  [the longest x14 26.4 us: neighbours(): far = lax.ppermute(block, 'blk', across)]
    another operation x2 -> x0, loops' own time: 9.48 us -> none  [the longest x1 4.86 us: on_device(): lax.scan(forward, first_level, (lower_tile_group[1:], lower_index[1:], si...]
    dynamic_slice x14 -> x0, local copies, waits for them, and re-layouts: 8.38 us -> none  [on_device(): lax.scan(forward, first_level, (lower_tile_group[1:], lower_index[1:], si...]
    ppermute x28, waiting for transfers between devices: 73 us -> 64.9 us  [the longest x14 64.8 us: neighbours(): far = lax.ppermute(block, 'blk', across)]
  transfers between devices with their start and end apart: 28 -> 28, of which waited for: 21 -> 13; matrix products, arithmetic and copies ran while one was open for 12% -> 1% of each run, Pallas kernels for 0% -> 10%
where the time goes in v1:
time: 124 us
  waiting for transfers between devices  64.9 us (52%)
  starting transfers between devices  26.5 us (21%)
  Pallas kernels  18.8 us (15%)
  local copies, waits for them, and re-layouts  13.3 us (11%)
    ppermute x14, waiting for transfers between devices, neighbours(): far = lax.ppermute(block, 'blk', across)  64.8 us
    ppermute x14, starting transfers between devices, neighbours(): far = lax.ppermute(block, 'blk', across)  26.4 us
    pallas_call x14, Pallas kernels, prepare(): pl.pallas_call(functools.partial(prepare_kernel, level, inverse is not No...  13 us
    unnamed x23, local copies, waits for them, and re-layouts  12 us
    pallas_call x14, Pallas kernels, finish(): pl.pallas_call(functools.partial(finish_kernel, inverse is not None), out...  5.86 us
  transfers between devices with their start and end apart: 28, of which 13 were waited for; matrix products, arithmetic and copies ran while one was open for 1% of the time, Pallas kernels for 10%

profile of v1, /device:TPU:6, one launch (start us, length us, event | category | flops | bytes accessed | tf_op | source)
XLA Modules:
  0.0 123.7 jit_solution(12433527105962777874)
XLA Ops:
  1.0 7.8 %collective-permute-start.1 = (bf16[8,64,128]{2,1,0:T(8,128)(2,1)S(1)}, bf16[8,64,128]{2,1,0:T(8,128)(2,1)S(1)}, u32[]{:S(2)}, u32[]{:S(2)}) collective-permute-start(bf16[8,64,128]{2,1,0:T(8,128)(2,1)S(1)} %fusion.own_ref.base_ref), channel_id=1, source_target_pairs={{0,252},{4,8},{8,4},{12,16},{16,12},{20,24},{24,20},{28,32},{32,28... | collective-permute-start | bytes 393224 | tf_op jit(solution)/shard_map/ppermute | solution.py:119
  9.9 2.8 %copy-done = bf16[8,8,1,3,128,128]{5,4,3,2,1,0:T(8,128)(2,1)S(1)} copy-done((bf16[8,8,1,3,128,128]{5,4,3,2,1,0:T(8,128)(2,1)S(1)}, bf16[8,8,1,3,128,128]{5,4,3,2,1,0:T(8,128)(2,1)}, u32[]{:S(2)}) %copy-start) | copy-done | bytes 6291480
  12.6 1.6 %copy-done.4 = f32[8,8,1,64,128]{4,3,2,1,0:T(8,128)S(1)} copy-done((f32[8,8,1,64,128]{4,3,2,1,0:T(8,128)S(1)}, f32[8,8,1,64,128]{4,3,2,1,0:T(8,128)}, u32[]{:S(2)}) %copy-start.4) | copy-done | bytes 2097176
  17.8 5.5 %collective-permute-done.3.far_ref = bf16[8,64,128]{2,1,0:T(8,128)(2,1)S(1)} collective-permute-done((bf16[8,64,128]{2,1,0:T(8,128)(2,1)S(1)}, bf16[8,64,128]{2,1,0:T(8,128)(2,1)S(1)}, u32[]{:S(2)}, u32[]{:S(2)}) %collective-permute-start.3) | collective-permute-done | bytes 131104 | tf_op jit(solution)/shard_map/ppermute | solution.py:119
  25.9 5.5 %collective-permute-done.5.far_ref = bf16[8,64,128]{2,1,0:T(8,128)(2,1)S(1)} collective-permute-done((bf16[8,64,128]{2,1,0:T(8,128)(2,1)S(1)}, bf16[8,64,128]{2,1,0:T(8,128)(2,1)S(1)}, u32[]{:S(2)}, u32[]{:S(2)}) %collective-permute-start.5) | collective-permute-done | bytes 131104 | tf_op jit(solution)/shard_map/ppermute | solution.py:119
  34.1 5.5 %collective-permute-done.7.far_ref = bf16[8,64,128]{2,1,0:T(8,128)(2,1)S(1)} collective-permute-done((bf16[8,64,128]{2,1,0:T(8,128)(2,1)S(1)}, bf16[8,64,128]{2,1,0:T(8,128)(2,1)S(1)}, u32[]{:S(2)}, u32[]{:S(2)}) %collective-permute-start.7) | collective-permute-done | bytes 131104 | tf_op jit(solution)/shard_map/ppermute | solution.py:119
  42.2 5.5 %collective-permute-done.9.far_ref = bf16[8,64,128]{2,1,0:T(8,128)(2,1)S(1)} collective-permute-done((bf16[8,64,128]{2,1,0:T(8,128)(2,1)S(1)}, bf16[8,64,128]{2,1,0:T(8,128)(2,1)S(1)}, u32[]{:S(2)}, u32[]{:S(2)}) %collective-permute-start.9) | collective-permute-done | bytes 131104 | tf_op jit(solution)/shard_map/ppermute | solution.py:119
  50.3 5.5 %collective-permute-done.11.far_ref = bf16[8,64,128]{2,1,0:T(8,128)(2,1)S(1)} collective-permute-done((bf16[8,64,128]{2,1,0:T(8,128)(2,1)S(1)}, bf16[8,64,128]{2,1,0:T(8,128)(2,1)S(1)}, u32[]{:S(2)}, u32[]{:S(2)}) %collective-permute-start.11) | collective-permute-done | bytes 131104 | tf_op jit(solution)/shard_map/ppermute | solution.py:119
  58.4 5.4 %collective-permute-done.13.far_ref = bf16[8,64,128]{2,1,0:T(8,128)(2,1)S(1)} collective-permute-done((bf16[8,64,128]{2,1,0:T(8,128)(2,1)S(1)}, bf16[8,64,128]{2,1,0:T(8,128)(2,1)S(1)}, u32[]{:S(2)}, u32[]{:S(2)}) %collective-permute-start.13) | collective-permute-done | bytes 131104 | tf_op jit(solution)/shard_map/ppermute | solution.py:119
  66.0 2.8 %copy-done.1 = bf16[8,8,1,3,128,128]{5,4,3,2,1,0:T(8,128)(2,1)S(1)} copy-done((bf16[8,8,1,3,128,128]{5,4,3,2,1,0:T(8,128)(2,1)S(1)}, bf16[8,8,1,3,128,128]{5,4,3,2,1,0:T(8,128)(2,1)}, u32[]{:S(2)}) %copy-start.1) | copy-done | bytes 6291480
  69.7 2.4 %collective-permute-done.15.far_ref = bf16[8,64,128]{2,1,0:T(8,128)(2,1)S(1)} collective-permute-done((bf16[8,64,128]{2,1,0:T(8,128)(2,1)S(1)}, bf16[8,64,128]{2,1,0:T(8,128)(2,1)S(1)}, u32[]{:S(2)}, u32[]{:S(2)}) %collective-permute-start.15) | collective-permute-done | bytes 131104 | tf_op jit(solution)/shard_map/ppermute | solution.py:119
  72.7 1.4 %collective-permute-start.17 = (bf16[8,64,128]{2,1,0:T(8,128)(2,1)S(1)}, bf16[8,64,128]{2,1,0:T(8,128)(2,1)S(1)}, u32[]{:S(2)}, u32[]{:S(2)}) collective-permute-start(bf16[8,64,128]{2,1,0:T(8,128)(2,1)S(1)} %finish.21.own_ref), channel_id=1, source_target_pairs={{0,252},{4,8},{8,4},{12,16},{16,12},{20,24},{24,20},{28,32},{32,28... | collective-permute-start | bytes 393224 | tf_op jit(solution)/shard_map/ppermute | solution.py:119
  74.1 2.8 %copy-done.2 = bf16[8,8,1,3,128,128]{5,4,3,2,1,0:T(8,128)(2,1)S(1)} copy-done((bf16[8,8,1,3,128,128]{5,4,3,2,1,0:T(8,128)(2,1)S(1)}, bf16[8,8,1,3,128,128]{5,4,3,2,1,0:T(8,128)(2,1)}, u32[]{:S(2)}) %copy-start.2) | copy-done | bytes 6291480
  77.8 2.6 %collective-permute-done.17.far_ref = bf16[8,64,128]{2,1,0:T(8,128)(2,1)S(1)} collective-permute-done((bf16[8,64,128]{2,1,0:T(8,128)(2,1)S(1)}, bf16[8,64,128]{2,1,0:T(8,128)(2,1)S(1)}, u32[]{:S(2)}, u32[]{:S(2)}) %collective-permute-start.17) | collective-permute-done | bytes 131104 | tf_op jit(solution)/shard_map/ppermute | solution.py:119
  81.0 1.4 %collective-permute-start.19 = (bf16[8,64,128]{2,1,0:T(8,128)(2,1)S(1)}, bf16[8,64,128]{2,1,0:T(8,128)(2,1)S(1)}, u32[]{:S(2)}, u32[]{:S(2)}) collective-permute-start(bf16[8,64,128]{2,1,0:T(8,128)(2,1)S(1)} %finish.22.own_ref), channel_id=1, source_target_pairs={{0,252},{4,8},{8,4},{12,16},{16,12},{20,24},{24,20},{28,32},{32,28... | collective-permute-start | bytes 393224 | tf_op jit(solution)/shard_map/ppermute | solution.py:119
  83.4 5.4 %collective-permute-done.19.far_ref = bf16[8,64,128]{2,1,0:T(8,128)(2,1)S(1)} collective-permute-done((bf16[8,64,128]{2,1,0:T(8,128)(2,1)S(1)}, bf16[8,64,128]{2,1,0:T(8,128)(2,1)S(1)}, u32[]{:S(2)}, u32[]{:S(2)}) %collective-permute-start.19) | collective-permute-done | bytes 131104 | tf_op jit(solution)/shard_map/ppermute | solution.py:119
  89.3 1.4 %collective-permute-start.21 = (bf16[8,64,128]{2,1,0:T(8,128)(2,1)S(1)}, bf16[8,64,128]{2,1,0:T(8,128)(2,1)S(1)}, u32[]{:S(2)}, u32[]{:S(2)}) collective-permute-start(bf16[8,64,128]{2,1,0:T(8,128)(2,1)S(1)} %finish.23.own_ref), channel_id=1, source_target_pairs={{0,252},{4,8},{8,4},{12,16},{16,12},{20,24},{24,20},{28,32},{32,28... | collective-permute-start | bytes 393224 | tf_op jit(solution)/shard_map/ppermute | solution.py:119
  91.7 5.4 %collective-permute-done.21.far_ref = bf16[8,64,128]{2,1,0:T(8,128)(2,1)S(1)} collective-permute-done((bf16[8,64,128]{2,1,0:T(8,128)(2,1)S(1)}, bf16[8,64,128]{2,1,0:T(8,128)(2,1)S(1)}, u32[]{:S(2)}, u32[]{:S(2)}) %collective-permute-start.21) | collective-permute-done | bytes 131104 | tf_op jit(solution)/shard_map/ppermute | solution.py:119
  97.6 1.4 %collective-permute-start.23 = (bf16[8,64,128]{2,1,0:T(8,128)(2,1)S(1)}, bf16[8,64,128]{2,1,0:T(8,128)(2,1)S(1)}, u32[]{:S(2)}, u32[]{:S(2)}) collective-permute-start(bf16[8,64,128]{2,1,0:T(8,128)(2,1)S(1)} %finish.24.own_ref), channel_id=1, source_target_pairs={{0,252},{4,8},{8,4},{12,16},{16,12},{20,24},{24,20},{28,32},{32,28... | collective-permute-start | bytes 393224 | tf_op jit(solution)/shard_map/ppermute | solution.py:119
  100.0 5.4 %collective-permute-done.23.far_ref = bf16[8,64,128]{2,1,0:T(8,128)(2,1)S(1)} collective-permute-done((bf16[8,64,128]{2,1,0:T(8,128)(2,1)S(1)}, bf16[8,64,128]{2,1,0:T(8,128)(2,1)S(1)}, u32[]{:S(2)}, u32[]{:S(2)}) %collective-permute-start.23) | collective-permute-done | bytes 131104 | tf_op jit(solution)/shard_map/ppermute | solution.py:119
  105.9 1.4 %collective-permute-start.25 = (bf16[8,64,128]{2,1,0:T(8,128)(2,1)S(1)}, bf16[8,64,128]{2,1,0:T(8,128)(2,1)S(1)}, u32[]{:S(2)}, u32[]{:S(2)}) collective-permute-start(bf16[8,64,128]{2,1,0:T(8,128)(2,1)S(1)} %finish.25.own_ref), channel_id=1, source_target_pairs={{0,252},{4,8},{8,4},{12,16},{16,12},{20,24},{24,20},{28,32},{32,28... | collective-permute-start | bytes 393224 | tf_op jit(solution)/shard_map/ppermute | solution.py:119
  108.3 5.4 %collective-permute-done.25.far_ref = bf16[8,64,128]{2,1,0:T(8,128)(2,1)S(1)} collective-permute-done((bf16[8,64,128]{2,1,0:T(8,128)(2,1)S(1)}, bf16[8,64,128]{2,1,0:T(8,128)(2,1)S(1)}, u32[]{:S(2)}, u32[]{:S(2)}) %collective-permute-start.25) | collective-permute-done | bytes 131104 | tf_op jit(solution)/shard_map/ppermute | solution.py:119
  114.2 1.4 %collective-permute-start.27 = (bf16[8,64,128]{2,1,0:T(8,128)(2,1)S(1)}, bf16[8,64,128]{2,1,0:T(8,128)(2,1)S(1)}, u32[]{:S(2)}, u32[]{:S(2)}) collective-permute-start(bf16[8,64,128]{2,1,0:T(8,128)(2,1)S(1)} %finish.26.own_ref), channel_id=1, source_target_pairs={{0,252},{4,8},{8,4},{12,16},{16,12},{20,24},{24,20},{28,32},{32,28... | collective-permute-start | bytes 393224 | tf_op jit(solution)/shard_map/ppermute | solution.py:119
  116.6 5.4 %collective-permute-done.27.far_ref = bf16[8,64,128]{2,1,0:T(8,128)(2,1)S(1)} collective-permute-done((bf16[8,64,128]{2,1,0:T(8,128)(2,1)S(1)}, bf16[8,64,128]{2,1,0:T(8,128)(2,1)S(1)}, u32[]{:S(2)}, u32[]{:S(2)}) %collective-permute-start.27) | collective-permute-done | bytes 131104 | tf_op jit(solution)/shard_map/ppermute | solution.py:119
  (88 shorter events, 32.3 us)
Async XLA Ops:
  1.0 14.2 %collective-permute-start.1 = (bf16[8,64,128]{2,1,0:T(8,128)(2,1)S(1)}, bf16[8,64,128]{2,1,0:T(8,128)(2,1)S(1)}, u32[]{:S(2)}, u32[]{:S(2)}) collective-permute-start(bf16[8,64,128]{2,1,0:T(8,128)(2,1)S(1)} %fusion.own_ref.base_ref), channel_id=1, source_target_pairs={{0,252},{4,8},{8,4},{12,16},{16,12},{20,24},{24,20},{28,32},{32,28... | collective-permute-start | bytes 393224 | tf_op jit(solution)/shard_map/ppermute | solution.py:119
  8.8 6.4 %collective-permute-start = (bf16[8,64,128]{2,1,0:T(8,128)(2,1)S(1)}, bf16[8,64,128]{2,1,0:T(8,128)(2,1)S(1)}, u32[]{:S(2)}, u32[]{:S(2)}) collective-permute-start(bf16[8,64,128]{2,1,0:T(8,128)(2,1)S(1)} %fusion.own_ref.base_ref), channel_id=1, source_target_pairs={{0,4},{4,0},{8,12},{12,8},{16,20},{20,16},{24,28},{28,24},{32,36},... | collective-permute-start | bytes 393224 | tf_op jit(solution)/shard_map/ppermute | solution.py:120
  15.5 7.8 %collective-permute-start.3 = (bf16[8,64,128]{2,1,0:T(8,128)(2,1)S(1)}, bf16[8,64,128]{2,1,0:T(8,128)(2,1)S(1)}, u32[]{:S(2)}, u32[]{:S(2)}) collective-permute-start(bf16[8,64,128]{2,1,0:T(8,128)(2,1)S(1)} %finish.14.own_ref.base_ref), channel_id=1, source_target_pairs={{0,252},{4,8},{8,4},{12,16},{16,12},{20,24},{24,20},{28,32},{32,28... | collective-permute-start | bytes 393224 | tf_op jit(solution)/shard_map/ppermute | solution.py:119
  16.9 6.4 %collective-permute-start.2 = (bf16[8,64,128]{2,1,0:T(8,128)(2,1)S(1)}, bf16[8,64,128]{2,1,0:T(8,128)(2,1)S(1)}, u32[]{:S(2)}, u32[]{:S(2)}) collective-permute-start(bf16[8,64,128]{2,1,0:T(8,128)(2,1)S(1)} %finish.14.own_ref.base_ref), channel_id=1, source_target_pairs={{0,4},{4,0},{8,12},{12,8},{16,20},{20,16},{24,28},{28,24},{32,36},... | collective-permute-start | bytes 393224 | tf_op jit(solution)/shard_map/ppermute | solution.py:120
  23.6 7.8 %collective-permute-start.5 = (bf16[8,64,128]{2,1,0:T(8,128)(2,1)S(1)}, bf16[8,64,128]{2,1,0:T(8,128)(2,1)S(1)}, u32[]{:S(2)}, u32[]{:S(2)}) collective-permute-start(bf16[8,64,128]{2,1,0:T(8,128)(2,1)S(1)} %finish.15.own_ref.base_ref), channel_id=1, source_target_pairs={{0,252},{4,8},{8,4},{12,16},{16,12},{20,24},{24,20},{28,32},{32,28... | collective-permute-start | bytes 393224 | tf_op jit(solution)/shard_map/ppermute | solution.py:119
  25.0 6.4 %collective-permute-start.4 = (bf16[8,64,128]{2,1,0:T(8,128)(2,1)S(1)}, bf16[8,64,128]{2,1,0:T(8,128)(2,1)S(1)}, u32[]{:S(2)}, u32[]{:S(2)}) collective-permute-start(bf16[8,64,128]{2,1,0:T(8,128)(2,1)S(1)} %finish.15.own_ref.base_ref), channel_id=1, source_target_pairs={{0,4},{4,0},{8,12},{12,8},{16,20},{20,16},{24,28},{28,24},{32,36},... | collective-permute-start | bytes 393224 | tf_op jit(solution)/shard_map/ppermute | solution.py:120
  31.7 7.8 %collective-permute-start.7 = (bf16[8,64,128]{2,1,0:T(8,128)(2,1)S(1)}, bf16[8,64,128]{2,1,0:T(8,128)(2,1)S(1)}, u32[]{:S(2)}, u32[]{:S(2)}) collective-permute-start(bf16[8,64,128]{2,1,0:T(8,128)(2,1)S(1)} %finish.16.own_ref.base_ref), channel_id=1, source_target_pairs={{0,252},{4,8},{8,4},{12,16},{16,12},{20,24},{24,20},{28,32},{32,28... | collective-permute-start | bytes 393224 | tf_op jit(solution)/shard_map/ppermute | solution.py:119
  33.1 6.4 %collective-permute-start.6 = (bf16[8,64,128]{2,1,0:T(8,128)(2,1)S(1)}, bf16[8,64,128]{2,1,0:T(8,128)(2,1)S(1)}, u32[]{:S(2)}, u32[]{:S(2)}) collective-permute-start(bf16[8,64,128]{2,1,0:T(8,128)(2,1)S(1)} %finish.16.own_ref.base_ref), channel_id=1, source_target_pairs={{0,4},{4,0},{8,12},{12,8},{16,20},{20,16},{24,28},{28,24},{32,36},... | collective-permute-start | bytes 393224 | tf_op jit(solution)/shard_map/ppermute | solution.py:120
  39.8 7.8 %collective-permute-start.9 = (bf16[8,64,128]{2,1,0:T(8,128)(2,1)S(1)}, bf16[8,64,128]{2,1,0:T(8,128)(2,1)S(1)}, u32[]{:S(2)}, u32[]{:S(2)}) collective-permute-start(bf16[8,64,128]{2,1,0:T(8,128)(2,1)S(1)} %finish.17.own_ref.base_ref), channel_id=1, source_target_pairs={{0,252},{4,8},{8,4},{12,16},{16,12},{20,24},{24,20},{28,32},{32,28... | collective-permute-start | bytes 393224 | tf_op jit(solution)/shard_map/ppermute | solution.py:119
  41.2 6.4 %collective-permute-start.8 = (bf16[8,64,128]{2,1,0:T(8,128)(2,1)S(1)}, bf16[8,64,128]{2,1,0:T(8,128)(2,1)S(1)}, u32[]{:S(2)}, u32[]{:S(2)}) collective-permute-start(bf16[8,64,128]{2,1,0:T(8,128)(2,1)S(1)} %finish.17.own_ref.base_ref), channel_id=1, source_target_pairs={{0,4},{4,0},{8,12},{12,8},{16,20},{20,16},{24,28},{28,24},{32,36},... | collective-permute-start | bytes 393224 | tf_op jit(solution)/shard_map/ppermute | solution.py:120
  47.9 7.8 %collective-permute-start.11 = (bf16[8,64,128]{2,1,0:T(8,128)(2,1)S(1)}, bf16[8,64,128]{2,1,0:T(8,128)(2,1)S(1)}, u32[]{:S(2)}, u32[]{:S(2)}) collective-permute-start(bf16[8,64,128]{2,1,0:T(8,128)(2,1)S(1)} %finish.18.own_ref.base_ref), channel_id=1, source_target_pairs={{0,252},{4,8},{8,4},{12,16},{16,12},{20,24},{24,20},{28,32},{32,28... | collective-permute-start | bytes 393224 | tf_op jit(solution)/shard_map/ppermute | solution.py:119
  49.3 6.4 %collective-permute-start.10 = (bf16[8,64,128]{2,1,0:T(8,128)(2,1)S(1)}, bf16[8,64,128]{2,1,0:T(8,128)(2,1)S(1)}, u32[]{:S(2)}, u32[]{:S(2)}) collective-permute-start(bf16[8,64,128]{2,1,0:T(8,128)(2,1)S(1)} %finish.18.own_ref.base_ref), channel_id=1, source_target_pairs={{0,4},{4,0},{8,12},{12,8},{16,20},{20,16},{24,28},{28,24},{32,36},... | collective-permute-start | bytes 393224 | tf_op jit(solution)/shard_map/ppermute | solution.py:120
  56.0 7.8 %collective-permute-start.13 = (bf16[8,64,128]{2,1,0:T(8,128)(2,1)S(1)}, bf16[8,64,128]{2,1,0:T(8,128)(2,1)S(1)}, u32[]{:S(2)}, u32[]{:S(2)}) collective-permute-start(bf16[8,64,128]{2,1,0:T(8,128)(2,1)S(1)} %finish.19.own_ref.base_ref), channel_id=1, source_target_pairs={{0,252},{4,8},{8,4},{12,16},{16,12},{20,24},{24,20},{28,32},{32,28... | collective-permute-start | bytes 393224 | tf_op jit(solution)/shard_map/ppermute | solution.py:119
  57.5 6.4 %collective-permute-start.12 = (bf16[8,64,128]{2,1,0:T(8,128)(2,1)S(1)}, bf16[8,64,128]{2,1,0:T(8,128)(2,1)S(1)}, u32[]{:S(2)}, u32[]{:S(2)}) collective-permute-start(bf16[8,64,128]{2,1,0:T(8,128)(2,1)S(1)} %finish.19.own_ref.base_ref), channel_id=1, source_target_pairs={{0,4},{4,0},{8,12},{12,8},{16,20},{20,16},{24,28},{28,24},{32,36},... | collective-permute-start | bytes 393224 | tf_op jit(solution)/shard_map/ppermute | solution.py:120
  64.3 7.8 %collective-permute-start.15 = (bf16[8,64,128]{2,1,0:T(8,128)(2,1)S(1)}, bf16[8,64,128]{2,1,0:T(8,128)(2,1)S(1)}, u32[]{:S(2)}, u32[]{:S(2)}) collective-permute-start(bf16[8,64,128]{2,1,0:T(8,128)(2,1)S(1)} %finish.20.own_ref), channel_id=1, source_target_pairs={{0,252},{4,8},{8,4},{12,16},{16,12},{20,24},{24,20},{28,32},{32,28... | collective-permute-start | bytes 393224 | tf_op jit(solution)/shard_map/ppermute | solution.py:119
  65.8 6.4 %collective-permute-start.14 = (bf16[8,64,128]{2,1,0:T(8,128)(2,1)S(1)}, bf16[8,64,128]{2,1,0:T(8,128)(2,1)S(1)}, u32[]{:S(2)}, u32[]{:S(2)}) collective-permute-start(bf16[8,64,128]{2,1,0:T(8,128)(2,1)S(1)} %finish.20.own_ref), channel_id=1, source_target_pairs={{0,4},{4,0},{8,12},{12,8},{16,20},{20,16},{24,28},{28,24},{32,36},... | collective-permute-start | bytes 393224 | tf_op jit(solution)/shard_map/ppermute | solution.py:120
  72.7 7.8 %collective-permute-start.17 = (bf16[8,64,128]{2,1,0:T(8,128)(2,1)S(1)}, bf16[8,64,128]{2,1,0:T(8,128)(2,1)S(1)}, u32[]{:S(2)}, u32[]{:S(2)}) collective-permute-start(bf16[8,64,128]{2,1,0:T(8,128)(2,1)S(1)} %finish.21.own_ref), channel_id=1, source_target_pairs={{0,252},{4,8},{8,4},{12,16},{16,12},{20,24},{24,20},{28,32},{32,28... | collective-permute-start | bytes 393224 | tf_op jit(solution)/shard_map/ppermute | solution.py:119
  81.0 7.8 %collective-permute-start.19 = (bf16[8,64,128]{2,1,0:T(8,128)(2,1)S(1)}, bf16[8,64,128]{2,1,0:T(8,128)(2,1)S(1)}, u32[]{:S(2)}, u32[]{:S(2)}) collective-permute-start(bf16[8,64,128]{2,1,0:T(8,128)(2,1)S(1)} %finish.22.own_ref), channel_id=1, source_target_pairs={{0,252},{4,8},{8,4},{12,16},{16,12},{20,24},{24,20},{28,32},{32,28... | collective-permute-start | bytes 393224 | tf_op jit(solution)/shard_map/ppermute | solution.py:119
  89.3 7.8 %collective-permute-start.21 = (bf16[8,64,128]{2,1,0:T(8,128)(2,1)S(1)}, bf16[8,64,128]{2,1,0:T(8,128)(2,1)S(1)}, u32[]{:S(2)}, u32[]{:S(2)}) collective-permute-start(bf16[8,64,128]{2,1,0:T(8,128)(2,1)S(1)} %finish.23.own_ref), channel_id=1, source_target_pairs={{0,252},{4,8},{8,4},{12,16},{16,12},{20,24},{24,20},{28,32},{32,28... | collective-permute-start | bytes 393224 | tf_op jit(solution)/shard_map/ppermute | solution.py:119
  97.6 7.8 %collective-permute-start.23 = (bf16[8,64,128]{2,1,0:T(8,128)(2,1)S(1)}, bf16[8,64,128]{2,1,0:T(8,128)(2,1)S(1)}, u32[]{:S(2)}, u32[]{:S(2)}) collective-permute-start(bf16[8,64,128]{2,1,0:T(8,128)(2,1)S(1)} %finish.24.own_ref), channel_id=1, source_target_pairs={{0,252},{4,8},{8,4},{12,16},{16,12},{20,24},{24,20},{28,32},{32,28... | collective-permute-start | bytes 393224 | tf_op jit(solution)/shard_map/ppermute | solution.py:119
  105.9 7.8 %collective-permute-start.25 = (bf16[8,64,128]{2,1,0:T(8,128)(2,1)S(1)}, bf16[8,64,128]{2,1,0:T(8,128)(2,1)S(1)}, u32[]{:S(2)}, u32[]{:S(2)}) collective-permute-start(bf16[8,64,128]{2,1,0:T(8,128)(2,1)S(1)} %finish.25.own_ref), channel_id=1, source_target_pairs={{0,252},{4,8},{8,4},{12,16},{16,12},{20,24},{24,20},{28,32},{32,28... | collective-permute-start | bytes 393224 | tf_op jit(solution)/shard_map/ppermute | solution.py:119
  107.3 6.4 %collective-permute-start.24 = (bf16[8,64,128]{2,1,0:T(8,128)(2,1)S(1)}, bf16[8,64,128]{2,1,0:T(8,128)(2,1)S(1)}, u32[]{:S(2)}, u32[]{:S(2)}) collective-permute-start(bf16[8,64,128]{2,1,0:T(8,128)(2,1)S(1)} %finish.25.own_ref), channel_id=1, source_target_pairs={{0,4},{4,0},{8,12},{12,8},{16,20},{20,16},{24,28},{28,24},{32,36},... | collective-permute-start | bytes 393224 | tf_op jit(solution)/shard_map/ppermute | solution.py:120
  114.2 7.8 %collective-permute-start.27 = (bf16[8,64,128]{2,1,0:T(8,128)(2,1)S(1)}, bf16[8,64,128]{2,1,0:T(8,128)(2,1)S(1)}, u32[]{:S(2)}, u32[]{:S(2)}) collective-permute-start(bf16[8,64,128]{2,1,0:T(8,128)(2,1)S(1)} %finish.26.own_ref), channel_id=1, source_target_pairs={{0,252},{4,8},{8,4},{12,16},{16,12},{20,24},{24,20},{28,32},{32,28... | collective-permute-start | bytes 393224 | tf_op jit(solution)/shard_map/ppermute | solution.py:119
  115.7 6.4 %collective-permute-start.26 = (bf16[8,64,128]{2,1,0:T(8,128)(2,1)S(1)}, bf16[8,64,128]{2,1,0:T(8,128)(2,1)S(1)}, u32[]{:S(2)}, u32[]{:S(2)}) collective-permute-start(bf16[8,64,128]{2,1,0:T(8,128)(2,1)S(1)} %finish.26.own_ref), channel_id=1, source_target_pairs={{0,4},{4,0},{8,12},{12,8},{16,20},{20,16},{24,28},{28,24},{32,36},... | collective-permute-start | bytes 393224 | tf_op jit(solution)/shard_map/ppermute | solution.py:120
  (11 other events, 54.2 us)

commit v2 on v1

v2 whole, which is shorter than its diff:
```python
import functools
import jax
import jax.numpy as jnp
from jax import lax
from jax.experimental import pallas as pl
from jax.experimental.pallas import tpu as pltpu
from jax.sharding import PartitionSpec as P

LANES_LAST = (((1,), (1,)), ((), ()))


def times_transposed(left, right):
    return lax.dot_general(left, right, LANES_LAST, preferred_element_type=jnp.float32)


def two_parts(value):
    coarse = value.astype(jnp.bfloat16)
    fine = (value - coarse.astype(jnp.float32)).astype(jnp.bfloat16)
    return jnp.concatenate([coarse, fine], axis=1)


def prepare_kernel(level, with_inverse, write_to, continued, place_ref, cols_ref, base_ref, tiles_ref, own_ref, near_ref, *refs):
    refs = list(refs)
    inverse_ref = refs.pop(0) if with_inverse else None
    if continued:
        refs.pop(0)
    total_ref, beside_ref = refs[:2]
    if write_to is not None:
        result_ref, sem = refs[2:]
        copy = pltpu.make_async_copy(own_ref, result_ref.at[write_to, :, 0], sem)
        copy.start()
    rows = own_ref.shape[0]
    here, span, partner, other = place_ref[0], place_ref[1], place_ref[2], place_ref[3]
    for m in range(rows):
        number = (level * rows + m) * span + here
        columns = [cols_ref[0, (level * rows + m) * 3 + k] for k in range(3)]
        spots = [jnp.where(c == number, -1, lax.rem(c, span)) for c in columns]

        def tile_of(spot):
            hits = [s == spot for s in spots]
            slot = jnp.where(hits[1], 1, jnp.where(hits[2], 2, 0))
            tile = tiles_ref[0, m, 0, slot]
            return jnp.where(hits[0] | hits[1] | hits[2], tile, jnp.zeros_like(tile))

        base = base_ref[m] if len(base_ref.shape) == 3 else base_ref[0, m, 0]
        both = jnp.concatenate([own_ref[m], near_ref[m]], axis=1)
        tiles = jnp.concatenate([tile_of(here), tile_of(partner)], axis=1)
        total = base.astype(jnp.float32) - times_transposed(both, tiles)
        if with_inverse:
            inverse = inverse_ref[0, m, 0]
            total = times_transposed(two_parts(total), jnp.concatenate([inverse, inverse], axis=1))
            beside_ref[m] = two_parts(
                jnp.dot(inverse, tile_of(other), preferred_element_type=jnp.float32)
            )
        else:
            beside_ref[m] = tile_of(other)
        total_ref[m] = total
    if write_to is not None:
        copy.wait()


def prepare(level, place, columns, base, tiles, own, near, inverse, write_to, result, result_shape):
    rows, sides, width = own.shape
    level_block = lambda a: pl.BlockSpec(
        (1,) + a.shape[1:], lambda i: (level,) + (0,) * (len(a.shape) - 1)
    )
    whole = lambda a: pl.BlockSpec(a.shape, lambda i: (0,) * len(a.shape))
    args = [place, columns, base, tiles, own, near]
    specs = [
        pl.BlockSpec(memory_space=pltpu.SMEM),
        pl.BlockSpec(memory_space=pltpu.SMEM),
        level_block(base) if len(base.shape) == 5 else whole(base),
        level_block(tiles),
        whole(own),
        whole(near),
    ]
    deep = width if inverse is None else 2 * width
    shapes = [
        jax.ShapeDtypeStruct((rows, sides, width), jnp.float32),
        jax.ShapeDtypeStruct((rows, width, deep), jnp.bfloat16),
    ]
    out_specs = [whole(s) for s in shapes]
    if inverse is not None:
        args.append(inverse)
        specs.append(level_block(inverse))
    aliases = {}
    if write_to is not None:
        shapes.append(result_shape)
        out_specs.append(pl.BlockSpec(memory_space=pltpu.HBM))
        if result is not None:
            aliases = {len(args): 2}
            args.append(result)
            specs.append(pl.BlockSpec(memory_space=pltpu.HBM))
    return pl.pallas_call(
        functools.partial(
            prepare_kernel, level, inverse is not None, write_to, result is not None
        ),
        grid=(1,),
        out_shape=shapes,
        in_specs=specs,
        out_specs=out_specs,
        scratch_shapes=[pltpu.SemaphoreType.DMA] if write_to is not None else [],
        input_output_aliases=aliases,
        compiler_params=pltpu.CompilerParams(vmem_limit_bytes=12 << 20),
        cost_estimate=pl.CostEstimate(flops=20_000_000, bytes_accessed=4 << 20, transcendentals=0),
        name="prepare",
    )(*args)


def finish_kernel(write_to, far_ref, total_ref, beside_ref, *refs):
    if write_to is None:
        (out_ref,) = refs
    else:
        _, result_ref, out_ref, sem = refs
    for m in range(far_ref.shape[0]):
        far = far_ref[m]
        if beside_ref.shape[2] == 2 * far.shape[1]:
            far = jnp.concatenate([far, far], axis=1)
        out_ref[m] = (total_ref[m] - times_transposed(far, beside_ref[m])).astype(jnp.bfloat16)
    if write_to is not None:
        copy = pltpu.make_async_copy(out_ref, result_ref.at[write_to, :, 0], sem)
        copy.start()
        copy.wait()


def finish(far, total, beside, write_to=None, result=None):
    whole = pl.BlockSpec(memory_space=pltpu.VMEM)
    args, specs = [far, total, beside], [whole] * 3
    more = {}
    out, out_spec = jax.ShapeDtypeStruct(far.shape, jnp.bfloat16), whole
    if write_to is not None:
        out, out_spec = jax.ShapeDtypeStruct(result.shape, result.dtype), pl.BlockSpec(memory_space=pltpu.HBM)
        args.append(result)
        specs.append(out_spec)
        more = dict(
            input_output_aliases={3: 0},
            scratch_shapes=[pltpu.VMEM(far.shape, jnp.bfloat16), pltpu.SemaphoreType.DMA],
        )
    return pl.pallas_call(
        functools.partial(finish_kernel, write_to),
        out_shape=out,
        in_specs=specs,
        out_specs=out_spec,
        compiler_params=pltpu.CompilerParams(vmem_limit_bytes=6 << 20),
        name="finish",
        **more,
    )(*args)


def on_device(rhs, lower_tiles, lower_block_columns, upper_tiles, upper_cols, diag_inverse):
    span = lax.axis_size("blk")
    here = lax.axis_index("blk")
    levels, rows, _, sides, width = rhs.shape
    odd = here % 2
    partner = here + 1 - 2 * odd
    other = (here - 1 + 2 * odd + span) % span
    place = jnp.stack([here, jnp.int32(span), partner, other]).astype(jnp.int32)
    lower_index = lower_block_columns.reshape(1, -1)
    upper_index = upper_cols.reshape(1, -1)
    pairs = [(i, i ^ 1) for i in range(span)]
    across = [(i, (i - 1 + 2 * (i % 2)) % span) for i in range(span)]
    result_shape = jax.ShapeDtypeStruct(rhs.shape, jnp.bfloat16)

    solved = [rhs[0, :, 0].astype(jnp.bfloat16)]
    current, result = solved[0], None
    steps = [(True, l) for l in range(1, levels)] + [(False, l) for l in range(levels - 2, -1, -1)]
    for forward, level in steps:
        tail = level == levels - 1 or not forward
        far = lax.ppermute(current, "blk", across)
        near = lax.ppermute(current, "blk", pairs)
        parts = prepare(
            level,
            place,
            lower_index if forward else upper_index,
            rhs if forward else solved[level],
            lower_tiles if forward else upper_tiles,
            current,
            near,
            diag_inverse if tail else None,
            None if forward else level + 1,
            result,
            result_shape,
        )
        if not forward:
            result = parts[2]
        if level or forward:
            current = finish(far, parts[0], parts[1])
        else:
            result = finish(far, parts[0], parts[1], level, result)
        if forward:
            solved.append(current)
    return result


def solution(mesh):
    return jax.shard_map(
        on_device,
        mesh=mesh,
        in_specs=(
            P(None, None, "blk", "rhs", None),
            P(None, None, "blk", None, None, None),
            P(None, None, "blk", None),
            P(None, None, "blk", None, None, None),
            P(None, None, "blk", None),
            P(None, None, "blk", None, None),
        ),
        out_specs=P(None, None, "blk", "rhs", None),
        check_vma=False,
    )
```

time: 124 us -> 124 us (level)
  waiting for transfers between devices: 64.9 us -> 46.7 us
  Pallas kernels: 18.8 us -> 28.5 us
  starting transfers between devices: 26.5 us -> 36 us
    ppermute x28, waiting for transfers between devices: 64.9 us -> 46.7 us  [the longest x14 46.6 us: on_device(): far = lax.ppermute(current, 'blk', across)]
    pallas_call x14, Pallas kernels: 13 us -> 23.8 us  [prepare(): pl.pallas_call(functools.partial(prepare_kernel, level, inverse is not No...]
    ppermute x28, starting transfers between devices: 26.5 us -> 36 us  [the longest x14 34.7 us: on_device(): far = lax.ppermute(current, 'blk', across)]
    unnamed x23 -> x14, local copies, waits for them, and re-layouts: 12 us -> 10.9 us
  transfers between devices with their start and end apart: 28 -> 28, of which waited for: 13 -> 12; matrix products, arithmetic and copies ran while one was open for 1% -> 1% of each run, Pallas kernels for 10% -> 19%
where the time goes in v2:
time: 124 us
  waiting for transfers between devices  46.7 us (38%)
  starting transfers between devices  36 us (29%)
  Pallas kernels  28.5 us (23%)
  local copies, waits for them, and re-layouts  12.1 us (10%)
    ppermute x14, waiting for transfers between devices, on_device(): far = lax.ppermute(current, 'blk', across)  46.6 us
    ppermute x14, starting transfers between devices, on_device(): far = lax.ppermute(current, 'blk', across)  34.7 us
    pallas_call x14, Pallas kernels, prepare(): pl.pallas_call(functools.partial(prepare_kernel, level, inverse is not No...  23.8 us
    unnamed x14, local copies, waits for them, and re-layouts  10.9 us
    pallas_call x14, Pallas kernels, finish(): pl.pallas_call(functools.partial(finish_kernel, write_to), out_shape=out,...  4.68 us
  transfers between devices with their start and end apart: 28, of which 12 were waited for; matrix products, arithmetic and copies ran while one was open for 1% of the time, Pallas kernels for 19%

profile of v2, /device:TPU:6, one launch (start us, length us, event | category | flops | bytes accessed | tf_op | source)
XLA Modules:
  0.0 123.8 jit_solution(1733944333742201293)
XLA Ops:
  1.1 8.4 %collective-permute-start = (bf16[8,64,128]{2,1,0:T(8,128)(2,1)S(1)}, bf16[8,64,128]{2,1,0:T(8,128)(2,1)S(1)}, u32[]{:S(2)}, u32[]{:S(2)}) collective-permute-start(bf16[8,64,128]{2,1,0:T(8,128)(2,1)S(1)} %fusion.own_ref.base_ref), channel_id=1, source_target_pairs={{0,252},{4,8},{8,4},{12,16},{16,12},{20,24},{24,20},{28,32},{32,28... | collective-permute-start | bytes 393224 | tf_op jit(solution)/shard_map/ppermute | solution.py:169
  10.5 2.8 %copy-done = bf16[8,8,1,3,128,128]{5,4,3,2,1,0:T(8,128)(2,1)S(1)} copy-done((bf16[8,8,1,3,128,128]{5,4,3,2,1,0:T(8,128)(2,1)S(1)}, bf16[8,8,1,3,128,128]{5,4,3,2,1,0:T(8,128)(2,1)}, u32[]{:S(2)}) %copy-start) | copy-done | bytes 6291480
  18.6 5.4 %collective-permute-done.2.far_ref = bf16[8,64,128]{2,1,0:T(8,128)(2,1)S(1)} collective-permute-done((bf16[8,64,128]{2,1,0:T(8,128)(2,1)S(1)}, bf16[8,64,128]{2,1,0:T(8,128)(2,1)S(1)}, u32[]{:S(2)}, u32[]{:S(2)}) %collective-permute-start.2) | collective-permute-done | bytes 131104 | tf_op jit(solution)/shard_map/ppermute | solution.py:169
  26.8 5.4 %collective-permute-done.4.far_ref = bf16[8,64,128]{2,1,0:T(8,128)(2,1)S(1)} collective-permute-done((bf16[8,64,128]{2,1,0:T(8,128)(2,1)S(1)}, bf16[8,64,128]{2,1,0:T(8,128)(2,1)S(1)}, u32[]{:S(2)}, u32[]{:S(2)}) %collective-permute-start.4) | collective-permute-done | bytes 131104 | tf_op jit(solution)/shard_map/ppermute | solution.py:169
  34.9 5.4 %collective-permute-done.6.far_ref = bf16[8,64,128]{2,1,0:T(8,128)(2,1)S(1)} collective-permute-done((bf16[8,64,128]{2,1,0:T(8,128)(2,1)S(1)}, bf16[8,64,128]{2,1,0:T(8,128)(2,1)S(1)}, u32[]{:S(2)}, u32[]{:S(2)}) %collective-permute-start.6) | collective-permute-done | bytes 131104 | tf_op jit(solution)/shard_map/ppermute | solution.py:169
  43.1 5.4 %collective-permute-done.8.far_ref = bf16[8,64,128]{2,1,0:T(8,128)(2,1)S(1)} collective-permute-done((bf16[8,64,128]{2,1,0:T(8,128)(2,1)S(1)}, bf16[8,64,128]{2,1,0:T(8,128)(2,1)S(1)}, u32[]{:S(2)}, u32[]{:S(2)}) %collective-permute-start.8) | collective-permute-done | bytes 131104 | tf_op jit(solution)/shard_map/ppermute | solution.py:169
  51.3 5.4 %collective-permute-done.10.far_ref = bf16[8,64,128]{2,1,0:T(8,128)(2,1)S(1)} collective-permute-done((bf16[8,64,128]{2,1,0:T(8,128)(2,1)S(1)}, bf16[8,64,128]{2,1,0:T(8,128)(2,1)S(1)}, u32[]{:S(2)}, u32[]{:S(2)}) %collective-permute-start.10) | collective-permute-done | bytes 131104 | tf_op jit(solution)/shard_map/ppermute | solution.py:169
  60.5 4.4 %collective-permute-done.12.far_ref = bf16[8,64,128]{2,1,0:T(8,128)(2,1)S(1)} collective-permute-done((bf16[8,64,128]{2,1,0:T(8,128)(2,1)S(1)}, bf16[8,64,128]{2,1,0:T(8,128)(2,1)S(1)}, u32[]{:S(2)}, u32[]{:S(2)}) %collective-permute-start.12) | collective-permute-done | bytes 131104 | tf_op jit(solution)/shard_map/ppermute | solution.py:169
  67.2 2.8 %copy-done.1 = bf16[8,8,1,3,128,128]{5,4,3,2,1,0:T(8,128)(2,1)S(1)} copy-done((bf16[8,8,1,3,128,128]{5,4,3,2,1,0:T(8,128)(2,1)S(1)}, bf16[8,8,1,3,128,128]{5,4,3,2,1,0:T(8,128)(2,1)}, u32[]{:S(2)}) %copy-start.1) | copy-done | bytes 6291480
  73.7 2.8 %collective-permute-start.16 = (bf16[8,64,128]{2,1,0:T(8,128)(2,1)S(1)}, bf16[8,64,128]{2,1,0:T(8,128)(2,1)S(1)}, u32[]{:S(2)}, u32[]{:S(2)}) collective-permute-start(bf16[8,64,128]{2,1,0:T(8,128)(2,1)S(1)} %finish.21.own_ref), channel_id=1, source_target_pairs={{0,252},{4,8},{8,4},{12,16},{16,12},{20,24},{24,20},{28,32},{32,28... | collective-permute-start | bytes 393224 | tf_op jit(solution)/shard_map/ppermute | solution.py:169
  76.6 2.8 %copy-done.2 = bf16[8,8,1,3,128,128]{5,4,3,2,1,0:T(8,128)(2,1)S(1)} copy-done((bf16[8,8,1,3,128,128]{5,4,3,2,1,0:T(8,128)(2,1)S(1)}, bf16[8,8,1,3,128,128]{5,4,3,2,1,0:T(8,128)(2,1)}, u32[]{:S(2)}) %copy-start.2) | copy-done | bytes 6291480
  82.1 2.7 %collective-permute-start.18 = (bf16[8,64,128]{2,1,0:T(8,128)(2,1)S(1)}, bf16[8,64,128]{2,1,0:T(8,128)(2,1)S(1)}, u32[]{:S(2)}, u32[]{:S(2)}) collective-permute-start(bf16[8,64,128]{2,1,0:T(8,128)(2,1)S(1)} %finish.22.own_ref), channel_id=1, source_target_pairs={{0,252},{4,8},{8,4},{12,16},{16,12},{20,24},{24,20},{28,32},{32,28... | collective-permute-start | bytes 393224 | tf_op jit(solution)/shard_map/ppermute | solution.py:169
  84.8 2.3 %prepare.23 = (f32[8,64,128]{2,1,0:T(8,128)S(1)}, bf16[8,128,256]{2,1,0:T(8,128)(2,1)S(1)}, bf16[8,8,1,64,128]{4,3,2,1,0:T(8,128)(2,1)}) custom-call(s32[4]{0:T(128)S(1)} %pad_add_fusion.place_ref, s32[1,192]{1,0:T(1,128)S(1)} %reshape.8.cols_ref, bf16[8,64,128]{2,1,0:T(8,128)(2,1)S(1)} %finish.17.own_ref.base_ref, ...), custom_call_target="tpu_custom_call", output_to_operand_aliasing={{2}: (7, {})} | custom-call | flops 20000000 | bytes 4194304 | tf_op jit(solution)/shard_map/prepare/pallas_call | solution.py:94
  87.1 2.8 %collective-permute-done.18.far_ref = bf16[8,64,128]{2,1,0:T(8,128)(2,1)S(1)} collective-permute-done((bf16[8,64,128]{2,1,0:T(8,128)(2,1)S(1)}, bf16[8,64,128]{2,1,0:T(8,128)(2,1)S(1)}, u32[]{:S(2)}, u32[]{:S(2)}) %collective-permute-start.18) | collective-permute-done | bytes 131104 | tf_op jit(solution)/shard_map/ppermute | solution.py:169
  90.3 2.7 %collective-permute-start.20 = (bf16[8,64,128]{2,1,0:T(8,128)(2,1)S(1)}, bf16[8,64,128]{2,1,0:T(8,128)(2,1)S(1)}, u32[]{:S(2)}, u32[]{:S(2)}) collective-permute-start(bf16[8,64,128]{2,1,0:T(8,128)(2,1)S(1)} %finish.23.own_ref), channel_id=1, source_target_pairs={{0,252},{4,8},{8,4},{12,16},{16,12},{20,24},{24,20},{28,32},{32,28... | collective-permute-start | bytes 393224 | tf_op jit(solution)/shard_map/ppermute | solution.py:169
  95.3 2.8 %collective-permute-done.20.far_ref = bf16[8,64,128]{2,1,0:T(8,128)(2,1)S(1)} collective-permute-done((bf16[8,64,128]{2,1,0:T(8,128)(2,1)S(1)}, bf16[8,64,128]{2,1,0:T(8,128)(2,1)S(1)}, u32[]{:S(2)}, u32[]{:S(2)}) %collective-permute-start.20) | collective-permute-done | bytes 131104 | tf_op jit(solution)/shard_map/ppermute | solution.py:169
  98.5 2.7 %collective-permute-start.22 = (bf16[8,64,128]{2,1,0:T(8,128)(2,1)S(1)}, bf16[8,64,128]{2,1,0:T(8,128)(2,1)S(1)}, u32[]{:S(2)}, u32[]{:S(2)}) collective-permute-start(bf16[8,64,128]{2,1,0:T(8,128)(2,1)S(1)} %finish.24.own_ref), channel_id=1, source_target_pairs={{0,252},{4,8},{8,4},{12,16},{16,12},{20,24},{24,20},{28,32},{32,28... | collective-permute-start | bytes 393224 | tf_op jit(solution)/shard_map/ppermute | solution.py:169
  101.2 2.3 %prepare.25 = (f32[8,64,128]{2,1,0:T(8,128)S(1)}, bf16[8,128,256]{2,1,0:T(8,128)(2,1)S(1)}, bf16[8,8,1,64,128]{4,3,2,1,0:T(8,128)(2,1)}) custom-call(s32[4]{0:T(128)S(1)} %pad_add_fusion.place_ref, s32[1,192]{1,0:T(1,128)S(1)} %reshape.8.cols_ref, bf16[8,64,128]{2,1,0:T(8,128)(2,1)S(1)} %finish.15.own_ref.base_ref, ...), custom_call_target="tpu_custom_call", output_to_operand_aliasing={{2}: (7, {})} | custom-call | flops 20000000 | bytes 4194304 | tf_op jit(solution)/shard_map/prepare/pallas_call | solution.py:94
  103.5 2.8 %collective-permute-done.22.far_ref = bf16[8,64,128]{2,1,0:T(8,128)(2,1)S(1)} collective-permute-done((bf16[8,64,128]{2,1,0:T(8,128)(2,1)S(1)}, bf16[8,64,128]{2,1,0:T(8,128)(2,1)S(1)}, u32[]{:S(2)}, u32[]{:S(2)}) %collective-permute-start.22) | collective-permute-done | bytes 131104 | tf_op jit(solution)/shard_map/ppermute | solution.py:169
  106.7 2.7 %collective-permute-start.24 = (bf16[8,64,128]{2,1,0:T(8,128)(2,1)S(1)}, bf16[8,64,128]{2,1,0:T(8,128)(2,1)S(1)}, u32[]{:S(2)}, u32[]{:S(2)}) collective-permute-start(bf16[8,64,128]{2,1,0:T(8,128)(2,1)S(1)} %finish.25.own_ref), channel_id=1, source_target_pairs={{0,252},{4,8},{8,4},{12,16},{16,12},{20,24},{24,20},{28,32},{32,28... | collective-permute-start | bytes 393224 | tf_op jit(solution)/shard_map/ppermute | solution.py:169
  109.4 2.3 %prepare.26 = (f32[8,64,128]{2,1,0:T(8,128)S(1)}, bf16[8,128,256]{2,1,0:T(8,128)(2,1)S(1)}, bf16[8,8,1,64,128]{4,3,2,1,0:T(8,128)(2,1)}) custom-call(s32[4]{0:T(128)S(1)} %pad_add_fusion.place_ref, s32[1,192]{1,0:T(1,128)S(1)} %reshape.8.cols_ref, bf16[8,64,128]{2,1,0:T(8,128)(2,1)S(1)} %finish.14.own_ref.base_ref, ...), custom_call_target="tpu_custom_call", output_to_operand_aliasing={{2}: (7, {})} | custom-call | flops 20000000 | bytes 4194304 | tf_op jit(solution)/shard_map/prepare/pallas_call | solution.py:94
  111.7 2.8 %collective-permute-done.24.far_ref = bf16[8,64,128]{2,1,0:T(8,128)(2,1)S(1)} collective-permute-done((bf16[8,64,128]{2,1,0:T(8,128)(2,1)S(1)}, bf16[8,64,128]{2,1,0:T(8,128)(2,1)S(1)}, u32[]{:S(2)}, u32[]{:S(2)}) %collective-permute-start.24) | collective-permute-done | bytes 131104 | tf_op jit(solution)/shard_map/ppermute | solution.py:169
  114.9 2.7 %collective-permute-start.26 = (bf16[8,64,128]{2,1,0:T(8,128)(2,1)S(1)}, bf16[8,64,128]{2,1,0:T(8,128)(2,1)S(1)}, u32[]{:S(2)}, u32[]{:S(2)}) collective-permute-start(bf16[8,64,128]{2,1,0:T(8,128)(2,1)S(1)} %finish.26.own_ref), channel_id=1, source_target_pairs={{0,252},{4,8},{8,4},{12,16},{16,12},{20,24},{24,20},{28,32},{32,28... | collective-permute-start | bytes 393224 | tf_op jit(solution)/shard_map/ppermute | solution.py:169
  119.9 2.8 %collective-permute-done.26.far_ref = bf16[8,64,128]{2,1,0:T(8,128)(2,1)S(1)} collective-permute-done((bf16[8,64,128]{2,1,0:T(8,128)(2,1)S(1)}, bf16[8,64,128]{2,1,0:T(8,128)(2,1)S(1)}, u32[]{:S(2)}, u32[]{:S(2)}) %collective-permute-start.26) | collective-permute-done | bytes 131104 | tf_op jit(solution)/shard_map/ppermute | solution.py:169
  (78 shorter events, 37.8 us)
Async XLA Ops:
  1.0 9.6 %collective-permute-start.1 = (bf16[8,64,128]{2,1,0:T(8,128)(2,1)S(1)}, bf16[8,64,128]{2,1,0:T(8,128)(2,1)S(1)}, u32[]{:S(2)}, u32[]{:S(2)}) collective-permute-start(bf16[8,64,128]{2,1,0:T(8,128)(2,1)S(1)} %fusion.own_ref.base_ref), channel_id=1, source_target_pairs={{0,4},{4,0},{8,12},{12,8},{16,20},{20,16},{24,28},{28,24},{32,36},... | collective-permute-start | bytes 393224 | tf_op jit(solution)/shard_map/ppermute | solution.py:170
  1.1 14.8 %collective-permute-start = (bf16[8,64,128]{2,1,0:T(8,128)(2,1)S(1)}, bf16[8,64,128]{2,1,0:T(8,128)(2,1)S(1)}, u32[]{:S(2)}, u32[]{:S(2)}) collective-permute-start(bf16[8,64,128]{2,1,0:T(8,128)(2,1)S(1)} %fusion.own_ref.base_ref), channel_id=1, source_target_pairs={{0,252},{4,8},{8,4},{12,16},{16,12},{20,24},{24,20},{28,32},{32,28... | collective-permute-start | bytes 393224 | tf_op jit(solution)/shard_map/ppermute | solution.py:169
  16.1 1.5 %collective-permute-start.3 = (bf16[8,64,128]{2,1,0:T(8,128)(2,1)S(1)}, bf16[8,64,128]{2,1,0:T(8,128)(2,1)S(1)}, u32[]{:S(2)}, u32[]{:S(2)}) collective-permute-start(bf16[8,64,128]{2,1,0:T(8,128)(2,1)S(1)} %finish.14.own_ref.base_ref), channel_id=1, source_target_pairs={{0,4},{4,0},{8,12},{12,8},{16,20},{20,16},{24,28},{28,24},{32,36},... | collective-permute-start | bytes 393224 | tf_op jit(solution)/shard_map/ppermute | solution.py:170
  16.2 7.8 %collective-permute-start.2 = (bf16[8,64,128]{2,1,0:T(8,128)(2,1)S(1)}, bf16[8,64,128]{2,1,0:T(8,128)(2,1)S(1)}, u32[]{:S(2)}, u32[]{:S(2)}) collective-permute-start(bf16[8,64,128]{2,1,0:T(8,128)(2,1)S(1)} %finish.14.own_ref.base_ref), channel_id=1, source_target_pairs={{0,252},{4,8},{8,4},{12,16},{16,12},{20,24},{24,20},{28,32},{32,28... | collective-permute-start | bytes 393224 | tf_op jit(solution)/shard_map/ppermute | solution.py:169
  24.3 1.5 %collective-permute-start.5 = (bf16[8,64,128]{2,1,0:T(8,128)(2,1)S(1)}, bf16[8,64,128]{2,1,0:T(8,128)(2,1)S(1)}, u32[]{:S(2)}, u32[]{:S(2)}) collective-permute-start(bf16[8,64,128]{2,1,0:T(8,128)(2,1)S(1)} %finish.15.own_ref.base_ref), channel_id=1, source_target_pairs={{0,4},{4,0},{8,12},{12,8},{16,20},{20,16},{24,28},{28,24},{32,36},... | collective-permute-start | bytes 393224 | tf_op jit(solution)/shard_map/ppermute | solution.py:170
  24.4 7.8 %collective-permute-start.4 = (bf16[8,64,128]{2,1,0:T(8,128)(2,1)S(1)}, bf16[8,64,128]{2,1,0:T(8,128)(2,1)S(1)}, u32[]{:S(2)}, u32[]{:S(2)}) collective-permute-start(bf16[8,64,128]{2,1,0:T(8,128)(2,1)S(1)} %finish.15.own_ref.base_ref), channel_id=1, source_target_pairs={{0,252},{4,8},{8,4},{12,16},{16,12},{20,24},{24,20},{28,32},{32,28... | collective-permute-start | bytes 393224 | tf_op jit(solution)/shard_map/ppermute | solution.py:169
  32.6 7.8 %collective-permute-start.6 = (bf16[8,64,128]{2,1,0:T(8,128)(2,1)S(1)}, bf16[8,64,128]{2,1,0:T(8,128)(2,1)S(1)}, u32[]{:S(2)}, u32[]{:S(2)}) collective-permute-start(bf16[8,64,128]{2,1,0:T(8,128)(2,1)S(1)} %finish.16.own_ref.base_ref), channel_id=1, source_target_pairs={{0,252},{4,8},{8,4},{12,16},{16,12},{20,24},{24,20},{28,32},{32,28... | collective-permute-start | bytes 393224 | tf_op jit(solution)/shard_map/ppermute | solution.py:169
  40.8 7.8 %collective-permute-start.8 = (bf16[8,64,128]{2,1,0:T(8,128)(2,1)S(1)}, bf16[8,64,128]{2,1,0:T(8,128)(2,1)S(1)}, u32[]{:S(2)}, u32[]{:S(2)}) collective-permute-start(bf16[8,64,128]{2,1,0:T(8,128)(2,1)S(1)} %finish.17.own_ref.base_ref), channel_id=1, source_target_pairs={{0,252},{4,8},{8,4},{12,16},{16,12},{20,24},{24,20},{28,32},{32,28... | collective-permute-start | bytes 393224 | tf_op jit(solution)/shard_map/ppermute | solution.py:169
  48.9 7.8 %collective-permute-start.10 = (bf16[8,64,128]{2,1,0:T(8,128)(2,1)S(1)}, bf16[8,64,128]{2,1,0:T(8,128)(2,1)S(1)}, u32[]{:S(2)}, u32[]{:S(2)}) collective-permute-start(bf16[8,64,128]{2,1,0:T(8,128)(2,1)S(1)} %finish.18.own_ref.base_ref), channel_id=1, source_target_pairs={{0,252},{4,8},{8,4},{12,16},{16,12},{20,24},{24,20},{28,32},{32,28... | collective-permute-start | bytes 393224 | tf_op jit(solution)/shard_map/ppermute | solution.py:169
  57.1 7.8 %collective-permute-start.12 = (bf16[8,64,128]{2,1,0:T(8,128)(2,1)S(1)}, bf16[8,64,128]{2,1,0:T(8,128)(2,1)S(1)}, u32[]{:S(2)}, u32[]{:S(2)}) collective-permute-start(bf16[8,64,128]{2,1,0:T(8,128)(2,1)S(1)} %finish.19.own_ref.base_ref), channel_id=1, source_target_pairs={{0,252},{4,8},{8,4},{12,16},{16,12},{20,24},{24,20},{28,32},{32,28... | collective-permute-start | bytes 393224 | tf_op jit(solution)/shard_map/ppermute | solution.py:169
  65.2 2.0 %collective-permute-start.15 = (bf16[8,64,128]{2,1,0:T(8,128)(2,1)S(1)}, bf16[8,64,128]{2,1,0:T(8,128)(2,1)S(1)}, u32[]{:S(2)}, u32[]{:S(2)}) collective-permute-start(bf16[8,64,128]{2,1,0:T(8,128)(2,1)S(1)} %finish.20.own_ref), channel_id=1, source_target_pairs={{0,4},{4,0},{8,12},{12,8},{16,20},{20,16},{24,28},{28,24},{32,36},... | collective-permute-start | bytes 393224 | tf_op jit(solution)/shard_map/ppermute | solution.py:170
  65.3 8.0 %collective-permute-start.14 = (bf16[8,64,128]{2,1,0:T(8,128)(2,1)S(1)}, bf16[8,64,128]{2,1,0:T(8,128)(2,1)S(1)}, u32[]{:S(2)}, u32[]{:S(2)}) collective-permute-start(bf16[8,64,128]{2,1,0:T(8,128)(2,1)S(1)} %finish.20.own_ref), channel_id=1, source_target_pairs={{0,252},{4,8},{8,4},{12,16},{16,12},{20,24},{24,20},{28,32},{32,28... | collective-permute-start | bytes 393224 | tf_op jit(solution)/shard_map/ppermute | solution.py:169
  73.6 2.9 %collective-permute-start.17 = (bf16[8,64,128]{2,1,0:T(8,128)(2,1)S(1)}, bf16[8,64,128]{2,1,0:T(8,128)(2,1)S(1)}, u32[]{:S(2)}, u32[]{:S(2)}) collective-permute-start(bf16[8,64,128]{2,1,0:T(8,128)(2,1)S(1)} %finish.21.own_ref), channel_id=1, source_target_pairs={{0,4},{4,0},{8,12},{12,8},{16,20},{20,16},{24,28},{28,24},{32,36},... | collective-permute-start | bytes 393224 | tf_op jit(solution)/shard_map/ppermute | solution.py:170
  73.7 8.0 %collective-permute-start.16 = (bf16[8,64,128]{2,1,0:T(8,128)(2,1)S(1)}, bf16[8,64,128]{2,1,0:T(8,128)(2,1)S(1)}, u32[]{:S(2)}, u32[]{:S(2)}) collective-permute-start(bf16[8,64,128]{2,1,0:T(8,128)(2,1)S(1)} %finish.21.own_ref), channel_id=1, source_target_pairs={{0,252},{4,8},{8,4},{12,16},{16,12},{20,24},{24,20},{28,32},{32,28... | collective-permute-start | bytes 393224 | tf_op jit(solution)/shard_map/ppermute | solution.py:169
  82.0 2.8 %collective-permute-start.19 = (bf16[8,64,128]{2,1,0:T(8,128)(2,1)S(1)}, bf16[8,64,128]{2,1,0:T(8,128)(2,1)S(1)}, u32[]{:S(2)}, u32[]{:S(2)}) collective-permute-start(bf16[8,64,128]{2,1,0:T(8,128)(2,1)S(1)} %finish.22.own_ref), channel_id=1, source_target_pairs={{0,4},{4,0},{8,12},{12,8},{16,20},{20,16},{24,28},{28,24},{32,36},... | collective-permute-start | bytes 393224 | tf_op jit(solution)/shard_map/ppermute | solution.py:170
  82.1 7.8 %collective-permute-start.18 = (bf16[8,64,128]{2,1,0:T(8,128)(2,1)S(1)}, bf16[8,64,128]{2,1,0:T(8,128)(2,1)S(1)}, u32[]{:S(2)}, u32[]{:S(2)}) collective-permute-start(bf16[8,64,128]{2,1,0:T(8,128)(2,1)S(1)} %finish.22.own_ref), channel_id=1, source_target_pairs={{0,252},{4,8},{8,4},{12,16},{16,12},{20,24},{24,20},{28,32},{32,28... | collective-permute-start | bytes 393224 | tf_op jit(solution)/shard_map/ppermute | solution.py:169
  90.2 2.8 %collective-permute-start.21 = (bf16[8,64,128]{2,1,0:T(8,128)(2,1)S(1)}, bf16[8,64,128]{2,1,0:T(8,128)(2,1)S(1)}, u32[]{:S(2)}, u32[]{:S(2)}) collective-permute-start(bf16[8,64,128]{2,1,0:T(8,128)(2,1)S(1)} %finish.23.own_ref), channel_id=1, source_target_pairs={{0,4},{4,0},{8,12},{12,8},{16,20},{20,16},{24,28},{28,24},{32,36},... | collective-permute-start | bytes 393224 | tf_op jit(solution)/shard_map/ppermute | solution.py:170
  90.3 7.8 %collective-permute-start.20 = (bf16[8,64,128]{2,1,0:T(8,128)(2,1)S(1)}, bf16[8,64,128]{2,1,0:T(8,128)(2,1)S(1)}, u32[]{:S(2)}, u32[]{:S(2)}) collective-permute-start(bf16[8,64,128]{2,1,0:T(8,128)(2,1)S(1)} %finish.23.own_ref), channel_id=1, source_target_pairs={{0,252},{4,8},{8,4},{12,16},{16,12},{20,24},{24,20},{28,32},{32,28... | collective-permute-start | bytes 393224 | tf_op jit(solution)/shard_map/ppermute | solution.py:169
  98.4 2.8 %collective-permute-start.23 = (bf16[8,64,128]{2,1,0:T(8,128)(2,1)S(1)}, bf16[8,64,128]{2,1,0:T(8,128)(2,1)S(1)}, u32[]{:S(2)}, u32[]{:S(2)}) collective-permute-start(bf16[8,64,128]{2,1,0:T(8,128)(2,1)S(1)} %finish.24.own_ref), channel_id=1, source_target_pairs={{0,4},{4,0},{8,12},{12,8},{16,20},{20,16},{24,28},{28,24},{32,36},... | collective-permute-start | bytes 393224 | tf_op jit(solution)/shard_map/ppermute | solution.py:170
  98.5 7.8 %collective-permute-start.22 = (bf16[8,64,128]{2,1,0:T(8,128)(2,1)S(1)}, bf16[8,64,128]{2,1,0:T(8,128)(2,1)S(1)}, u32[]{:S(2)}, u32[]{:S(2)}) collective-permute-start(bf16[8,64,128]{2,1,0:T(8,128)(2,1)S(1)} %finish.24.own_ref), channel_id=1, source_target_pairs={{0,252},{4,8},{8,4},{12,16},{16,12},{20,24},{24,20},{28,32},{32,28... | collective-permute-start | bytes 393224 | tf_op jit(solution)/shard_map/ppermute | solution.py:169
  106.6 2.8 %collective-permute-start.25 = (bf16[8,64,128]{2,1,0:T(8,128)(2,1)S(1)}, bf16[8,64,128]{2,1,0:T(8,128)(2,1)S(1)}, u32[]{:S(2)}, u32[]{:S(2)}) collective-permute-start(bf16[8,64,128]{2,1,0:T(8,128)(2,1)S(1)} %finish.25.own_ref), channel_id=1, source_target_pairs={{0,4},{4,0},{8,12},{12,8},{16,20},{20,16},{24,28},{28,24},{32,36},... | collective-permute-start | bytes 393224 | tf_op jit(solution)/shard_map/ppermute | solution.py:170
  106.7 7.8 %collective-permute-start.24 = (bf16[8,64,128]{2,1,0:T(8,128)(2,1)S(1)}, bf16[8,64,128]{2,1,0:T(8,128)(2,1)S(1)}, u32[]{:S(2)}, u32[]{:S(2)}) collective-permute-start(bf16[8,64,128]{2,1,0:T(8,128)(2,1)S(1)} %finish.25.own_ref), channel_id=1, source_target_pairs={{0,252},{4,8},{8,4},{12,16},{16,12},{20,24},{24,20},{28,32},{32,28... | collective-permute-start | bytes 393224 | tf_op jit(solution)/shard_map/ppermute | solution.py:169
  114.8 2.8 %collective-permute-start.27 = (bf16[8,64,128]{2,1,0:T(8,128)(2,1)S(1)}, bf16[8,64,128]{2,1,0:T(8,128)(2,1)S(1)}, u32[]{:S(2)}, u32[]{:S(2)}) collective-permute-start(bf16[8,64,128]{2,1,0:T(8,128)(2,1)S(1)} %finish.26.own_ref), channel_id=1, source_target_pairs={{0,4},{4,0},{8,12},{12,8},{16,20},{20,16},{24,28},{28,24},{32,36},... | collective-permute-start | bytes 393224 | tf_op jit(solution)/shard_map/ppermute | solution.py:170
  114.9 7.8 %collective-permute-start.26 = (bf16[8,64,128]{2,1,0:T(8,128)(2,1)S(1)}, bf16[8,64,128]{2,1,0:T(8,128)(2,1)S(1)}, u32[]{:S(2)}, u32[]{:S(2)}) collective-permute-start(bf16[8,64,128]{2,1,0:T(8,128)(2,1)S(1)} %finish.26.own_ref), channel_id=1, source_target_pairs={{0,252},{4,8},{8,4},{12,16},{16,12},{20,24},{24,20},{28,32},{32,28... | collective-permute-start | bytes 393224 | tf_op jit(solution)/shard_map/ppermute | solution.py:169
  (10 other events, 34.1 us)

commit v3 on v2

--- a/solution.py
+++ b/solution.py
@@ -19,7 +19,7 @@
     return jnp.concatenate([coarse, fine], axis=1)
 
 
-def prepare_kernel(level, with_inverse, write_to, continued, place_ref, cols_ref, base_ref, tiles_ref, own_ref, near_ref, *refs):
+def prepare_kernel(level, with_inverse, write_to, continued, place_ref, cols_ref, base_ref, tiles_ref, own_ref, *refs):
     refs = list(refs)
     inverse_ref = refs.pop(0) if with_inverse else None
     if continued:
@@ -43,38 +43,33 @@
             return jnp.where(hits[0] | hits[1] | hits[2], tile, jnp.zeros_like(tile))
 
         base = base_ref[m] if len(base_ref.shape) == 3 else base_ref[0, m, 0]
-        both = jnp.concatenate([own_ref[m], near_ref[m]], axis=1)
-        tiles = jnp.concatenate([tile_of(here), tile_of(partner)], axis=1)
-        total = base.astype(jnp.float32) - times_transposed(both, tiles)
+        beside = jnp.concatenate([tile_of(partner), tile_of(other)], axis=1)
+        total = base.astype(jnp.float32) - times_transposed(own_ref[m], tile_of(here))
         if with_inverse:
             inverse = inverse_ref[0, m, 0]
             total = times_transposed(two_parts(total), jnp.concatenate([inverse, inverse], axis=1))
-            beside_ref[m] = two_parts(
-                jnp.dot(inverse, tile_of(other), preferred_element_type=jnp.float32)
-            )
-        else:
-            beside_ref[m] = tile_of(other)
+            beside = two_parts(jnp.dot(inverse, beside, preferred_element_type=jnp.float32))
+        beside_ref[m] = beside
         total_ref[m] = total
     if write_to is not None:
         copy.wait()
 
 
-def prepare(level, place, columns, base, tiles, own, near, inverse, write_to, result, result_shape):
+def prepare(level, place, columns, base, tiles, own, inverse, write_to, result, result_shape):
     rows, sides, width = own.shape
     level_block = lambda a: pl.BlockSpec(
         (1,) + a.shape[1:], lambda i: (level,) + (0,) * (len(a.shape) - 1)
     )
     whole = lambda a: pl.BlockSpec(a.shape, lambda i: (0,) * len(a.shape))
-    args = [place, columns, base, tiles, own, near]
+    args = [place, columns, base, tiles, own]
     specs = [
         pl.BlockSpec(memory_space=pltpu.SMEM),
         pl.BlockSpec(memory_space=pltpu.SMEM),
         level_block(base) if len(base.shape) == 5 else whole(base),
         level_block(tiles),
         whole(own),
-        whole(near),
     ]
-    deep = width if inverse is None else 2 * width
+    deep = 2 * width if inverse is None else 4 * width
     shapes = [
         jax.ShapeDtypeStruct((rows, sides, width), jnp.float32),
         jax.ShapeDtypeStruct((rows, width, deep), jnp.bfloat16),
@@ -107,25 +102,34 @@
     )(*args)
 
 
-def finish_kernel(write_to, far_ref, total_ref, beside_ref, *refs):
+def finish_kernel(write_to, far_ref, near_ref, total_ref, beside_ref, *refs):
     if write_to is None:
         (out_ref,) = refs
     else:
-        _, result_ref, out_ref, sem = refs
-    for m in range(far_ref.shape[0]):
-        far = far_ref[m]
-        if beside_ref.shape[2] == 2 * far.shape[1]:
-            far = jnp.concatenate([far, far], axis=1)
-        out_ref[m] = (total_ref[m] - times_transposed(far, beside_ref[m])).astype(jnp.bfloat16)
-    if write_to is not None:
-        copy = pltpu.make_async_copy(out_ref, result_ref.at[write_to, :, 0], sem)
-        copy.start()
+        _, result_ref, out_ref, sems = refs
+    rows = far_ref.shape[0]
+    copies = []
+    for m in range(rows):
+        both = [near_ref[m], far_ref[m]]
+        if beside_ref.shape[2] == 4 * far_ref.shape[2]:
+            both = both + both
+        term = times_transposed(jnp.concatenate(both, axis=1), beside_ref[m])
+        out_ref[m] = (total_ref[m] - term).astype(jnp.bfloat16)
+        if write_to is not None and m % 4 == 3:
+            part = pl.ds(m - 3, 4)
+            copies.append(
+                pltpu.make_async_copy(
+                    out_ref.at[part], result_ref.at[write_to, part, 0], sems.at[m // 4]
+                )
+            )
+            copies[-1].start()
+    for copy in copies:
         copy.wait()
 
 
-def finish(far, total, beside, write_to=None, result=None):
+def finish(near, far, total, beside, write_to=None, result=None):
     whole = pl.BlockSpec(memory_space=pltpu.VMEM)
-    args, specs = [far, total, beside], [whole] * 3
+    args, specs = [far, near, total, beside], [whole] * 4
     more = {}
     out, out_spec = jax.ShapeDtypeStruct(far.shape, jnp.bfloat16), whole
     if write_to is not None:
@@ -133,8 +137,8 @@
         args.append(result)
         specs.append(out_spec)
         more = dict(
-            input_output_aliases={3: 0},
-            scratch_shapes=[pltpu.VMEM(far.shape, jnp.bfloat16), pltpu.SemaphoreType.DMA],
+            input_output_aliases={4: 0},
+            scratch_shapes=[pltpu.VMEM(far.shape, jnp.bfloat16), pltpu.SemaphoreType.DMA((2,))],
         )
     return pl.pallas_call(
         functools.partial(finish_kernel, write_to),
@@ -175,7 +179,6 @@
             rhs if forward else solved[level],
             lower_tiles if forward else upper_tiles,
             current,
-            near,
             diag_inverse if tail else None,
             None if forward else level + 1,
             result,
@@ -184,9 +187,9 @@
         if not forward:
             result = parts[2]
         if level or forward:
-            current = finish(far, parts[0], parts[1])
+            current = finish(near, far, parts[0], parts[1])
         else:
-            result = finish(far, parts[0], parts[1], level, result)
+            result = finish(near, far, parts[0], parts[1], level, result)
         if forward:
             solved.append(current)
     return result

time: 124 us -> 124 us (level)
  starting transfers between devices: 36 us -> 33.6 us
  waiting for transfers between devices: 46.7 us -> 49 us
    ppermute x14, waiting for transfers between devices: 46.6 us -> 49 us  [on_device(): far = lax.ppermute(current, 'blk', across)]
    pallas_call x14, Pallas kernels: 23.8 us -> 21.8 us  [prepare(): pl.pallas_call(functools.partial(prepare_kernel, level, inverse is not No...]
    pallas_call x14, Pallas kernels: 4.68 us -> 6.33 us  [finish(): pl.pallas_call(functools.partial(finish_kernel, write_to), out_shape=out,...]
    ppermute x14, starting transfers between devices: 1.3 us -> 0.04 us  [on_device(): near = lax.ppermute(current, 'blk', pairs)]
  transfers between devices with their start and end apart: 28 -> 28, of which waited for: 12 -> 13; matrix products, arithmetic and copies ran while one was open for 1% -> 1% of each run, Pallas kernels for 19% -> 18%
where the time goes in v3:
time: 124 us; the launch traced here: 123 us
  waiting for transfers between devices  49 us (40%)
  starting transfers between devices  33.6 us (27%)
  Pallas kernels  28.1 us (23%)
  local copies, waits for them, and re-layouts  12.1 us (10%)
    ppermute x14, waiting for transfers between devices, on_device(): far = lax.ppermute(current, 'blk', across)  49 us
    ppermute x14, starting transfers between devices, on_device(): far = lax.ppermute(current, 'blk', across)  33.6 us
    pallas_call x14, Pallas kernels, prepare(): pl.pallas_call(functools.partial(prepare_kernel, level, inverse is not No...  21.8 us
    unnamed x14, local copies, waits for them, and re-layouts  10.9 us
    pallas_call x14, Pallas kernels, finish(): pl.pallas_call(functools.partial(finish_kernel, write_to), out_shape=out,...  6.33 us
  transfers between devices with their start and end apart: 28, of which 13 were waited for; matrix products, arithmetic and copies ran while one was open for 1% of the time, Pallas kernels for 18%

profile of v3, /device:TPU:6, one launch (start us, length us, event | category | flops | bytes accessed | tf_op | source)
XLA Modules:
  0.0 123.3 jit_solution(5281937092094962925)
XLA Ops:
  1.0 7.8 %collective-permute-start = (bf16[8,64,128]{2,1,0:T(8,128)(2,1)S(1)}, bf16[8,64,128]{2,1,0:T(8,128)(2,1)S(1)}, u32[]{:S(2)}, u32[]{:S(2)}) collective-permute-start(bf16[8,64,128]{2,1,0:T(8,128)(2,1)S(1)} %fusion.own_ref.base_ref), channel_id=1, source_target_pairs={{0,252},{4,8},{8,4},{12,16},{16,12},{20,24},{24,20},{28,32},{32,28... | collective-permute-start | bytes 393224 | tf_op jit(solution)/shard_map/ppermute | solution.py:173
  9.9 2.8 %copy-done = bf16[8,8,1,3,128,128]{5,4,3,2,1,0:T(8,128)(2,1)S(1)} copy-done((bf16[8,8,1,3,128,128]{5,4,3,2,1,0:T(8,128)(2,1)S(1)}, bf16[8,8,1,3,128,128]{5,4,3,2,1,0:T(8,128)(2,1)}, u32[]{:S(2)}) %copy-start) | copy-done | bytes 6291480
  17.8 5.5 %collective-permute-done.2.far_ref = bf16[8,64,128]{2,1,0:T(8,128)(2,1)S(1)} collective-permute-done((bf16[8,64,128]{2,1,0:T(8,128)(2,1)S(1)}, bf16[8,64,128]{2,1,0:T(8,128)(2,1)S(1)}, u32[]{:S(2)}, u32[]{:S(2)}) %collective-permute-start.2) | collective-permute-done | bytes 131104 | tf_op jit(solution)/shard_map/ppermute | solution.py:173
  25.9 5.5 %collective-permute-done.4.far_ref = bf16[8,64,128]{2,1,0:T(8,128)(2,1)S(1)} collective-permute-done((bf16[8,64,128]{2,1,0:T(8,128)(2,1)S(1)}, bf16[8,64,128]{2,1,0:T(8,128)(2,1)S(1)}, u32[]{:S(2)}, u32[]{:S(2)}) %collective-permute-start.4) | collective-permute-done | bytes 131104 | tf_op jit(solution)/shard_map/ppermute | solution.py:173
  34.0 5.5 %collective-permute-done.6.far_ref = bf16[8,64,128]{2,1,0:T(8,128)(2,1)S(1)} collective-permute-done((bf16[8,64,128]{2,1,0:T(8,128)(2,1)S(1)}, bf16[8,64,128]{2,1,0:T(8,128)(2,1)S(1)}, u32[]{:S(2)}, u32[]{:S(2)}) %collective-permute-start.6) | collective-permute-done | bytes 131104 | tf_op jit(solution)/shard_map/ppermute | solution.py:173
  42.1 5.5 %collective-permute-done.8.far_ref = bf16[8,64,128]{2,1,0:T(8,128)(2,1)S(1)} collective-permute-done((bf16[8,64,128]{2,1,0:T(8,128)(2,1)S(1)}, bf16[8,64,128]{2,1,0:T(8,128)(2,1)S(1)}, u32[]{:S(2)}, u32[]{:S(2)}) %collective-permute-start.8) | collective-permute-done | bytes 131104 | tf_op jit(solution)/shard_map/ppermute | solution.py:173
  50.2 5.4 %collective-permute-done.10.far_ref = bf16[8,64,128]{2,1,0:T(8,128)(2,1)S(1)} collective-permute-done((bf16[8,64,128]{2,1,0:T(8,128)(2,1)S(1)}, bf16[8,64,128]{2,1,0:T(8,128)(2,1)S(1)}, u32[]{:S(2)}, u32[]{:S(2)}) %collective-permute-start.10) | collective-permute-done | bytes 131104 | tf_op jit(solution)/shard_map/ppermute | solution.py:173
  59.4 4.4 %collective-permute-done.12.far_ref = bf16[8,64,128]{2,1,0:T(8,128)(2,1)S(1)} collective-permute-done((bf16[8,64,128]{2,1,0:T(8,128)(2,1)S(1)}, bf16[8,64,128]{2,1,0:T(8,128)(2,1)S(1)}, u32[]{:S(2)}, u32[]{:S(2)}) %collective-permute-start.12) | collective-permute-done | bytes 131104 | tf_op jit(solution)/shard_map/ppermute | solution.py:173
  66.2 2.8 %copy-done.1 = bf16[8,8,1,3,128,128]{5,4,3,2,1,0:T(8,128)(2,1)S(1)} copy-done((bf16[8,8,1,3,128,128]{5,4,3,2,1,0:T(8,128)(2,1)S(1)}, bf16[8,8,1,3,128,128]{5,4,3,2,1,0:T(8,128)(2,1)}, u32[]{:S(2)}) %copy-start.1) | copy-done | bytes 6291480
  69.0 2.1 %prepare.21 = (f32[8,64,128]{2,1,0:T(8,128)S(1)}, bf16[8,128,512]{2,1,0:T(8,128)(2,1)S(1)}, bf16[8,8,1,64,128]{4,3,2,1,0:T(8,128)(2,1)}) custom-call(s32[4]{0:T(128)S(1)} %pad_add_fusion.place_ref, s32[1,192]{1,0:T(1,128)S(1)} %reshape.8.cols_ref, bf16[8,64,128]{2,1,0:T(8,128)(2,1)S(1)} %finish.19.own_ref.base_ref, ...), custom_call_target="tpu_custom_call" | custom-call | flops 20000000 | bytes 4194304 | tf_op jit(solution)/shard_map/prepare/pallas_call | solution.py:89
  72.8 2.6 %collective-permute-start.16 = (bf16[8,64,128]{2,1,0:T(8,128)(2,1)S(1)}, bf16[8,64,128]{2,1,0:T(8,128)(2,1)S(1)}, u32[]{:S(2)}, u32[]{:S(2)}) collective-permute-start(bf16[8,64,128]{2,1,0:T(8,128)(2,1)S(1)} %finish.21.own_ref), channel_id=1, source_target_pairs={{0,252},{4,8},{8,4},{12,16},{16,12},{20,24},{24,20},{28,32},{32,28... | collective-permute-start | bytes 393224 | tf_op jit(solution)/shard_map/ppermute | solution.py:173
  75.4 2.8 %copy-done.2 = bf16[8,8,1,3,128,128]{5,4,3,2,1,0:T(8,128)(2,1)S(1)} copy-done((bf16[8,8,1,3,128,128]{5,4,3,2,1,0:T(8,128)(2,1)S(1)}, bf16[8,8,1,3,128,128]{5,4,3,2,1,0:T(8,128)(2,1)}, u32[]{:S(2)}) %copy-start.2) | copy-done | bytes 6291480
  78.1 2.1 %prepare.22 = (f32[8,64,128]{2,1,0:T(8,128)S(1)}, bf16[8,128,512]{2,1,0:T(8,128)(2,1)S(1)}, bf16[8,8,1,64,128]{4,3,2,1,0:T(8,128)(2,1)}) custom-call(s32[4]{0:T(128)S(1)} %pad_add_fusion.place_ref, s32[1,192]{1,0:T(1,128)S(1)} %reshape.8.cols_ref, bf16[8,64,128]{2,1,0:T(8,128)(2,1)S(1)} %finish.18.own_ref.base_ref, ...), custom_call_target="tpu_custom_call", output_to_operand_aliasing={{2}: (6, {})} | custom-call | flops 20000000 | bytes 4194304 | tf_op jit(solution)/shard_map/prepare/pallas_call | solution.py:89
  81.1 2.6 %collective-permute-start.18 = (bf16[8,64,128]{2,1,0:T(8,128)(2,1)S(1)}, bf16[8,64,128]{2,1,0:T(8,128)(2,1)S(1)}, u32[]{:S(2)}, u32[]{:S(2)}) collective-permute-start(bf16[8,64,128]{2,1,0:T(8,128)(2,1)S(1)} %finish.22.own_ref), channel_id=1, source_target_pairs={{0,252},{4,8},{8,4},{12,16},{16,12},{20,24},{24,20},{28,32},{32,28... | collective-permute-start | bytes 393224 | tf_op jit(solution)/shard_map/ppermute | solution.py:173
  85.7 3.1 %collective-permute-done.18.far_ref = bf16[8,64,128]{2,1,0:T(8,128)(2,1)S(1)} collective-permute-done((bf16[8,64,128]{2,1,0:T(8,128)(2,1)S(1)}, bf16[8,64,128]{2,1,0:T(8,128)(2,1)S(1)}, u32[]{:S(2)}, u32[]{:S(2)}) %collective-permute-start.18) | collective-permute-done | bytes 131104 | tf_op jit(solution)/shard_map/ppermute | solution.py:173
  89.3 2.6 %collective-permute-start.20 = (bf16[8,64,128]{2,1,0:T(8,128)(2,1)S(1)}, bf16[8,64,128]{2,1,0:T(8,128)(2,1)S(1)}, u32[]{:S(2)}, u32[]{:S(2)}) collective-permute-start(bf16[8,64,128]{2,1,0:T(8,128)(2,1)S(1)} %finish.23.own_ref), channel_id=1, source_target_pairs={{0,252},{4,8},{8,4},{12,16},{16,12},{20,24},{24,20},{28,32},{32,28... | collective-permute-start | bytes 393224 | tf_op jit(solution)/shard_map/ppermute | solution.py:173
  94.0 3.1 %collective-permute-done.20.far_ref = bf16[8,64,128]{2,1,0:T(8,128)(2,1)S(1)} collective-permute-done((bf16[8,64,128]{2,1,0:T(8,128)(2,1)S(1)}, bf16[8,64,128]{2,1,0:T(8,128)(2,1)S(1)}, u32[]{:S(2)}, u32[]{:S(2)}) %collective-permute-start.20) | collective-permute-done | bytes 131104 | tf_op jit(solution)/shard_map/ppermute | solution.py:173
  97.6 2.6 %collective-permute-start.22 = (bf16[8,64,128]{2,1,0:T(8,128)(2,1)S(1)}, bf16[8,64,128]{2,1,0:T(8,128)(2,1)S(1)}, u32[]{:S(2)}, u32[]{:S(2)}) collective-permute-start(bf16[8,64,128]{2,1,0:T(8,128)(2,1)S(1)} %finish.24.own_ref), channel_id=1, source_target_pairs={{0,252},{4,8},{8,4},{12,16},{16,12},{20,24},{24,20},{28,32},{32,28... | collective-permute-start | bytes 393224 | tf_op jit(solution)/shard_map/ppermute | solution.py:173
  100.2 2.1 %prepare.25 = (f32[8,64,128]{2,1,0:T(8,128)S(1)}, bf16[8,128,512]{2,1,0:T(8,128)(2,1)S(1)}, bf16[8,8,1,64,128]{4,3,2,1,0:T(8,128)(2,1)}) custom-call(s32[4]{0:T(128)S(1)} %pad_add_fusion.place_ref, s32[1,192]{1,0:T(1,128)S(1)} %reshape.8.cols_ref, bf16[8,64,128]{2,1,0:T(8,128)(2,1)S(1)} %finish.15.own_ref.base_ref, ...), custom_call_target="tpu_custom_call", output_to_operand_aliasing={{2}: (6, {})} | custom-call | flops 20000000 | bytes 4194304 | tf_op jit(solution)/shard_map/prepare/pallas_call | solution.py:89
  102.3 3.1 %collective-permute-done.22.far_ref = bf16[8,64,128]{2,1,0:T(8,128)(2,1)S(1)} collective-permute-done((bf16[8,64,128]{2,1,0:T(8,128)(2,1)S(1)}, bf16[8,64,128]{2,1,0:T(8,128)(2,1)S(1)}, u32[]{:S(2)}, u32[]{:S(2)}) %collective-permute-start.22) | collective-permute-done | bytes 131104 | tf_op jit(solution)/shard_map/ppermute | solution.py:173
  105.9 2.6 %collective-permute-start.24 = (bf16[8,64,128]{2,1,0:T(8,128)(2,1)S(1)}, bf16[8,64,128]{2,1,0:T(8,128)(2,1)S(1)}, u32[]{:S(2)}, u32[]{:S(2)}) collective-permute-start(bf16[8,64,128]{2,1,0:T(8,128)(2,1)S(1)} %finish.25.own_ref), channel_id=1, source_target_pairs={{0,252},{4,8},{8,4},{12,16},{16,12},{20,24},{24,20},{28,32},{32,28... | collective-permute-start | bytes 393224 | tf_op jit(solution)/shard_map/ppermute | solution.py:173
  110.6 3.1 %collective-permute-done.24.far_ref = bf16[8,64,128]{2,1,0:T(8,128)(2,1)S(1)} collective-permute-done((bf16[8,64,128]{2,1,0:T(8,128)(2,1)S(1)}, bf16[8,64,128]{2,1,0:T(8,128)(2,1)S(1)}, u32[]{:S(2)}, u32[]{:S(2)}) %collective-permute-start.24) | collective-permute-done | bytes 131104 | tf_op jit(solution)/shard_map/ppermute | solution.py:173
  114.2 2.6 %collective-permute-start.26 = (bf16[8,64,128]{2,1,0:T(8,128)(2,1)S(1)}, bf16[8,64,128]{2,1,0:T(8,128)(2,1)S(1)}, u32[]{:S(2)}, u32[]{:S(2)}) collective-permute-start(bf16[8,64,128]{2,1,0:T(8,128)(2,1)S(1)} %finish.26.own_ref), channel_id=1, source_target_pairs={{0,252},{4,8},{8,4},{12,16},{16,12},{20,24},{24,20},{28,32},{32,28... | collective-permute-start | bytes 393224 | tf_op jit(solution)/shard_map/ppermute | solution.py:173
  118.9 3.1 %collective-permute-done.26.far_ref = bf16[8,64,128]{2,1,0:T(8,128)(2,1)S(1)} collective-permute-done((bf16[8,64,128]{2,1,0:T(8,128)(2,1)S(1)}, bf16[8,64,128]{2,1,0:T(8,128)(2,1)S(1)}, u32[]{:S(2)}, u32[]{:S(2)}) %collective-permute-start.26) | collective-permute-done | bytes 131104 | tf_op jit(solution)/shard_map/ppermute | solution.py:173
  (78 shorter events, 37.8 us)
Async XLA Ops:
  1.0 14.2 %collective-permute-start = (bf16[8,64,128]{2,1,0:T(8,128)(2,1)S(1)}, bf16[8,64,128]{2,1,0:T(8,128)(2,1)S(1)}, u32[]{:S(2)}, u32[]{:S(2)}) collective-permute-start(bf16[8,64,128]{2,1,0:T(8,128)(2,1)S(1)} %fusion.own_ref.base_ref), channel_id=1, source_target_pairs={{0,252},{4,8},{8,4},{12,16},{16,12},{20,24},{24,20},{28,32},{32,28... | collective-permute-start | bytes 393224 | tf_op jit(solution)/shard_map/ppermute | solution.py:173
  8.8 6.3 %collective-permute-start.1 = (bf16[8,64,128]{2,1,0:T(8,128)(2,1)S(1)}, bf16[8,64,128]{2,1,0:T(8,128)(2,1)S(1)}, u32[]{:S(2)}, u32[]{:S(2)}) collective-permute-start(bf16[8,64,128]{2,1,0:T(8,128)(2,1)S(1)} %fusion.own_ref.base_ref), channel_id=1, source_target_pairs={{0,4},{4,0},{8,12},{12,8},{16,20},{20,16},{24,28},{28,24},{32,36},... | collective-permute-start | bytes 393224 | tf_op jit(solution)/shard_map/ppermute | solution.py:174
  15.5 7.8 %collective-permute-start.2 = (bf16[8,64,128]{2,1,0:T(8,128)(2,1)S(1)}, bf16[8,64,128]{2,1,0:T(8,128)(2,1)S(1)}, u32[]{:S(2)}, u32[]{:S(2)}) collective-permute-start(bf16[8,64,128]{2,1,0:T(8,128)(2,1)S(1)} %finish.14.own_ref.base_ref), channel_id=1, source_target_pairs={{0,252},{4,8},{8,4},{12,16},{16,12},{20,24},{24,20},{28,32},{32,28... | collective-permute-start | bytes 393224 | tf_op jit(solution)/shard_map/ppermute | solution.py:173
  16.9 6.4 %collective-permute-start.3 = (bf16[8,64,128]{2,1,0:T(8,128)(2,1)S(1)}, bf16[8,64,128]{2,1,0:T(8,128)(2,1)S(1)}, u32[]{:S(2)}, u32[]{:S(2)}) collective-permute-start(bf16[8,64,128]{2,1,0:T(8,128)(2,1)S(1)} %finish.14.own_ref.base_ref), channel_id=1, source_target_pairs={{0,4},{4,0},{8,12},{12,8},{16,20},{20,16},{24,28},{28,24},{32,36},... | collective-permute-start | bytes 393224 | tf_op jit(solution)/shard_map/ppermute | solution.py:174
  23.6 7.8 %collective-permute-start.4 = (bf16[8,64,128]{2,1,0:T(8,128)(2,1)S(1)}, bf16[8,64,128]{2,1,0:T(8,128)(2,1)S(1)}, u32[]{:S(2)}, u32[]{:S(2)}) collective-permute-start(bf16[8,64,128]{2,1,0:T(8,128)(2,1)S(1)} %finish.15.own_ref.base_ref), channel_id=1, source_target_pairs={{0,252},{4,8},{8,4},{12,16},{16,12},{20,24},{24,20},{28,32},{32,28... | collective-permute-start | bytes 393224 | tf_op jit(solution)/shard_map/ppermute | solution.py:173
  25.0 6.4 %collective-permute-start.5 = (bf16[8,64,128]{2,1,0:T(8,128)(2,1)S(1)}, bf16[8,64,128]{2,1,0:T(8,128)(2,1)S(1)}, u32[]{:S(2)}, u32[]{:S(2)}) collective-permute-start(bf16[8,64,128]{2,1,0:T(8,128)(2,1)S(1)} %finish.15.own_ref.base_ref), channel_id=1, source_target_pairs={{0,4},{4,0},{8,12},{12,8},{16,20},{20,16},{24,28},{28,24},{32,36},... | collective-permute-start | bytes 393224 | tf_op jit(solution)/shard_map/ppermute | solution.py:174
  31.7 7.8 %collective-permute-start.6 = (bf16[8,64,128]{2,1,0:T(8,128)(2,1)S(1)}, bf16[8,64,128]{2,1,0:T(8,128)(2,1)S(1)}, u32[]{:S(2)}, u32[]{:S(2)}) collective-permute-start(bf16[8,64,128]{2,1,0:T(8,128)(2,1)S(1)} %finish.16.own_ref.base_ref), channel_id=1, source_target_pairs={{0,252},{4,8},{8,4},{12,16},{16,12},{20,24},{24,20},{28,32},{32,28... | collective-permute-start | bytes 393224 | tf_op jit(solution)/shard_map/ppermute | solution.py:173
  33.1 6.4 %collective-permute-start.7 = (bf16[8,64,128]{2,1,0:T(8,128)(2,1)S(1)}, bf16[8,64,128]{2,1,0:T(8,128)(2,1)S(1)}, u32[]{:S(2)}, u32[]{:S(2)}) collective-permute-start(bf16[8,64,128]{2,1,0:T(8,128)(2,1)S(1)} %finish.16.own_ref.base_ref), channel_id=1, source_target_pairs={{0,4},{4,0},{8,12},{12,8},{16,20},{20,16},{24,28},{28,24},{32,36},... | collective-permute-start | bytes 393224 | tf_op jit(solution)/shard_map/ppermute | solution.py:174
  39.8 7.8 %collective-permute-start.8 = (bf16[8,64,128]{2,1,0:T(8,128)(2,1)S(1)}, bf16[8,64,128]{2,1,0:T(8,128)(2,1)S(1)}, u32[]{:S(2)}, u32[]{:S(2)}) collective-permute-start(bf16[8,64,128]{2,1,0:T(8,128)(2,1)S(1)} %finish.17.own_ref.base_ref), channel_id=1, source_target_pairs={{0,252},{4,8},{8,4},{12,16},{16,12},{20,24},{24,20},{28,32},{32,28... | collective-permute-start | bytes 393224 | tf_op jit(solution)/shard_map/ppermute | solution.py:173
  41.2 6.4 %collective-permute-start.9 = (bf16[8,64,128]{2,1,0:T(8,128)(2,1)S(1)}, bf16[8,64,128]{2,1,0:T(8,128)(2,1)S(1)}, u32[]{:S(2)}, u32[]{:S(2)}) collective-permute-start(bf16[8,64,128]{2,1,0:T(8,128)(2,1)S(1)} %finish.17.own_ref.base_ref), channel_id=1, source_target_pairs={{0,4},{4,0},{8,12},{12,8},{16,20},{20,16},{24,28},{28,24},{32,36},... | collective-permute-start | bytes 393224 | tf_op jit(solution)/shard_map/ppermute | solution.py:174
  47.9 7.8 %collective-permute-start.10 = (bf16[8,64,128]{2,1,0:T(8,128)(2,1)S(1)}, bf16[8,64,128]{2,1,0:T(8,128)(2,1)S(1)}, u32[]{:S(2)}, u32[]{:S(2)}) collective-permute-start(bf16[8,64,128]{2,1,0:T(8,128)(2,1)S(1)} %finish.18.own_ref.base_ref), channel_id=1, source_target_pairs={{0,252},{4,8},{8,4},{12,16},{16,12},{20,24},{24,20},{28,32},{32,28... | collective-permute-start | bytes 393224 | tf_op jit(solution)/shard_map/ppermute | solution.py:173
  49.3 6.4 %collective-permute-start.11 = (bf16[8,64,128]{2,1,0:T(8,128)(2,1)S(1)}, bf16[8,64,128]{2,1,0:T(8,128)(2,1)S(1)}, u32[]{:S(2)}, u32[]{:S(2)}) collective-permute-start(bf16[8,64,128]{2,1,0:T(8,128)(2,1)S(1)} %finish.18.own_ref.base_ref), channel_id=1, source_target_pairs={{0,4},{4,0},{8,12},{12,8},{16,20},{20,16},{24,28},{28,24},{32,36},... | collective-permute-start | bytes 393224 | tf_op jit(solution)/shard_map/ppermute | solution.py:174
  56.0 7.8 %collective-permute-start.12 = (bf16[8,64,128]{2,1,0:T(8,128)(2,1)S(1)}, bf16[8,64,128]{2,1,0:T(8,128)(2,1)S(1)}, u32[]{:S(2)}, u32[]{:S(2)}) collective-permute-start(bf16[8,64,128]{2,1,0:T(8,128)(2,1)S(1)} %finish.19.own_ref.base_ref), channel_id=1, source_target_pairs={{0,252},{4,8},{8,4},{12,16},{16,12},{20,24},{24,20},{28,32},{32,28... | collective-permute-start | bytes 393224 | tf_op jit(solution)/shard_map/ppermute | solution.py:173
  57.5 6.4 %collective-permute-start.13 = (bf16[8,64,128]{2,1,0:T(8,128)(2,1)S(1)}, bf16[8,64,128]{2,1,0:T(8,128)(2,1)S(1)}, u32[]{:S(2)}, u32[]{:S(2)}) collective-permute-start(bf16[8,64,128]{2,1,0:T(8,128)(2,1)S(1)} %finish.19.own_ref.base_ref), channel_id=1, source_target_pairs={{0,4},{4,0},{8,12},{12,8},{16,20},{20,16},{24,28},{28,24},{32,36},... | collective-permute-start | bytes 393224 | tf_op jit(solution)/shard_map/ppermute | solution.py:174
  64.3 8.0 %collective-permute-start.14 = (bf16[8,64,128]{2,1,0:T(8,128)(2,1)S(1)}, bf16[8,64,128]{2,1,0:T(8,128)(2,1)S(1)}, u32[]{:S(2)}, u32[]{:S(2)}) collective-permute-start(bf16[8,64,128]{2,1,0:T(8,128)(2,1)S(1)} %finish.20.own_ref), channel_id=1, source_target_pairs={{0,252},{4,8},{8,4},{12,16},{16,12},{20,24},{24,20},{28,32},{32,28... | collective-permute-start | bytes 393224 | tf_op jit(solution)/shard_map/ppermute | solution.py:173
  65.9 6.4 %collective-permute-start.15 = (bf16[8,64,128]{2,1,0:T(8,128)(2,1)S(1)}, bf16[8,64,128]{2,1,0:T(8,128)(2,1)S(1)}, u32[]{:S(2)}, u32[]{:S(2)}) collective-permute-start(bf16[8,64,128]{2,1,0:T(8,128)(2,1)S(1)} %finish.20.own_ref), channel_id=1, source_target_pairs={{0,4},{4,0},{8,12},{12,8},{16,20},{20,16},{24,28},{28,24},{32,36},... | collective-permute-start | bytes 393224 | tf_op jit(solution)/shard_map/ppermute | solution.py:174
  72.8 7.8 %collective-permute-start.16 = (bf16[8,64,128]{2,1,0:T(8,128)(2,1)S(1)}, bf16[8,64,128]{2,1,0:T(8,128)(2,1)S(1)}, u32[]{:S(2)}, u32[]{:S(2)}) collective-permute-start(bf16[8,64,128]{2,1,0:T(8,128)(2,1)S(1)} %finish.21.own_ref), channel_id=1, source_target_pairs={{0,252},{4,8},{8,4},{12,16},{16,12},{20,24},{24,20},{28,32},{32,28... | collective-permute-start | bytes 393224 | tf_op jit(solution)/shard_map/ppermute | solution.py:173
  81.1 7.8 %collective-permute-start.18 = (bf16[8,64,128]{2,1,0:T(8,128)(2,1)S(1)}, bf16[8,64,128]{2,1,0:T(8,128)(2,1)S(1)}, u32[]{:S(2)}, u32[]{:S(2)}) collective-permute-start(bf16[8,64,128]{2,1,0:T(8,128)(2,1)S(1)} %finish.22.own_ref), channel_id=1, source_target_pairs={{0,252},{4,8},{8,4},{12,16},{16,12},{20,24},{24,20},{28,32},{32,28... | collective-permute-start | bytes 393224 | tf_op jit(solution)/shard_map/ppermute | solution.py:173
  89.3 7.8 %collective-permute-start.20 = (bf16[8,64,128]{2,1,0:T(8,128)(2,1)S(1)}, bf16[8,64,128]{2,1,0:T(8,128)(2,1)S(1)}, u32[]{:S(2)}, u32[]{:S(2)}) collective-permute-start(bf16[8,64,128]{2,1,0:T(8,128)(2,1)S(1)} %finish.23.own_ref), channel_id=1, source_target_pairs={{0,252},{4,8},{8,4},{12,16},{16,12},{20,24},{24,20},{28,32},{32,28... | collective-permute-start | bytes 393224 | tf_op jit(solution)/shard_map/ppermute | solution.py:173
  91.9 5.2 %collective-permute-start.21 = (bf16[8,64,128]{2,1,0:T(8,128)(2,1)S(1)}, bf16[8,64,128]{2,1,0:T(8,128)(2,1)S(1)}, u32[]{:S(2)}, u32[]{:S(2)}) collective-permute-start(bf16[8,64,128]{2,1,0:T(8,128)(2,1)S(1)} %finish.23.own_ref), channel_id=1, source_target_pairs={{0,4},{4,0},{8,12},{12,8},{16,20},{20,16},{24,28},{28,24},{32,36},... | collective-permute-start | bytes 393224 | tf_op jit(solution)/shard_map/ppermute | solution.py:174
  97.6 7.8 %collective-permute-start.22 = (bf16[8,64,128]{2,1,0:T(8,128)(2,1)S(1)}, bf16[8,64,128]{2,1,0:T(8,128)(2,1)S(1)}, u32[]{:S(2)}, u32[]{:S(2)}) collective-permute-start(bf16[8,64,128]{2,1,0:T(8,128)(2,1)S(1)} %finish.24.own_ref), channel_id=1, source_target_pairs={{0,252},{4,8},{8,4},{12,16},{16,12},{20,24},{24,20},{28,32},{32,28... | collective-permute-start | bytes 393224 | tf_op jit(solution)/shard_map/ppermute | solution.py:173
  100.2 5.2 %collective-permute-start.23 = (bf16[8,64,128]{2,1,0:T(8,128)(2,1)S(1)}, bf16[8,64,128]{2,1,0:T(8,128)(2,1)S(1)}, u32[]{:S(2)}, u32[]{:S(2)}) collective-permute-start(bf16[8,64,128]{2,1,0:T(8,128)(2,1)S(1)} %finish.24.own_ref), channel_id=1, source_target_pairs={{0,4},{4,0},{8,12},{12,8},{16,20},{20,16},{24,28},{28,24},{32,36},... | collective-permute-start | bytes 393224 | tf_op jit(solution)/shard_map/ppermute | solution.py:174
  105.9 7.8 %collective-permute-start.24 = (bf16[8,64,128]{2,1,0:T(8,128)(2,1)S(1)}, bf16[8,64,128]{2,1,0:T(8,128)(2,1)S(1)}, u32[]{:S(2)}, u32[]{:S(2)}) collective-permute-start(bf16[8,64,128]{2,1,0:T(8,128)(2,1)S(1)} %finish.25.own_ref), channel_id=1, source_target_pairs={{0,252},{4,8},{8,4},{12,16},{16,12},{20,24},{24,20},{28,32},{32,28... | collective-permute-start | bytes 393224 | tf_op jit(solution)/shard_map/ppermute | solution.py:173
  114.2 7.8 %collective-permute-start.26 = (bf16[8,64,128]{2,1,0:T(8,128)(2,1)S(1)}, bf16[8,64,128]{2,1,0:T(8,128)(2,1)S(1)}, u32[]{:S(2)}, u32[]{:S(2)}) collective-permute-start(bf16[8,64,128]{2,1,0:T(8,128)(2,1)S(1)} %finish.26.own_ref), channel_id=1, source_target_pairs={{0,252},{4,8},{8,4},{12,16},{16,12},{20,24},{24,20},{28,32},{32,28... | collective-permute-start | bytes 393224 | tf_op jit(solution)/shard_map/ppermute | solution.py:173
  (10 other events, 48.9 us)

commit v4 on v2

--- a/solution.py
+++ b/solution.py
@@ -19,7 +19,7 @@
     return jnp.concatenate([coarse, fine], axis=1)
 
 
-def prepare_kernel(level, with_inverse, write_to, continued, place_ref, cols_ref, base_ref, tiles_ref, own_ref, near_ref, *refs):
+def prepare_kernel(level, with_inverse, write_to, continued, place_ref, cols_ref, base_ref, tiles_ref, own_ref, low_ref, high_ref, *refs):
     refs = list(refs)
     inverse_ref = refs.pop(0) if with_inverse else None
     if continued:
@@ -43,7 +43,8 @@
             return jnp.where(hits[0] | hits[1] | hits[2], tile, jnp.zeros_like(tile))
 
         base = base_ref[m] if len(base_ref.shape) == 3 else base_ref[0, m, 0]
-        both = jnp.concatenate([own_ref[m], near_ref[m]], axis=1)
+        near = low_ref[m] if m < rows // 2 else high_ref[m - rows // 2]
+        both = jnp.concatenate([own_ref[m], near], axis=1)
         tiles = jnp.concatenate([tile_of(here), tile_of(partner)], axis=1)
         total = base.astype(jnp.float32) - times_transposed(both, tiles)
         if with_inverse:
@@ -65,14 +66,15 @@
         (1,) + a.shape[1:], lambda i: (level,) + (0,) * (len(a.shape) - 1)
     )
     whole = lambda a: pl.BlockSpec(a.shape, lambda i: (0,) * len(a.shape))
-    args = [place, columns, base, tiles, own, near]
+    args = [place, columns, base, tiles, own, *near]
     specs = [
         pl.BlockSpec(memory_space=pltpu.SMEM),
         pl.BlockSpec(memory_space=pltpu.SMEM),
         level_block(base) if len(base.shape) == 5 else whole(base),
         level_block(tiles),
         whole(own),
-        whole(near),
+        whole(near[0]),
+        whole(near[1]),
     ]
     deep = width if inverse is None else 2 * width
     shapes = [
@@ -108,15 +110,19 @@
 
 
 def finish_kernel(write_to, far_ref, total_ref, beside_ref, *refs):
+    rows = far_ref.shape[0]
     if write_to is None:
-        (out_ref,) = refs
+        out_ref, *halves = refs
     else:
         _, result_ref, out_ref, sem = refs
-    for m in range(far_ref.shape[0]):
+    for m in range(rows):
         far = far_ref[m]
         if beside_ref.shape[2] == 2 * far.shape[1]:
             far = jnp.concatenate([far, far], axis=1)
-        out_ref[m] = (total_ref[m] - times_transposed(far, beside_ref[m])).astype(jnp.bfloat16)
+        value = (total_ref[m] - times_transposed(far, beside_ref[m])).astype(jnp.bfloat16)
+        out_ref[m] = value
+        if write_to is None:
+            halves[m * 2 // rows][m % (rows // 2)] = value
     if write_to is not None:
         copy = pltpu.make_async_copy(out_ref, result_ref.at[write_to, :, 0], sem)
         copy.start()
@@ -127,7 +133,8 @@
     whole = pl.BlockSpec(memory_space=pltpu.VMEM)
     args, specs = [far, total, beside], [whole] * 3
     more = {}
-    out, out_spec = jax.ShapeDtypeStruct(far.shape, jnp.bfloat16), whole
+    half = jax.ShapeDtypeStruct((far.shape[0] // 2,) + far.shape[1:], jnp.bfloat16)
+    out, out_spec = [jax.ShapeDtypeStruct(far.shape, jnp.bfloat16), half, half], [whole] * 3
     if write_to is not None:
         out, out_spec = jax.ShapeDtypeStruct(result.shape, result.dtype), pl.BlockSpec(memory_space=pltpu.HBM)
         args.append(result)
@@ -163,11 +170,12 @@
 
     solved = [rhs[0, :, 0].astype(jnp.bfloat16)]
     current, result = solved[0], None
+    halves = (current[: rows // 2], current[rows // 2 :])
     steps = [(True, l) for l in range(1, levels)] + [(False, l) for l in range(levels - 2, -1, -1)]
     for forward, level in steps:
         tail = level == levels - 1 or not forward
         far = lax.ppermute(current, "blk", across)
-        near = lax.ppermute(current, "blk", pairs)
+        near = [lax.ppermute(half, "blk", pairs) for half in halves]
         parts = prepare(
             level,
             place,
@@ -184,7 +192,7 @@
         if not forward:
             result = parts[2]
         if level or forward:
-            current = finish(far, parts[0], parts[1])
+            current, *halves = finish(far, parts[0], parts[1])
         else:
             result = finish(far, parts[0], parts[1], level, result)
         if forward:

time: 124 us -> 126 us (1.016)
  starting transfers between devices: 36 us -> 48.3 us
  waiting for transfers between devices: 46.7 us -> 35.9 us
  other arithmetic: 0.08 us -> 2.02 us
  local copies, waits for them, and re-layouts: 12.1 us -> 10.5 us
    ppermute x14, waiting for transfers between devices: 46.6 us -> 23.9 us  [on_device(): far = lax.ppermute(current, 'blk', across)]
    ppermute x14 -> x28, waiting for transfers between devices: 0.04 us -> 12 us  [on_device(): near = [lax.ppermute(half, 'blk', pairs) for half in halves]]
    ppermute x14, starting transfers between devices: 34.7 us -> 41.1 us  [on_device(): far = lax.ppermute(current, 'blk', across)]
    ppermute x14 -> x28, starting transfers between devices: 1.3 us -> 7.22 us  [on_device(): near = [lax.ppermute(half, 'blk', pairs) for half in halves]]
    another operation x0 -> x1, other arithmetic: none -> 1.94 us
    unnamed x14 -> x18, local copies, waits for them, and re-layouts: 10.9 us -> 10.2 us
  transfers between devices with their start and end apart: 28 -> 42, of which waited for: 12 -> 39; matrix products, arithmetic and copies ran while one was open for 1% -> 0% of each run, Pallas kernels for 19% -> 19%
where the time goes in v4:
time: 126 us
  starting transfers between devices  48.3 us (38%)
  waiting for transfers between devices  35.9 us (28%)
  Pallas kernels  28.6 us (23%)
  local copies, waits for them, and re-layouts  10.5 us (8%)
  other arithmetic  2.02 us (2%)
    ppermute x14, starting transfers between devices, on_device(): far = lax.ppermute(current, 'blk', across)  41.1 us
    ppermute x14, waiting for transfers between devices, on_device(): far = lax.ppermute(current, 'blk', across)  23.9 us
    pallas_call x14, Pallas kernels, prepare(): pl.pallas_call(functools.partial(prepare_kernel, level, inverse is not No...  23.9 us
    ppermute x28, waiting for transfers between devices, on_device(): near = [lax.ppermute(half, 'blk', pairs) for half in halves]  12 us
    unnamed x18, local copies, waits for them, and re-layouts  10.2 us
    ppermute x28, starting transfers between devices, on_device(): near = [lax.ppermute(half, 'blk', pairs) for half in halves]  7.22 us
    pallas_call x14, Pallas kernels, finish(): pl.pallas_call(functools.partial(finish_kernel, write_to), out_shape=out,...  4.73 us
  transfers between devices with their start and end apart: 42, of which 39 were waited for; matrix products, arithmetic and copies ran while one was open for 0% of the time, Pallas kernels for 19%

profile of v4, /device:TPU:6, one launch (start us, length us, event | category | flops | bytes accessed | tf_op | source)
XLA Modules:
  0.0 125.8 jit_solution(7751988180839056553)
XLA Ops:
  2.0 7.8 %collective-permute-start = (bf16[8,64,128]{2,1,0:T(8,128)(2,1)S(1)}, bf16[8,64,128]{2,1,0:T(8,128)(2,1)S(1)}, u32[]{:S(2)}, u32[]{:S(2)}) collective-permute-start(bf16[8,64,128]{2,1,0:T(8,128)(2,1)S(1)} %slice_bitcast_fusion.own_ref.base_ref), channel_id=1, source_target_pairs={{0,252},{4,8},{8,4},{12,16},{16,12},{20,24},{24,20},{28,32},{32,28... | collective-permute-start | bytes 393224 | tf_op jit(solution)/shard_map/ppermute | solution.py:177
  11.3 2.8 %copy-done = bf16[8,8,1,3,128,128]{5,4,3,2,1,0:T(8,128)(2,1)S(1)} copy-done((bf16[8,8,1,3,128,128]{5,4,3,2,1,0:T(8,128)(2,1)S(1)}, bf16[8,8,1,3,128,128]{5,4,3,2,1,0:T(8,128)(2,1)}, u32[]{:S(2)}) %copy-start) | copy-done | bytes 6291480
  15.3 2.5 %collective-permute-start.3 = (bf16[8,64,128]{2,1,0:T(8,128)(2,1)S(1)}, bf16[8,64,128]{2,1,0:T(8,128)(2,1)S(1)}, u32[]{:S(2)}, u32[]{:S(2)}) collective-permute-start(bf16[8,64,128]{2,1,0:T(8,128)(2,1)S(1)} %get-tuple-element.81.own_ref.base_ref), channel_id=1, source_target_pairs={{0,252},{4,8},{8,4},{12,16},{16,12},{20,24},{24,20},{28,32},{32,28... | collective-permute-start | bytes 393224 | tf_op jit(solution)/shard_map/ppermute | solution.py:177
  20.2 2.9 %collective-permute-done.3.far_ref = bf16[8,64,128]{2,1,0:T(8,128)(2,1)S(1)} collective-permute-done((bf16[8,64,128]{2,1,0:T(8,128)(2,1)S(1)}, bf16[8,64,128]{2,1,0:T(8,128)(2,1)S(1)}, u32[]{:S(2)}, u32[]{:S(2)}) %collective-permute-start.3) | collective-permute-done | bytes 131104 | tf_op jit(solution)/shard_map/ppermute | solution.py:177
  23.4 2.5 %collective-permute-start.6 = (bf16[8,64,128]{2,1,0:T(8,128)(2,1)S(1)}, bf16[8,64,128]{2,1,0:T(8,128)(2,1)S(1)}, u32[]{:S(2)}, u32[]{:S(2)}) collective-permute-start(bf16[8,64,128]{2,1,0:T(8,128)(2,1)S(1)} %get-tuple-element.86.own_ref.base_ref), channel_id=1, source_target_pairs={{0,252},{4,8},{8,4},{12,16},{16,12},{20,24},{24,20},{28,32},{32,28... | collective-permute-start | bytes 393224 | tf_op jit(solution)/shard_map/ppermute | solution.py:177
  28.3 2.9 %collective-permute-done.6.far_ref = bf16[8,64,128]{2,1,0:T(8,128)(2,1)S(1)} collective-permute-done((bf16[8,64,128]{2,1,0:T(8,128)(2,1)S(1)}, bf16[8,64,128]{2,1,0:T(8,128)(2,1)S(1)}, u32[]{:S(2)}, u32[]{:S(2)}) %collective-permute-start.6) | collective-permute-done | bytes 131104 | tf_op jit(solution)/shard_map/ppermute | solution.py:177
  31.5 2.5 %collective-permute-start.9 = (bf16[8,64,128]{2,1,0:T(8,128)(2,1)S(1)}, bf16[8,64,128]{2,1,0:T(8,128)(2,1)S(1)}, u32[]{:S(2)}, u32[]{:S(2)}) collective-permute-start(bf16[8,64,128]{2,1,0:T(8,128)(2,1)S(1)} %get-tuple-element.91.own_ref.base_ref), channel_id=1, source_target_pairs={{0,252},{4,8},{8,4},{12,16},{16,12},{20,24},{24,20},{28,32},{32,28... | collective-permute-start | bytes 393224 | tf_op jit(solution)/shard_map/ppermute | solution.py:177
  36.4 2.9 %collective-permute-done.9.far_ref = bf16[8,64,128]{2,1,0:T(8,128)(2,1)S(1)} collective-permute-done((bf16[8,64,128]{2,1,0:T(8,128)(2,1)S(1)}, bf16[8,64,128]{2,1,0:T(8,128)(2,1)S(1)}, u32[]{:S(2)}, u32[]{:S(2)}) %collective-permute-start.9) | collective-permute-done | bytes 131104 | tf_op jit(solution)/shard_map/ppermute | solution.py:177
  39.6 2.5 %collective-permute-start.12 = (bf16[8,64,128]{2,1,0:T(8,128)(2,1)S(1)}, bf16[8,64,128]{2,1,0:T(8,128)(2,1)S(1)}, u32[]{:S(2)}, u32[]{:S(2)}) collective-permute-start(bf16[8,64,128]{2,1,0:T(8,128)(2,1)S(1)} %get-tuple-element.96.own_ref.base_ref), channel_id=1, source_target_pairs={{0,252},{4,8},{8,4},{12,16},{16,12},{20,24},{24,20},{28,32},{32,28... | collective-permute-start | bytes 393224 | tf_op jit(solution)/shard_map/ppermute | solution.py:177
  44.5 2.9 %collective-permute-done.12.far_ref = bf16[8,64,128]{2,1,0:T(8,128)(2,1)S(1)} collective-permute-done((bf16[8,64,128]{2,1,0:T(8,128)(2,1)S(1)}, bf16[8,64,128]{2,1,0:T(8,128)(2,1)S(1)}, u32[]{:S(2)}, u32[]{:S(2)}) %collective-permute-start.12) | collective-permute-done | bytes 131104 | tf_op jit(solution)/shard_map/ppermute | solution.py:177
  47.7 2.5 %collective-permute-start.15 = (bf16[8,64,128]{2,1,0:T(8,128)(2,1)S(1)}, bf16[8,64,128]{2,1,0:T(8,128)(2,1)S(1)}, u32[]{:S(2)}, u32[]{:S(2)}) collective-permute-start(bf16[8,64,128]{2,1,0:T(8,128)(2,1)S(1)} %get-tuple-element.101.own_ref.base_ref), channel_id=1, source_target_pairs={{0,252},{4,8},{8,4},{12,16},{16,12},{20,24},{24,20},{28,32},{32,28... | collective-permute-start | bytes 393224 | tf_op jit(solution)/shard_map/ppermute | solution.py:177
  52.6 2.9 %collective-permute-done.15.far_ref = bf16[8,64,128]{2,1,0:T(8,128)(2,1)S(1)} collective-permute-done((bf16[8,64,128]{2,1,0:T(8,128)(2,1)S(1)}, bf16[8,64,128]{2,1,0:T(8,128)(2,1)S(1)}, u32[]{:S(2)}, u32[]{:S(2)}) %collective-permute-start.15) | collective-permute-done | bytes 131104 | tf_op jit(solution)/shard_map/ppermute | solution.py:177
  55.8 2.5 %collective-permute-start.18 = (bf16[8,64,128]{2,1,0:T(8,128)(2,1)S(1)}, bf16[8,64,128]{2,1,0:T(8,128)(2,1)S(1)}, u32[]{:S(2)}, u32[]{:S(2)}) collective-permute-start(bf16[8,64,128]{2,1,0:T(8,128)(2,1)S(1)} %get-tuple-element.106.own_ref.base_ref), channel_id=1, source_target_pairs={{0,252},{4,8},{8,4},{12,16},{16,12},{20,24},{24,20},{28,32},{32,28... | collective-permute-start | bytes 393224 | tf_op jit(solution)/shard_map/ppermute | solution.py:177
  63.9 2.5 %collective-permute-start.21 = (bf16[8,64,128]{2,1,0:T(8,128)(2,1)S(1)}, bf16[8,64,128]{2,1,0:T(8,128)(2,1)S(1)}, u32[]{:S(2)}, u32[]{:S(2)}) collective-permute-start(bf16[8,64,128]{2,1,0:T(8,128)(2,1)S(1)} %get-tuple-element.111.own_ref), channel_id=1, source_target_pairs={{0,252},{4,8},{8,4},{12,16},{16,12},{20,24},{24,20},{28,32},{32,28... | collective-permute-start | bytes 393224 | tf_op jit(solution)/shard_map/ppermute | solution.py:177
  67.8 2.8 %copy-done.1 = bf16[8,8,1,3,128,128]{5,4,3,2,1,0:T(8,128)(2,1)S(1)} copy-done((bf16[8,8,1,3,128,128]{5,4,3,2,1,0:T(8,128)(2,1)S(1)}, bf16[8,8,1,3,128,128]{5,4,3,2,1,0:T(8,128)(2,1)}, u32[]{:S(2)}) %copy-start.1) | copy-done | bytes 6291480
  74.9 2.7 %collective-permute-start.24 = (bf16[8,64,128]{2,1,0:T(8,128)(2,1)S(1)}, bf16[8,64,128]{2,1,0:T(8,128)(2,1)S(1)}, u32[]{:S(2)}, u32[]{:S(2)}) collective-permute-start(bf16[8,64,128]{2,1,0:T(8,128)(2,1)S(1)} %get-tuple-element.116.own_ref), channel_id=1, source_target_pairs={{0,252},{4,8},{8,4},{12,16},{16,12},{20,24},{24,20},{28,32},{32,28... | collective-permute-start | bytes 393224 | tf_op jit(solution)/shard_map/ppermute | solution.py:177
  79.0 2.8 %copy-done.2 = bf16[8,8,1,3,128,128]{5,4,3,2,1,0:T(8,128)(2,1)S(1)} copy-done((bf16[8,8,1,3,128,128]{5,4,3,2,1,0:T(8,128)(2,1)S(1)}, bf16[8,8,1,3,128,128]{5,4,3,2,1,0:T(8,128)(2,1)}, u32[]{:S(2)}) %copy-start.2) | copy-done | bytes 6291480
  84.4 2.5 %collective-permute-start.27 = (bf16[8,64,128]{2,1,0:T(8,128)(2,1)S(1)}, bf16[8,64,128]{2,1,0:T(8,128)(2,1)S(1)}, u32[]{:S(2)}, u32[]{:S(2)}) collective-permute-start(bf16[8,64,128]{2,1,0:T(8,128)(2,1)S(1)} %get-tuple-element.122.own_ref), channel_id=1, source_target_pairs={{0,252},{4,8},{8,4},{12,16},{16,12},{20,24},{24,20},{28,32},{32,28... | collective-permute-start | bytes 393224 | tf_op jit(solution)/shard_map/ppermute | solution.py:177
  88.4 2.3 %prepare.23 = (f32[8,64,128]{2,1,0:T(8,128)S(1)}, bf16[8,128,256]{2,1,0:T(8,128)(2,1)S(1)}, bf16[8,8,1,64,128]{4,3,2,1,0:T(8,128)(2,1)}) custom-call(s32[4]{0:T(128)S(1)} %pad_add_fusion.place_ref, s32[1,192]{1,0:T(1,128)S(1)} %reshape.10.cols_ref, bf16[8,64,128]{2,1,0:T(8,128)(2,1)S(1)} %get-tuple-element.96.own_ref.base_ref, ...), custom_call_target="tpu_custom_call", output_to_operand_aliasing={{2}: (8, {})} | custom-call | flops 20000000 | bytes 4194304 | tf_op jit(solution)/shard_map/prepare/pallas_call | solution.py:96
  92.5 2.5 %collective-permute-start.30 = (bf16[8,64,128]{2,1,0:T(8,128)(2,1)S(1)}, bf16[8,64,128]{2,1,0:T(8,128)(2,1)S(1)}, u32[]{:S(2)}, u32[]{:S(2)}) collective-permute-start(bf16[8,64,128]{2,1,0:T(8,128)(2,1)S(1)} %get-tuple-element.128.own_ref), channel_id=1, source_target_pairs={{0,252},{4,8},{8,4},{12,16},{16,12},{20,24},{24,20},{28,32},{32,28... | collective-permute-start | bytes 393224 | tf_op jit(solution)/shard_map/ppermute | solution.py:177
  100.6 2.5 %collective-permute-start.33 = (bf16[8,64,128]{2,1,0:T(8,128)(2,1)S(1)}, bf16[8,64,128]{2,1,0:T(8,128)(2,1)S(1)}, u32[]{:S(2)}, u32[]{:S(2)}) collective-permute-start(bf16[8,64,128]{2,1,0:T(8,128)(2,1)S(1)} %get-tuple-element.134.own_ref), channel_id=1, source_target_pairs={{0,252},{4,8},{8,4},{12,16},{16,12},{20,24},{24,20},{28,32},{32,28... | collective-permute-start | bytes 393224 | tf_op jit(solution)/shard_map/ppermute | solution.py:177
  108.7 2.5 %collective-permute-start.36 = (bf16[8,64,128]{2,1,0:T(8,128)(2,1)S(1)}, bf16[8,64,128]{2,1,0:T(8,128)(2,1)S(1)}, u32[]{:S(2)}, u32[]{:S(2)}) collective-permute-start(bf16[8,64,128]{2,1,0:T(8,128)(2,1)S(1)} %get-tuple-element.140.own_ref), channel_id=1, source_target_pairs={{0,252},{4,8},{8,4},{12,16},{16,12},{20,24},{24,20},{28,32},{32,28... | collective-permute-start | bytes 393224 | tf_op jit(solution)/shard_map/ppermute | solution.py:177
  112.7 2.3 %prepare.26 = (f32[8,64,128]{2,1,0:T(8,128)S(1)}, bf16[8,128,256]{2,1,0:T(8,128)(2,1)S(1)}, bf16[8,8,1,64,128]{4,3,2,1,0:T(8,128)(2,1)}) custom-call(s32[4]{0:T(128)S(1)} %pad_add_fusion.place_ref, s32[1,192]{1,0:T(1,128)S(1)} %reshape.10.cols_ref, bf16[8,64,128]{2,1,0:T(8,128)(2,1)S(1)} %get-tuple-element.81.own_ref.base_ref, ...), custom_call_target="tpu_custom_call", output_to_operand_aliasing={{2}: (8, {})} | custom-call | flops 20000000 | bytes 4194304 | tf_op jit(solution)/shard_map/prepare/pallas_call | solution.py:96
  116.8 2.5 %collective-permute-start.39 = (bf16[8,64,128]{2,1,0:T(8,128)(2,1)S(1)}, bf16[8,64,128]{2,1,0:T(8,128)(2,1)S(1)}, u32[]{:S(2)}, u32[]{:S(2)}) collective-permute-start(bf16[8,64,128]{2,1,0:T(8,128)(2,1)S(1)} %get-tuple-element.146.own_ref), channel_id=1, source_target_pairs={{0,252},{4,8},{8,4},{12,16},{16,12},{20,24},{24,20},{28,32},{32,28... | collective-permute-start | bytes 393224 | tf_op jit(solution)/shard_map/ppermute | solution.py:177
  (112 shorter events, 56.7 us)
Async XLA Ops:
  2.0 13.1 %collective-permute-start = (bf16[8,64,128]{2,1,0:T(8,128)(2,1)S(1)}, bf16[8,64,128]{2,1,0:T(8,128)(2,1)S(1)}, u32[]{:S(2)}, u32[]{:S(2)}) collective-permute-start(bf16[8,64,128]{2,1,0:T(8,128)(2,1)S(1)} %slice_bitcast_fusion.own_ref.base_ref), channel_id=1, source_target_pairs={{0,252},{4,8},{8,4},{12,16},{16,12},{20,24},{24,20},{28,32},{32,28... | collective-permute-start | bytes 393224 | tf_op jit(solution)/shard_map/ppermute | solution.py:177
  15.3 7.8 %collective-permute-start.3 = (bf16[8,64,128]{2,1,0:T(8,128)(2,1)S(1)}, bf16[8,64,128]{2,1,0:T(8,128)(2,1)S(1)}, u32[]{:S(2)}, u32[]{:S(2)}) collective-permute-start(bf16[8,64,128]{2,1,0:T(8,128)(2,1)S(1)} %get-tuple-element.81.own_ref.base_ref), channel_id=1, source_target_pairs={{0,252},{4,8},{8,4},{12,16},{16,12},{20,24},{24,20},{28,32},{32,28... | collective-permute-start | bytes 393224 | tf_op jit(solution)/shard_map/ppermute | solution.py:177
  17.9 1.4 %collective-permute-start.5 = (bf16[4,64,128]{2,1,0:T(8,128)(2,1)S(1)}, bf16[4,64,128]{2,1,0:T(8,128)(2,1)S(1)}, u32[]{:S(2)}, u32[]{:S(2)}) collective-permute-start(bf16[4,64,128]{2,1,0:T(8,128)(2,1)S(1)} %get-tuple-element.83), channel_id=1, source_target_pairs={{0,4},{4,0},{8,12},{12,8},{16,20},{20,16},{24,28},{28,24},{32,36},... | collective-permute-start | bytes 196616 | tf_op jit(solution)/shard_map/ppermute | solution.py:178
  23.4 7.8 %collective-permute-start.6 = (bf16[8,64,128]{2,1,0:T(8,128)(2,1)S(1)}, bf16[8,64,128]{2,1,0:T(8,128)(2,1)S(1)}, u32[]{:S(2)}, u32[]{:S(2)}) collective-permute-start(bf16[8,64,128]{2,1,0:T(8,128)(2,1)S(1)} %get-tuple-element.86.own_ref.base_ref), channel_id=1, source_target_pairs={{0,252},{4,8},{8,4},{12,16},{16,12},{20,24},{24,20},{28,32},{32,28... | collective-permute-start | bytes 393224 | tf_op jit(solution)/shard_map/ppermute | solution.py:177
  26.0 1.4 %collective-permute-start.8 = (bf16[4,64,128]{2,1,0:T(8,128)(2,1)S(1)}, bf16[4,64,128]{2,1,0:T(8,128)(2,1)S(1)}, u32[]{:S(2)}, u32[]{:S(2)}) collective-permute-start(bf16[4,64,128]{2,1,0:T(8,128)(2,1)S(1)} %get-tuple-element.88), channel_id=1, source_target_pairs={{0,4},{4,0},{8,12},{12,8},{16,20},{20,16},{24,28},{28,24},{32,36},... | collective-permute-start | bytes 196616 | tf_op jit(solution)/shard_map/ppermute | solution.py:178
  31.5 7.8 %collective-permute-start.9 = (bf16[8,64,128]{2,1,0:T(8,128)(2,1)S(1)}, bf16[8,64,128]{2,1,0:T(8,128)(2,1)S(1)}, u32[]{:S(2)}, u32[]{:S(2)}) collective-permute-start(bf16[8,64,128]{2,1,0:T(8,128)(2,1)S(1)} %get-tuple-element.91.own_ref.base_ref), channel_id=1, source_target_pairs={{0,252},{4,8},{8,4},{12,16},{16,12},{20,24},{24,20},{28,32},{32,28... | collective-permute-start | bytes 393224 | tf_op jit(solution)/shard_map/ppermute | solution.py:177
  34.1 1.4 %collective-permute-start.11 = (bf16[4,64,128]{2,1,0:T(8,128)(2,1)S(1)}, bf16[4,64,128]{2,1,0:T(8,128)(2,1)S(1)}, u32[]{:S(2)}, u32[]{:S(2)}) collective-permute-start(bf16[4,64,128]{2,1,0:T(8,128)(2,1)S(1)} %get-tuple-element.93), channel_id=1, source_target_pairs={{0,4},{4,0},{8,12},{12,8},{16,20},{20,16},{24,28},{28,24},{32,36},... | collective-permute-start | bytes 196616 | tf_op jit(solution)/shard_map/ppermute | solution.py:178
  39.6 7.8 %collective-permute-start.12 = (bf16[8,64,128]{2,1,0:T(8,128)(2,1)S(1)}, bf16[8,64,128]{2,1,0:T(8,128)(2,1)S(1)}, u32[]{:S(2)}, u32[]{:S(2)}) collective-permute-start(bf16[8,64,128]{2,1,0:T(8,128)(2,1)S(1)} %get-tuple-element.96.own_ref.base_ref), channel_id=1, source_target_pairs={{0,252},{4,8},{8,4},{12,16},{16,12},{20,24},{24,20},{28,32},{32,28... | collective-permute-start | bytes 393224 | tf_op jit(solution)/shard_map/ppermute | solution.py:177
  42.1 1.4 %collective-permute-start.14 = (bf16[4,64,128]{2,1,0:T(8,128)(2,1)S(1)}, bf16[4,64,128]{2,1,0:T(8,128)(2,1)S(1)}, u32[]{:S(2)}, u32[]{:S(2)}) collective-permute-start(bf16[4,64,128]{2,1,0:T(8,128)(2,1)S(1)} %get-tuple-element.98), channel_id=1, source_target_pairs={{0,4},{4,0},{8,12},{12,8},{16,20},{20,16},{24,28},{28,24},{32,36},... | collective-permute-start | bytes 196616 | tf_op jit(solution)/shard_map/ppermute | solution.py:178
  47.7 7.8 %collective-permute-start.15 = (bf16[8,64,128]{2,1,0:T(8,128)(2,1)S(1)}, bf16[8,64,128]{2,1,0:T(8,128)(2,1)S(1)}, u32[]{:S(2)}, u32[]{:S(2)}) collective-permute-start(bf16[8,64,128]{2,1,0:T(8,128)(2,1)S(1)} %get-tuple-element.101.own_ref.base_ref), channel_id=1, source_target_pairs={{0,252},{4,8},{8,4},{12,16},{16,12},{20,24},{24,20},{28,32},{32,28... | collective-permute-start | bytes 393224 | tf_op jit(solution)/shard_map/ppermute | solution.py:177
  50.2 1.4 %collective-permute-start.17 = (bf16[4,64,128]{2,1,0:T(8,128)(2,1)S(1)}, bf16[4,64,128]{2,1,0:T(8,128)(2,1)S(1)}, u32[]{:S(2)}, u32[]{:S(2)}) collective-permute-start(bf16[4,64,128]{2,1,0:T(8,128)(2,1)S(1)} %get-tuple-element.103), channel_id=1, source_target_pairs={{0,4},{4,0},{8,12},{12,8},{16,20},{20,16},{24,28},{28,24},{32,36},... | collective-permute-start | bytes 196616 | tf_op jit(solution)/shard_map/ppermute | solution.py:178
  55.8 7.8 %collective-permute-start.18 = (bf16[8,64,128]{2,1,0:T(8,128)(2,1)S(1)}, bf16[8,64,128]{2,1,0:T(8,128)(2,1)S(1)}, u32[]{:S(2)}, u32[]{:S(2)}) collective-permute-start(bf16[8,64,128]{2,1,0:T(8,128)(2,1)S(1)} %get-tuple-element.106.own_ref.base_ref), channel_id=1, source_target_pairs={{0,252},{4,8},{8,4},{12,16},{16,12},{20,24},{24,20},{28,32},{32,28... | collective-permute-start | bytes 393224 | tf_op jit(solution)/shard_map/ppermute | solution.py:177
  58.3 1.4 %collective-permute-start.20 = (bf16[4,64,128]{2,1,0:T(8,128)(2,1)S(1)}, bf16[4,64,128]{2,1,0:T(8,128)(2,1)S(1)}, u32[]{:S(2)}, u32[]{:S(2)}) collective-permute-start(bf16[4,64,128]{2,1,0:T(8,128)(2,1)S(1)} %get-tuple-element.108), channel_id=1, source_target_pairs={{0,4},{4,0},{8,12},{12,8},{16,20},{20,16},{24,28},{28,24},{32,36},... | collective-permute-start | bytes 196616 | tf_op jit(solution)/shard_map/ppermute | solution.py:178
  63.9 10.7 %collective-permute-start.21 = (bf16[8,64,128]{2,1,0:T(8,128)(2,1)S(1)}, bf16[8,64,128]{2,1,0:T(8,128)(2,1)S(1)}, u32[]{:S(2)}, u32[]{:S(2)}) collective-permute-start(bf16[8,64,128]{2,1,0:T(8,128)(2,1)S(1)} %get-tuple-element.111.own_ref), channel_id=1, source_target_pairs={{0,252},{4,8},{8,4},{12,16},{16,12},{20,24},{24,20},{28,32},{32,28... | collective-permute-start | bytes 393224 | tf_op jit(solution)/shard_map/ppermute | solution.py:177
  66.4 1.4 %collective-permute-start.23 = (bf16[4,64,128]{2,1,0:T(8,128)(2,1)S(1)}, bf16[4,64,128]{2,1,0:T(8,128)(2,1)S(1)}, u32[]{:S(2)}, u32[]{:S(2)}) collective-permute-start(bf16[4,64,128]{2,1,0:T(8,128)(2,1)S(1)} %get-tuple-element.113), channel_id=1, source_target_pairs={{0,4},{4,0},{8,12},{12,8},{16,20},{20,16},{24,28},{28,24},{32,36},... | collective-permute-start | bytes 196616 | tf_op jit(solution)/shard_map/ppermute | solution.py:178
  74.9 9.2 %collective-permute-start.24 = (bf16[8,64,128]{2,1,0:T(8,128)(2,1)S(1)}, bf16[8,64,128]{2,1,0:T(8,128)(2,1)S(1)}, u32[]{:S(2)}, u32[]{:S(2)}) collective-permute-start(bf16[8,64,128]{2,1,0:T(8,128)(2,1)S(1)} %get-tuple-element.116.own_ref), channel_id=1, source_target_pairs={{0,252},{4,8},{8,4},{12,16},{16,12},{20,24},{24,20},{28,32},{32,28... | collective-permute-start | bytes 393224 | tf_op jit(solution)/shard_map/ppermute | solution.py:177
  77.5 1.4 %collective-permute-start.26 = (bf16[4,64,128]{2,1,0:T(8,128)(2,1)S(1)}, bf16[4,64,128]{2,1,0:T(8,128)(2,1)S(1)}, u32[]{:S(2)}, u32[]{:S(2)}) collective-permute-start(bf16[4,64,128]{2,1,0:T(8,128)(2,1)S(1)} %get-tuple-element.118), channel_id=1, source_target_pairs={{0,4},{4,0},{8,12},{12,8},{16,20},{20,16},{24,28},{28,24},{32,36},... | collective-permute-start | bytes 196616 | tf_op jit(solution)/shard_map/ppermute | solution.py:178
  84.4 7.8 %collective-permute-start.27 = (bf16[8,64,128]{2,1,0:T(8,128)(2,1)S(1)}, bf16[8,64,128]{2,1,0:T(8,128)(2,1)S(1)}, u32[]{:S(2)}, u32[]{:S(2)}) collective-permute-start(bf16[8,64,128]{2,1,0:T(8,128)(2,1)S(1)} %get-tuple-element.122.own_ref), channel_id=1, source_target_pairs={{0,252},{4,8},{8,4},{12,16},{16,12},{20,24},{24,20},{28,32},{32,28... | collective-permute-start | bytes 393224 | tf_op jit(solution)/shard_map/ppermute | solution.py:177
  87.0 1.4 %collective-permute-start.29 = (bf16[4,64,128]{2,1,0:T(8,128)(2,1)S(1)}, bf16[4,64,128]{2,1,0:T(8,128)(2,1)S(1)}, u32[]{:S(2)}, u32[]{:S(2)}) collective-permute-start(bf16[4,64,128]{2,1,0:T(8,128)(2,1)S(1)} %get-tuple-element.124), channel_id=1, source_target_pairs={{0,4},{4,0},{8,12},{12,8},{16,20},{20,16},{24,28},{28,24},{32,36},... | collective-permute-start | bytes 196616 | tf_op jit(solution)/shard_map/ppermute | solution.py:178
  92.5 7.8 %collective-permute-start.30 = (bf16[8,64,128]{2,1,0:T(8,128)(2,1)S(1)}, bf16[8,64,128]{2,1,0:T(8,128)(2,1)S(1)}, u32[]{:S(2)}, u32[]{:S(2)}) collective-permute-start(bf16[8,64,128]{2,1,0:T(8,128)(2,1)S(1)} %get-tuple-element.128.own_ref), channel_id=1, source_target_pairs={{0,252},{4,8},{8,4},{12,16},{16,12},{20,24},{24,20},{28,32},{32,28... | collective-permute-start | bytes 393224 | tf_op jit(solution)/shard_map/ppermute | solution.py:177
  95.1 1.4 %collective-permute-start.32 = (bf16[4,64,128]{2,1,0:T(8,128)(2,1)S(1)}, bf16[4,64,128]{2,1,0:T(8,128)(2,1)S(1)}, u32[]{:S(2)}, u32[]{:S(2)}) collective-permute-start(bf16[4,64,128]{2,1,0:T(8,128)(2,1)S(1)} %get-tuple-element.130), channel_id=1, source_target_pairs={{0,4},{4,0},{8,12},{12,8},{16,20},{20,16},{24,28},{28,24},{32,36},... | collective-permute-start | bytes 196616 | tf_op jit(solution)/shard_map/ppermute | solution.py:178
  100.6 7.8 %collective-permute-start.33 = (bf16[8,64,128]{2,1,0:T(8,128)(2,1)S(1)}, bf16[8,64,128]{2,1,0:T(8,128)(2,1)S(1)}, u32[]{:S(2)}, u32[]{:S(2)}) collective-permute-start(bf16[8,64,128]{2,1,0:T(8,128)(2,1)S(1)} %get-tuple-element.134.own_ref), channel_id=1, source_target_pairs={{0,252},{4,8},{8,4},{12,16},{16,12},{20,24},{24,20},{28,32},{32,28... | collective-permute-start | bytes 393224 | tf_op jit(solution)/shard_map/ppermute | solution.py:177
  108.7 7.8 %collective-permute-start.36 = (bf16[8,64,128]{2,1,0:T(8,128)(2,1)S(1)}, bf16[8,64,128]{2,1,0:T(8,128)(2,1)S(1)}, u32[]{:S(2)}, u32[]{:S(2)}) collective-permute-start(bf16[8,64,128]{2,1,0:T(8,128)(2,1)S(1)} %get-tuple-element.140.own_ref), channel_id=1, source_target_pairs={{0,252},{4,8},{8,4},{12,16},{16,12},{20,24},{24,20},{28,32},{32,28... | collective-permute-start | bytes 393224 | tf_op jit(solution)/shard_map/ppermute | solution.py:177
  116.8 7.8 %collective-permute-start.39 = (bf16[8,64,128]{2,1,0:T(8,128)(2,1)S(1)}, bf16[8,64,128]{2,1,0:T(8,128)(2,1)S(1)}, u32[]{:S(2)}, u32[]{:S(2)}) collective-permute-start(bf16[8,64,128]{2,1,0:T(8,128)(2,1)S(1)} %get-tuple-element.146.own_ref), channel_id=1, source_target_pairs={{0,252},{4,8},{8,4},{12,16},{16,12},{20,24},{24,20},{28,32},{32,28... | collective-permute-start | bytes 393224 | tf_op jit(solution)/shard_map/ppermute | solution.py:177
  (26 other events, 71.7 us)

commit v5 on v3

--- a/solution.py
+++ b/solution.py
@@ -48,7 +48,8 @@
         if with_inverse:
             inverse = inverse_ref[0, m, 0]
             total = times_transposed(two_parts(total), jnp.concatenate([inverse, inverse], axis=1))
-            beside = two_parts(jnp.dot(inverse, beside, preferred_element_type=jnp.float32))
+            beside = jnp.dot(inverse, beside, preferred_element_type=jnp.float32)
+            beside = beside.astype(jnp.bfloat16)
         beside_ref[m] = beside
         total_ref[m] = total
     if write_to is not None:
@@ -69,10 +70,9 @@
         level_block(tiles),
         whole(own),
     ]
-    deep = 2 * width if inverse is None else 4 * width
     shapes = [
         jax.ShapeDtypeStruct((rows, sides, width), jnp.float32),
-        jax.ShapeDtypeStruct((rows, width, deep), jnp.bfloat16),
+        jax.ShapeDtypeStruct((rows, width, 2 * width), jnp.bfloat16),
     ]
     out_specs = [whole(s) for s in shapes]
     if inverse is not None:
@@ -110,10 +110,8 @@
     rows = far_ref.shape[0]
     copies = []
     for m in range(rows):
-        both = [near_ref[m], far_ref[m]]
-        if beside_ref.shape[2] == 4 * far_ref.shape[2]:
-            both = both + both
-        term = times_transposed(jnp.concatenate(both, axis=1), beside_ref[m])
+        both = jnp.concatenate([near_ref[m], far_ref[m]], axis=1)
+        term = times_transposed(both, beside_ref[m])
         out_ref[m] = (total_ref[m] - term).astype(jnp.bfloat16)
         if write_to is not None and m % 4 == 3:
             part = pl.ds(m - 3, 4)

time: 124 us -> 122 us (0.984)
    pallas_call x14, Pallas kernels: 6.33 us -> 4.87 us  [finish(): pl.pallas_call(functools.partial(finish_kernel, write_to), out_shape=out,...]
where the time goes in v5:
time: 122 us
  waiting for transfers between devices  48.4 us (40%)
  starting transfers between devices  33.9 us (28%)
  Pallas kernels  27 us (22%)
  local copies, waits for them, and re-layouts  12.1 us (10%)
    ppermute x14, waiting for transfers between devices, on_device(): far = lax.ppermute(current, 'blk', across)  48.3 us
    ppermute x14, starting transfers between devices, on_device(): far = lax.ppermute(current, 'blk', across)  33.9 us
    pallas_call x14, Pallas kernels, prepare(): pl.pallas_call(functools.partial(prepare_kernel, level, inverse is not No...  22.1 us
    unnamed x14, local copies, waits for them, and re-layouts  10.9 us
    pallas_call x14, Pallas kernels, finish(): pl.pallas_call(functools.partial(finish_kernel, write_to), out_shape=out,...  4.87 us
  transfers between devices with their start and end apart: 28, of which 13 were waited for; matrix products, arithmetic and copies ran while one was open for 1% of the time, Pallas kernels for 18%

profile of v5, /device:TPU:6, one launch (start us, length us, event | category | flops | bytes accessed | tf_op | source)
XLA Modules:
  0.0 121.9 jit_solution(9733079426665999232)
XLA Ops:
  1.0 7.8 %collective-permute-start = (bf16[8,64,128]{2,1,0:T(8,128)(2,1)S(1)}, bf16[8,64,128]{2,1,0:T(8,128)(2,1)S(1)}, u32[]{:S(2)}, u32[]{:S(2)}) collective-permute-start(bf16[8,64,128]{2,1,0:T(8,128)(2,1)S(1)} %fusion.own_ref.base_ref), channel_id=1, source_target_pairs={{0,252},{4,8},{8,4},{12,16},{16,12},{20,24},{24,20},{28,32},{32,28... | collective-permute-start | bytes 393224 | tf_op jit(solution)/shard_map/ppermute | solution.py:171
  9.9 2.8 %copy-done = bf16[8,8,1,3,128,128]{5,4,3,2,1,0:T(8,128)(2,1)S(1)} copy-done((bf16[8,8,1,3,128,128]{5,4,3,2,1,0:T(8,128)(2,1)S(1)}, bf16[8,8,1,3,128,128]{5,4,3,2,1,0:T(8,128)(2,1)}, u32[]{:S(2)}) %copy-start) | copy-done | bytes 6291480
  17.8 5.5 %collective-permute-done.2.far_ref = bf16[8,64,128]{2,1,0:T(8,128)(2,1)S(1)} collective-permute-done((bf16[8,64,128]{2,1,0:T(8,128)(2,1)S(1)}, bf16[8,64,128]{2,1,0:T(8,128)(2,1)S(1)}, u32[]{:S(2)}, u32[]{:S(2)}) %collective-permute-start.2) | collective-permute-done | bytes 131104 | tf_op jit(solution)/shard_map/ppermute | solution.py:171
  25.9 5.5 %collective-permute-done.4.far_ref = bf16[8,64,128]{2,1,0:T(8,128)(2,1)S(1)} collective-permute-done((bf16[8,64,128]{2,1,0:T(8,128)(2,1)S(1)}, bf16[8,64,128]{2,1,0:T(8,128)(2,1)S(1)}, u32[]{:S(2)}, u32[]{:S(2)}) %collective-permute-start.4) | collective-permute-done | bytes 131104 | tf_op jit(solution)/shard_map/ppermute | solution.py:171
  34.0 5.5 %collective-permute-done.6.far_ref = bf16[8,64,128]{2,1,0:T(8,128)(2,1)S(1)} collective-permute-done((bf16[8,64,128]{2,1,0:T(8,128)(2,1)S(1)}, bf16[8,64,128]{2,1,0:T(8,128)(2,1)S(1)}, u32[]{:S(2)}, u32[]{:S(2)}) %collective-permute-start.6) | collective-permute-done | bytes 131104 | tf_op jit(solution)/shard_map/ppermute | solution.py:171
  42.1 5.5 %collective-permute-done.8.far_ref = bf16[8,64,128]{2,1,0:T(8,128)(2,1)S(1)} collective-permute-done((bf16[8,64,128]{2,1,0:T(8,128)(2,1)S(1)}, bf16[8,64,128]{2,1,0:T(8,128)(2,1)S(1)}, u32[]{:S(2)}, u32[]{:S(2)}) %collective-permute-start.8) | collective-permute-done | bytes 131104 | tf_op jit(solution)/shard_map/ppermute | solution.py:171
  50.2 5.4 %collective-permute-done.10.far_ref = bf16[8,64,128]{2,1,0:T(8,128)(2,1)S(1)} collective-permute-done((bf16[8,64,128]{2,1,0:T(8,128)(2,1)S(1)}, bf16[8,64,128]{2,1,0:T(8,128)(2,1)S(1)}, u32[]{:S(2)}, u32[]{:S(2)}) %collective-permute-start.10) | collective-permute-done | bytes 131104 | tf_op jit(solution)/shard_map/ppermute | solution.py:171
  59.4 4.4 %collective-permute-done.12.far_ref = bf16[8,64,128]{2,1,0:T(8,128)(2,1)S(1)} collective-permute-done((bf16[8,64,128]{2,1,0:T(8,128)(2,1)S(1)}, bf16[8,64,128]{2,1,0:T(8,128)(2,1)S(1)}, u32[]{:S(2)}, u32[]{:S(2)}) %collective-permute-start.12) | collective-permute-done | bytes 131104 | tf_op jit(solution)/shard_map/ppermute | solution.py:171
  66.0 2.8 %copy-done.1 = bf16[8,8,1,3,128,128]{5,4,3,2,1,0:T(8,128)(2,1)S(1)} copy-done((bf16[8,8,1,3,128,128]{5,4,3,2,1,0:T(8,128)(2,1)S(1)}, bf16[8,8,1,3,128,128]{5,4,3,2,1,0:T(8,128)(2,1)}, u32[]{:S(2)}) %copy-start.1) | copy-done | bytes 6291480
  72.4 2.6 %collective-permute-start.16 = (bf16[8,64,128]{2,1,0:T(8,128)(2,1)S(1)}, bf16[8,64,128]{2,1,0:T(8,128)(2,1)S(1)}, u32[]{:S(2)}, u32[]{:S(2)}) collective-permute-start(bf16[8,64,128]{2,1,0:T(8,128)(2,1)S(1)} %finish.21.own_ref), channel_id=1, source_target_pairs={{0,252},{4,8},{8,4},{12,16},{16,12},{20,24},{24,20},{28,32},{32,28... | collective-permute-start | bytes 393224 | tf_op jit(solution)/shard_map/ppermute | solution.py:171
  75.0 2.8 %copy-done.2 = bf16[8,8,1,3,128,128]{5,4,3,2,1,0:T(8,128)(2,1)S(1)} copy-done((bf16[8,8,1,3,128,128]{5,4,3,2,1,0:T(8,128)(2,1)S(1)}, bf16[8,8,1,3,128,128]{5,4,3,2,1,0:T(8,128)(2,1)}, u32[]{:S(2)}) %copy-start.2) | copy-done | bytes 6291480
  80.5 2.6 %collective-permute-start.18 = (bf16[8,64,128]{2,1,0:T(8,128)(2,1)S(1)}, bf16[8,64,128]{2,1,0:T(8,128)(2,1)S(1)}, u32[]{:S(2)}, u32[]{:S(2)}) collective-permute-start(bf16[8,64,128]{2,1,0:T(8,128)(2,1)S(1)} %finish.22.own_ref), channel_id=1, source_target_pairs={{0,252},{4,8},{8,4},{12,16},{16,12},{20,24},{24,20},{28,32},{32,28... | collective-permute-start | bytes 393224 | tf_op jit(solution)/shard_map/ppermute | solution.py:171
  83.2 2.1 %prepare.23 = (f32[8,64,128]{2,1,0:T(8,128)S(1)}, bf16[8,128,256]{2,1,0:T(8,128)(2,1)S(1)}, bf16[8,8,1,64,128]{4,3,2,1,0:T(8,128)(2,1)}) custom-call(s32[4]{0:T(128)S(1)} %pad_add_fusion.place_ref, s32[1,192]{1,0:T(1,128)S(1)} %reshape.8.cols_ref, bf16[8,64,128]{2,1,0:T(8,128)(2,1)S(1)} %finish.17.own_ref.base_ref, ...), custom_call_target="tpu_custom_call", output_to_operand_aliasing={{2}: (6, {})} | custom-call | flops 20000000 | bytes 4194304 | tf_op jit(solution)/shard_map/prepare/pallas_call | solution.py:89
  85.3 3.0 %collective-permute-done.18.far_ref = bf16[8,64,128]{2,1,0:T(8,128)(2,1)S(1)} collective-permute-done((bf16[8,64,128]{2,1,0:T(8,128)(2,1)S(1)}, bf16[8,64,128]{2,1,0:T(8,128)(2,1)S(1)}, u32[]{:S(2)}, u32[]{:S(2)}) %collective-permute-start.18) | collective-permute-done | bytes 131104 | tf_op jit(solution)/shard_map/ppermute | solution.py:171
  88.6 2.6 %collective-permute-start.20 = (bf16[8,64,128]{2,1,0:T(8,128)(2,1)S(1)}, bf16[8,64,128]{2,1,0:T(8,128)(2,1)S(1)}, u32[]{:S(2)}, u32[]{:S(2)}) collective-permute-start(bf16[8,64,128]{2,1,0:T(8,128)(2,1)S(1)} %finish.23.own_ref), channel_id=1, source_target_pairs={{0,252},{4,8},{8,4},{12,16},{16,12},{20,24},{24,20},{28,32},{32,28... | collective-permute-start | bytes 393224 | tf_op jit(solution)/shard_map/ppermute | solution.py:171
  91.3 2.1 %prepare.24 = (f32[8,64,128]{2,1,0:T(8,128)S(1)}, bf16[8,128,256]{2,1,0:T(8,128)(2,1)S(1)}, bf16[8,8,1,64,128]{4,3,2,1,0:T(8,128)(2,1)}) custom-call(s32[4]{0:T(128)S(1)} %pad_add_fusion.place_ref, s32[1,192]{1,0:T(1,128)S(1)} %reshape.8.cols_ref, bf16[8,64,128]{2,1,0:T(8,128)(2,1)S(1)} %finish.16.own_ref.base_ref, ...), custom_call_target="tpu_custom_call", output_to_operand_aliasing={{2}: (6, {})} | custom-call | flops 20000000 | bytes 4194304 | tf_op jit(solution)/shard_map/prepare/pallas_call | solution.py:89
  93.4 3.0 %collective-permute-done.20.far_ref = bf16[8,64,128]{2,1,0:T(8,128)(2,1)S(1)} collective-permute-done((bf16[8,64,128]{2,1,0:T(8,128)(2,1)S(1)}, bf16[8,64,128]{2,1,0:T(8,128)(2,1)S(1)}, u32[]{:S(2)}, u32[]{:S(2)}) %collective-permute-start.20) | collective-permute-done | bytes 131104 | tf_op jit(solution)/shard_map/ppermute | solution.py:171
  96.7 2.6 %collective-permute-start.22 = (bf16[8,64,128]{2,1,0:T(8,128)(2,1)S(1)}, bf16[8,64,128]{2,1,0:T(8,128)(2,1)S(1)}, u32[]{:S(2)}, u32[]{:S(2)}) collective-permute-start(bf16[8,64,128]{2,1,0:T(8,128)(2,1)S(1)} %finish.24.own_ref), channel_id=1, source_target_pairs={{0,252},{4,8},{8,4},{12,16},{16,12},{20,24},{24,20},{28,32},{32,28... | collective-permute-start | bytes 393224 | tf_op jit(solution)/shard_map/ppermute | solution.py:171
  101.5 3.0 %collective-permute-done.22.far_ref = bf16[8,64,128]{2,1,0:T(8,128)(2,1)S(1)} collective-permute-done((bf16[8,64,128]{2,1,0:T(8,128)(2,1)S(1)}, bf16[8,64,128]{2,1,0:T(8,128)(2,1)S(1)}, u32[]{:S(2)}, u32[]{:S(2)}) %collective-permute-start.22) | collective-permute-done | bytes 131104 | tf_op jit(solution)/shard_map/ppermute | solution.py:171
  104.8 2.6 %collective-permute-start.24 = (bf16[8,64,128]{2,1,0:T(8,128)(2,1)S(1)}, bf16[8,64,128]{2,1,0:T(8,128)(2,1)S(1)}, u32[]{:S(2)}, u32[]{:S(2)}) collective-permute-start(bf16[8,64,128]{2,1,0:T(8,128)(2,1)S(1)} %finish.25.own_ref), channel_id=1, source_target_pairs={{0,252},{4,8},{8,4},{12,16},{16,12},{20,24},{24,20},{28,32},{32,28... | collective-permute-start | bytes 393224 | tf_op jit(solution)/shard_map/ppermute | solution.py:171
  109.6 3.0 %collective-permute-done.24.far_ref = bf16[8,64,128]{2,1,0:T(8,128)(2,1)S(1)} collective-permute-done((bf16[8,64,128]{2,1,0:T(8,128)(2,1)S(1)}, bf16[8,64,128]{2,1,0:T(8,128)(2,1)S(1)}, u32[]{:S(2)}, u32[]{:S(2)}) %collective-permute-start.24) | collective-permute-done | bytes 131104 | tf_op jit(solution)/shard_map/ppermute | solution.py:171
  113.0 2.6 %collective-permute-start.26 = (bf16[8,64,128]{2,1,0:T(8,128)(2,1)S(1)}, bf16[8,64,128]{2,1,0:T(8,128)(2,1)S(1)}, u32[]{:S(2)}, u32[]{:S(2)}) collective-permute-start(bf16[8,64,128]{2,1,0:T(8,128)(2,1)S(1)} %finish.26.own_ref), channel_id=1, source_target_pairs={{0,252},{4,8},{8,4},{12,16},{16,12},{20,24},{24,20},{28,32},{32,28... | collective-permute-start | bytes 393224 | tf_op jit(solution)/shard_map/ppermute | solution.py:171
  115.6 2.1 %prepare.27 = (f32[8,64,128]{2,1,0:T(8,128)S(1)}, bf16[8,128,256]{2,1,0:T(8,128)(2,1)S(1)}, bf16[8,8,1,64,128]{4,3,2,1,0:T(8,128)(2,1)}) custom-call(s32[4]{0:T(128)S(1)} %pad_add_fusion.place_ref, s32[1,192]{1,0:T(1,128)S(1)} %reshape.8.cols_ref, bf16[8,64,128]{2,1,0:T(8,128)(2,1)S(1)} %fusion.own_ref.base_ref, ...), custom_call_target="tpu_custom_call", output_to_operand_aliasing={{2}: (6, {})} | custom-call | flops 20000000 | bytes 4194304 | tf_op jit(solution)/shard_map/prepare/pallas_call | solution.py:89
  117.7 3.0 %collective-permute-done.26.far_ref = bf16[8,64,128]{2,1,0:T(8,128)(2,1)S(1)} collective-permute-done((bf16[8,64,128]{2,1,0:T(8,128)(2,1)S(1)}, bf16[8,64,128]{2,1,0:T(8,128)(2,1)S(1)}, u32[]{:S(2)}, u32[]{:S(2)}) %collective-permute-start.26) | collective-permute-done | bytes 131104 | tf_op jit(solution)/shard_map/ppermute | solution.py:171
  (78 shorter events, 36.3 us)
Async XLA Ops:
  1.0 14.2 %collective-permute-start = (bf16[8,64,128]{2,1,0:T(8,128)(2,1)S(1)}, bf16[8,64,128]{2,1,0:T(8,128)(2,1)S(1)}, u32[]{:S(2)}, u32[]{:S(2)}) collective-permute-start(bf16[8,64,128]{2,1,0:T(8,128)(2,1)S(1)} %fusion.own_ref.base_ref), channel_id=1, source_target_pairs={{0,252},{4,8},{8,4},{12,16},{16,12},{20,24},{24,20},{28,32},{32,28... | collective-permute-start | bytes 393224 | tf_op jit(solution)/shard_map/ppermute | solution.py:171
  8.8 6.3 %collective-permute-start.1 = (bf16[8,64,128]{2,1,0:T(8,128)(2,1)S(1)}, bf16[8,64,128]{2,1,0:T(8,128)(2,1)S(1)}, u32[]{:S(2)}, u32[]{:S(2)}) collective-permute-start(bf16[8,64,128]{2,1,0:T(8,128)(2,1)S(1)} %fusion.own_ref.base_ref), channel_id=1, source_target_pairs={{0,4},{4,0},{8,12},{12,8},{16,20},{20,16},{24,28},{28,24},{32,36},... | collective-permute-start | bytes 393224 | tf_op jit(solution)/shard_map/ppermute | solution.py:172
  15.5 7.8 %collective-permute-start.2 = (bf16[8,64,128]{2,1,0:T(8,128)(2,1)S(1)}, bf16[8,64,128]{2,1,0:T(8,128)(2,1)S(1)}, u32[]{:S(2)}, u32[]{:S(2)}) collective-permute-start(bf16[8,64,128]{2,1,0:T(8,128)(2,1)S(1)} %finish.14.own_ref.base_ref), channel_id=1, source_target_pairs={{0,252},{4,8},{8,4},{12,16},{16,12},{20,24},{24,20},{28,32},{32,28... | collective-permute-start | bytes 393224 | tf_op jit(solution)/shard_map/ppermute | solution.py:171
  16.9 6.4 %collective-permute-start.3 = (bf16[8,64,128]{2,1,0:T(8,128)(2,1)S(1)}, bf16[8,64,128]{2,1,0:T(8,128)(2,1)S(1)}, u32[]{:S(2)}, u32[]{:S(2)}) collective-permute-start(bf16[8,64,128]{2,1,0:T(8,128)(2,1)S(1)} %finish.14.own_ref.base_ref), channel_id=1, source_target_pairs={{0,4},{4,0},{8,12},{12,8},{16,20},{20,16},{24,28},{28,24},{32,36},... | collective-permute-start | bytes 393224 | tf_op jit(solution)/shard_map/ppermute | solution.py:172
  23.6 7.8 %collective-permute-start.4 = (bf16[8,64,128]{2,1,0:T(8,128)(2,1)S(1)}, bf16[8,64,128]{2,1,0:T(8,128)(2,1)S(1)}, u32[]{:S(2)}, u32[]{:S(2)}) collective-permute-start(bf16[8,64,128]{2,1,0:T(8,128)(2,1)S(1)} %finish.15.own_ref.base_ref), channel_id=1, source_target_pairs={{0,252},{4,8},{8,4},{12,16},{16,12},{20,24},{24,20},{28,32},{32,28... | collective-permute-start | bytes 393224 | tf_op jit(solution)/shard_map/ppermute | solution.py:171
  25.0 6.4 %collective-permute-start.5 = (bf16[8,64,128]{2,1,0:T(8,128)(2,1)S(1)}, bf16[8,64,128]{2,1,0:T(8,128)(2,1)S(1)}, u32[]{:S(2)}, u32[]{:S(2)}) collective-permute-start(bf16[8,64,128]{2,1,0:T(8,128)(2,1)S(1)} %finish.15.own_ref.base_ref), channel_id=1, source_target_pairs={{0,4},{4,0},{8,12},{12,8},{16,20},{20,16},{24,28},{28,24},{32,36},... | collective-permute-start | bytes 393224 | tf_op jit(solution)/shard_map/ppermute | solution.py:172
  31.7 7.8 %collective-permute-start.6 = (bf16[8,64,128]{2,1,0:T(8,128)(2,1)S(1)}, bf16[8,64,128]{2,1,0:T(8,128)(2,1)S(1)}, u32[]{:S(2)}, u32[]{:S(2)}) collective-permute-start(bf16[8,64,128]{2,1,0:T(8,128)(2,1)S(1)} %finish.16.own_ref.base_ref), channel_id=1, source_target_pairs={{0,252},{4,8},{8,4},{12,16},{16,12},{20,24},{24,20},{28,32},{32,28... | collective-permute-start | bytes 393224 | tf_op jit(solution)/shard_map/ppermute | solution.py:171
  33.1 6.4 %collective-permute-start.7 = (bf16[8,64,128]{2,1,0:T(8,128)(2,1)S(1)}, bf16[8,64,128]{2,1,0:T(8,128)(2,1)S(1)}, u32[]{:S(2)}, u32[]{:S(2)}) collective-permute-start(bf16[8,64,128]{2,1,0:T(8,128)(2,1)S(1)} %finish.16.own_ref.base_ref), channel_id=1, source_target_pairs={{0,4},{4,0},{8,12},{12,8},{16,20},{20,16},{24,28},{28,24},{32,36},... | collective-permute-start | bytes 393224 | tf_op jit(solution)/shard_map/ppermute | solution.py:172
  39.8 7.8 %collective-permute-start.8 = (bf16[8,64,128]{2,1,0:T(8,128)(2,1)S(1)}, bf16[8,64,128]{2,1,0:T(8,128)(2,1)S(1)}, u32[]{:S(2)}, u32[]{:S(2)}) collective-permute-start(bf16[8,64,128]{2,1,0:T(8,128)(2,1)S(1)} %finish.17.own_ref.base_ref), channel_id=1, source_target_pairs={{0,252},{4,8},{8,4},{12,16},{16,12},{20,24},{24,20},{28,32},{32,28... | collective-permute-start | bytes 393224 | tf_op jit(solution)/shard_map/ppermute | solution.py:171
  41.2 6.4 %collective-permute-start.9 = (bf16[8,64,128]{2,1,0:T(8,128)(2,1)S(1)}, bf16[8,64,128]{2,1,0:T(8,128)(2,1)S(1)}, u32[]{:S(2)}, u32[]{:S(2)}) collective-permute-start(bf16[8,64,128]{2,1,0:T(8,128)(2,1)S(1)} %finish.17.own_ref.base_ref), channel_id=1, source_target_pairs={{0,4},{4,0},{8,12},{12,8},{16,20},{20,16},{24,28},{28,24},{32,36},... | collective-permute-start | bytes 393224 | tf_op jit(solution)/shard_map/ppermute | solution.py:172
  47.9 7.8 %collective-permute-start.10 = (bf16[8,64,128]{2,1,0:T(8,128)(2,1)S(1)}, bf16[8,64,128]{2,1,0:T(8,128)(2,1)S(1)}, u32[]{:S(2)}, u32[]{:S(2)}) collective-permute-start(bf16[8,64,128]{2,1,0:T(8,128)(2,1)S(1)} %finish.18.own_ref.base_ref), channel_id=1, source_target_pairs={{0,252},{4,8},{8,4},{12,16},{16,12},{20,24},{24,20},{28,32},{32,28... | collective-permute-start | bytes 393224 | tf_op jit(solution)/shard_map/ppermute | solution.py:171
  49.3 6.4 %collective-permute-start.11 = (bf16[8,64,128]{2,1,0:T(8,128)(2,1)S(1)}, bf16[8,64,128]{2,1,0:T(8,128)(2,1)S(1)}, u32[]{:S(2)}, u32[]{:S(2)}) collective-permute-start(bf16[8,64,128]{2,1,0:T(8,128)(2,1)S(1)} %finish.18.own_ref.base_ref), channel_id=1, source_target_pairs={{0,4},{4,0},{8,12},{12,8},{16,20},{20,16},{24,28},{28,24},{32,36},... | collective-permute-start | bytes 393224 | tf_op jit(solution)/shard_map/ppermute | solution.py:172
  56.0 7.8 %collective-permute-start.12 = (bf16[8,64,128]{2,1,0:T(8,128)(2,1)S(1)}, bf16[8,64,128]{2,1,0:T(8,128)(2,1)S(1)}, u32[]{:S(2)}, u32[]{:S(2)}) collective-permute-start(bf16[8,64,128]{2,1,0:T(8,128)(2,1)S(1)} %finish.19.own_ref.base_ref), channel_id=1, source_target_pairs={{0,252},{4,8},{8,4},{12,16},{16,12},{20,24},{24,20},{28,32},{32,28... | collective-permute-start | bytes 393224 | tf_op jit(solution)/shard_map/ppermute | solution.py:171
  57.5 6.4 %collective-permute-start.13 = (bf16[8,64,128]{2,1,0:T(8,128)(2,1)S(1)}, bf16[8,64,128]{2,1,0:T(8,128)(2,1)S(1)}, u32[]{:S(2)}, u32[]{:S(2)}) collective-permute-start(bf16[8,64,128]{2,1,0:T(8,128)(2,1)S(1)} %finish.19.own_ref.base_ref), channel_id=1, source_target_pairs={{0,4},{4,0},{8,12},{12,8},{16,20},{20,16},{24,28},{28,24},{32,36},... | collective-permute-start | bytes 393224 | tf_op jit(solution)/shard_map/ppermute | solution.py:172
  64.1 8.0 %collective-permute-start.14 = (bf16[8,64,128]{2,1,0:T(8,128)(2,1)S(1)}, bf16[8,64,128]{2,1,0:T(8,128)(2,1)S(1)}, u32[]{:S(2)}, u32[]{:S(2)}) collective-permute-start(bf16[8,64,128]{2,1,0:T(8,128)(2,1)S(1)} %finish.20.own_ref), channel_id=1, source_target_pairs={{0,252},{4,8},{8,4},{12,16},{16,12},{20,24},{24,20},{28,32},{32,28... | collective-permute-start | bytes 393224 | tf_op jit(solution)/shard_map/ppermute | solution.py:171
  65.7 6.4 %collective-permute-start.15 = (bf16[8,64,128]{2,1,0:T(8,128)(2,1)S(1)}, bf16[8,64,128]{2,1,0:T(8,128)(2,1)S(1)}, u32[]{:S(2)}, u32[]{:S(2)}) collective-permute-start(bf16[8,64,128]{2,1,0:T(8,128)(2,1)S(1)} %finish.20.own_ref), channel_id=1, source_target_pairs={{0,4},{4,0},{8,12},{12,8},{16,20},{20,16},{24,28},{28,24},{32,36},... | collective-permute-start | bytes 393224 | tf_op jit(solution)/shard_map/ppermute | solution.py:172
  72.4 7.8 %collective-permute-start.16 = (bf16[8,64,128]{2,1,0:T(8,128)(2,1)S(1)}, bf16[8,64,128]{2,1,0:T(8,128)(2,1)S(1)}, u32[]{:S(2)}, u32[]{:S(2)}) collective-permute-start(bf16[8,64,128]{2,1,0:T(8,128)(2,1)S(1)} %finish.21.own_ref), channel_id=1, source_target_pairs={{0,252},{4,8},{8,4},{12,16},{16,12},{20,24},{24,20},{28,32},{32,28... | collective-permute-start | bytes 393224 | tf_op jit(solution)/shard_map/ppermute | solution.py:171
  80.5 7.8 %collective-permute-start.18 = (bf16[8,64,128]{2,1,0:T(8,128)(2,1)S(1)}, bf16[8,64,128]{2,1,0:T(8,128)(2,1)S(1)}, u32[]{:S(2)}, u32[]{:S(2)}) collective-permute-start(bf16[8,64,128]{2,1,0:T(8,128)(2,1)S(1)} %finish.22.own_ref), channel_id=1, source_target_pairs={{0,252},{4,8},{8,4},{12,16},{16,12},{20,24},{24,20},{28,32},{32,28... | collective-permute-start | bytes 393224 | tf_op jit(solution)/shard_map/ppermute | solution.py:171
  88.6 7.8 %collective-permute-start.20 = (bf16[8,64,128]{2,1,0:T(8,128)(2,1)S(1)}, bf16[8,64,128]{2,1,0:T(8,128)(2,1)S(1)}, u32[]{:S(2)}, u32[]{:S(2)}) collective-permute-start(bf16[8,64,128]{2,1,0:T(8,128)(2,1)S(1)} %finish.23.own_ref), channel_id=1, source_target_pairs={{0,252},{4,8},{8,4},{12,16},{16,12},{20,24},{24,20},{28,32},{32,28... | collective-permute-start | bytes 393224 | tf_op jit(solution)/shard_map/ppermute | solution.py:171
  96.7 7.8 %collective-permute-start.22 = (bf16[8,64,128]{2,1,0:T(8,128)(2,1)S(1)}, bf16[8,64,128]{2,1,0:T(8,128)(2,1)S(1)}, u32[]{:S(2)}, u32[]{:S(2)}) collective-permute-start(bf16[8,64,128]{2,1,0:T(8,128)(2,1)S(1)} %finish.24.own_ref), channel_id=1, source_target_pairs={{0,252},{4,8},{8,4},{12,16},{16,12},{20,24},{24,20},{28,32},{32,28... | collective-permute-start | bytes 393224 | tf_op jit(solution)/shard_map/ppermute | solution.py:171
  104.8 7.8 %collective-permute-start.24 = (bf16[8,64,128]{2,1,0:T(8,128)(2,1)S(1)}, bf16[8,64,128]{2,1,0:T(8,128)(2,1)S(1)}, u32[]{:S(2)}, u32[]{:S(2)}) collective-permute-start(bf16[8,64,128]{2,1,0:T(8,128)(2,1)S(1)} %finish.25.own_ref), channel_id=1, source_target_pairs={{0,252},{4,8},{8,4},{12,16},{16,12},{20,24},{24,20},{28,32},{32,28... | collective-permute-start | bytes 393224 | tf_op jit(solution)/shard_map/ppermute | solution.py:171
  107.5 5.2 %collective-permute-start.25 = (bf16[8,64,128]{2,1,0:T(8,128)(2,1)S(1)}, bf16[8,64,128]{2,1,0:T(8,128)(2,1)S(1)}, u32[]{:S(2)}, u32[]{:S(2)}) collective-permute-start(bf16[8,64,128]{2,1,0:T(8,128)(2,1)S(1)} %finish.25.own_ref), channel_id=1, source_target_pairs={{0,4},{4,0},{8,12},{12,8},{16,20},{20,16},{24,28},{28,24},{32,36},... | collective-permute-start | bytes 393224 | tf_op jit(solution)/shard_map/ppermute | solution.py:172
  113.0 7.8 %collective-permute-start.26 = (bf16[8,64,128]{2,1,0:T(8,128)(2,1)S(1)}, bf16[8,64,128]{2,1,0:T(8,128)(2,1)S(1)}, u32[]{:S(2)}, u32[]{:S(2)}) collective-permute-start(bf16[8,64,128]{2,1,0:T(8,128)(2,1)S(1)} %finish.26.own_ref), channel_id=1, source_target_pairs={{0,252},{4,8},{8,4},{12,16},{16,12},{20,24},{24,20},{28,32},{32,28... | collective-permute-start | bytes 393224 | tf_op jit(solution)/shard_map/ppermute | solution.py:171
  115.6 5.2 %collective-permute-start.27 = (bf16[8,64,128]{2,1,0:T(8,128)(2,1)S(1)}, bf16[8,64,128]{2,1,0:T(8,128)(2,1)S(1)}, u32[]{:S(2)}, u32[]{:S(2)}) collective-permute-start(bf16[8,64,128]{2,1,0:T(8,128)(2,1)S(1)} %finish.26.own_ref), channel_id=1, source_target_pairs={{0,4},{4,0},{8,12},{12,8},{16,20},{20,16},{24,28},{28,24},{32,36},... | collective-permute-start | bytes 393224 | tf_op jit(solution)/shard_map/ppermute | solution.py:172
  (10 other events, 48.5 us)
